TPU v7x, 32 devices: a whole 2x2x4 slice. The times are simulated.
32 devices in a mesh: batch: 4 (over z), ctx: 4 (over y, core), heads: 2 (over x).
Axes of the slice: x: 2, y: 2, z: 4, core: 2. Of those that a mesh axis runs over, the one named last changes fastest.
Arguments:
- tokens: bfloat16 [49152, 768], P(('batch', 'ctx', 'heads')), may hold values from -6 to 6
- lengths: int32 [4, 2], P('batch'), may hold values from 1536 to 10752, as said below
- gain_one: float32 [768], replicated, may hold values from 0.25 to 1.75
- w_qkv: bfloat16 [768, 3, 768], P(None, None, 'heads'), may hold values from -0.21875 to 0.21875
- f_query: bfloat16 [12, 64, 64], P('heads'), may hold values from -1.5 to 1.5
- f_key: bfloat16 [12, 64, 64], P('heads'), may hold values from -1.5 to 1.5
- w_out: bfloat16 [768, 768], P('heads'), may hold values from -3.5 to 3.5
- gain_two: float32 [768], replicated, may hold values from 0.25 to 1.75
- w_up: bfloat16 [768, 3072], P(None, 'heads'), may hold values from -0.21875 to 0.21875
- w_down: bfloat16 [3072, 768], P('heads'), may hold values from -0.109375 to 0.109375
- d_out: bfloat16 [49152, 768], P(('batch', 'ctx', 'heads')), may hold values from -6 to 6
Outputs:
- mixed: bfloat16 [49152, 768], P(('batch', 'ctx', 'heads'))
- grad_tokens: bfloat16 [49152, 768], P(('batch', 'ctx', 'heads'))
- grad_gain_one: float32 [768], replicated
- grad_w_qkv: float32 [768, 3, 768], P(None, None, 'heads')
- grad_f_query: float32 [12, 64, 64], P('heads')
- grad_f_key: float32 [12, 64, 64], P('heads')
- grad_w_out: float32 [768, 768], P('heads')
- grad_gain_two: float32 [768], replicated
- grad_w_up: float32 [768, 3072], P(None, 'heads')
- grad_w_down: float32 [3072, 768], P('heads')
Inputs may be any that keep to these rules, and one draw needn't show every extreme that they name: `lengths`: each row holds 1536 and 10752 in one of the two orders.
All inputs are finite; a program needn't handle non-finite values.
Results may differ from a plain program's by a relative error of at most 0.015.
Values may be sent and summed in bfloat16 or wider, within the bound.
No kernel may reach another device: no remote copies, remote signals or barrier semaphores. Data moves between devices by JAX's collectives and lax.ppermute only.
A program may use at most 448 MiB of HBM per device.

v0:
```python
import jax
import jax.numpy as jnp
from jax import lax
from jax.sharding import PartitionSpec as P

SPAN = 64


highest = lax.Precision.HIGHEST
epsilon = 1e-05


def prefix_2(value, axis, join, neutral, backward):
    count = lax.axis_size(axis)
    place = lax.axis_index(axis)
    ahead = count - 1 - place if backward else place
    gathered = jax.tree.map(
        lambda a, kind: lax.all_gather(a.astype(kind), axis),
        value,
        jax.tree.map(lambda a: jnp.bfloat16 if a.dtype == jnp.float32 else a.dtype, value),
    )
    state = jax.tree.map(lambda a, e: jnp.zeros_like(a) + jnp.asarray(e, a.dtype), value, neutral)

    def one(step, state):
        source = count - 1 - step if backward else step
        return join(
            state,
            jax.tree.map(
                lambda a, own: lax.dynamic_index_in_dim(a, source, 0, False).astype(own.dtype),
                gathered,
                value,
            ),
        )

    return lax.fori_loop(0, ahead, one, state)


def contract_rows(left, right):
    return lax.dot_general(
        left, right, (((0,), (0,)), ((), ())), preferred_element_type=jnp.float32
    )


def contract_cols(left, right):
    return lax.dot_general(
        left, right, (((1,), (1,)), ((), ())), preferred_element_type=jnp.float32
    )


def norm_rows(values, norm_gain):
    centred = values - jnp.mean(values, axis=1, keepdims=True)
    spread = lax.rsqrt(jnp.mean(centred * centred, axis=1, keepdims=True) + epsilon)
    normed = centred * spread
    return (normed, spread, normed * norm_gain)


def norm_back(gradient, normed, spread, norm_gain):
    scaled = gradient * norm_gain
    centred = (
        scaled
        - jnp.mean(scaled, axis=1, keepdims=True)
        - normed * jnp.mean(scaled * normed, axis=1, keepdims=True)
    )
    return (spread * centred, jnp.sum(gradient * normed, axis=0))


def feature_map(vectors, feature_weights):
    logits = jnp.einsum(
        "rhe,hef->rhf", vectors, feature_weights, preferred_element_type=jnp.float32
    )
    return (jax.nn.softmax(logits, axis=-1), jax.nn.softmax(-logits, axis=-1))


def feature_back(plus_soft, minus_soft, grad_phi, vectors, feature_weights):
    head_size = plus_soft.shape[-1]
    grad_plus = grad_phi[..., :head_size]
    grad_minus = grad_phi[..., head_size:]
    grad_logits = plus_soft * (grad_plus - jnp.sum(grad_plus * plus_soft, axis=-1, keepdims=True))
    grad_logits = grad_logits - minus_soft * (
        grad_minus - jnp.sum(grad_minus * minus_soft, axis=-1, keepdims=True)
    )
    grad_vectors = jnp.einsum(
        "rhf,hef->rhe", grad_logits, feature_weights.astype(jnp.float32), precision=highest
    )
    grad_weights = jnp.einsum(
        "rhe,rhf->hef", vectors.astype(jnp.float32), grad_logits, precision=highest
    )
    return (grad_vectors, grad_weights)


def attention_parts(qkv, f_query, f_key, doc_masks):
    row_count = qkv.shape[0]
    head_count = f_query.shape[0]
    head_size = f_query.shape[1]
    span_count = row_count // SPAN
    vectors = qkv.reshape(row_count, 3, head_count, head_size)
    query_plus, query_minus = feature_map(vectors[:, 0], f_query)
    key_plus, key_minus = feature_map(vectors[:, 1], f_key)
    phi_query = (
        jnp.concatenate([query_plus, query_minus], axis=-1)
        .astype(jnp.bfloat16)
        .reshape(span_count, SPAN, head_count, 2 * head_size)
    )
    phi_key = (
        jnp.concatenate([key_plus, key_minus], axis=-1)
        .astype(jnp.bfloat16)
        .reshape(span_count, SPAN, head_count, 2 * head_size)
    )
    values = vectors[:, 2].reshape(span_count, SPAN, head_count, head_size)
    key_masked = doc_masks.astype(jnp.bfloat16)[:, :, :, None, None] * phi_key[None]
    key_state = jnp.einsum(
        "dcjhf,cjhe->dchfe", key_masked, values, preferred_element_type=jnp.float32
    )
    norm_state = jnp.sum(key_masked, axis=2, dtype=jnp.float32)
    return (
        query_plus,
        query_minus,
        key_plus,
        key_minus,
        phi_query,
        phi_key,
        values,
        key_state,
        norm_state,
    )


def add_pair(earlier, latter):
    return (earlier[0] + latter[0], earlier[1] + latter[1])


def forward_states(pieces, zero_pair):
    return prefix_2(pieces, "ctx", add_pair, zero_pair, False)


def backward_states(pieces, zero_pair):
    return prefix_2(pieces, "ctx", add_pair, zero_pair, True)


def state_prefix(incoming, key_state, norm_state, earlier_spans):
    key_before = incoming[0][:, None] + jnp.einsum(
        "cn,dnhfe->dchfe", earlier_spans, key_state, precision=highest
    )
    norm_before = incoming[1][:, None] + jnp.einsum(
        "cn,dnhf->dchf", earlier_spans, norm_state, precision=highest
    )
    return (key_before, norm_before)


def attend_spans(attn_parts, prefix, doc_masks, allowed):
    phi_query, phi_key, values = (attn_parts[4], attn_parts[5], attn_parts[6])
    query_masked = doc_masks[:, :, :, None, None] * phi_query[None]
    numerator = jnp.einsum("dcihf,dchfe->cihe", query_masked, prefix[0], precision=highest)
    denominator = jnp.einsum("dcihf,dchf->cih", query_masked, prefix[1], precision=highest)
    scores = (
        jnp.einsum("cihf,cjhf->chij", phi_query, phi_key, preferred_element_type=jnp.float32)
        * allowed[:, None]
    )
    numerator = numerator + jnp.einsum("chij,cjhe->cihe", scores, values, precision=highest)
    denominator = denominator + jnp.einsum("chij->cih", scores)
    return (numerator / denominator[..., None], denominator, scores)


def spans_back(attn_parts, prefix, doc_masks, allowed, exact_out, denominator, scores, grad_out):
    phi_query, phi_key, values = (attn_parts[4], attn_parts[5], attn_parts[6])
    grad_numer = grad_out / denominator[..., None]
    grad_denom = -jnp.sum(grad_out * exact_out, axis=-1) / denominator
    grad_scores = jnp.einsum("cihe,cjhe->chij", grad_numer, values, precision=highest)
    grad_scores = (grad_scores + jnp.transpose(grad_denom, (0, 2, 1))[..., None]) * allowed[:, None]
    grad_values = jnp.einsum("chij,cihe->cjhe", scores, grad_numer, precision=highest)
    grad_query = jnp.einsum("chij,cjhf->cihf", grad_scores, phi_key, precision=highest)
    grad_key = jnp.einsum("chij,cihf->cjhf", grad_scores, phi_query, precision=highest)
    from_state = jnp.einsum("dchfe,cihe->dcihf", prefix[0], grad_numer, precision=highest)
    from_state = from_state + prefix[1][:, :, None] * grad_denom[None, :, :, :, None]
    grad_query = grad_query + jnp.sum(doc_masks[:, :, :, None, None] * from_state, axis=0)
    query_masked = doc_masks[:, :, :, None, None] * phi_query[None]
    grad_key_before = jnp.einsum("dcihf,cihe->dchfe", query_masked, grad_numer, precision=highest)
    grad_norm_before = jnp.einsum("dcihf,cih->dchf", query_masked, grad_denom, precision=highest)
    return (grad_query, grad_key, grad_values, grad_key_before, grad_norm_before)


def shards(tokens, lengths, gain_one, w_qkv, f_query, f_key, w_out, gain_two, w_up, w_down, d_out):
    own_rows = tokens.shape[0]
    pair_size = lax.axis_size("heads")
    model_width = tokens.shape[1]
    row_count = own_rows * pair_size
    first_row = lax.axis_index("ctx") * row_count
    local_width = w_out.shape[0]
    head_count = f_query.shape[0]
    head_size = f_query.shape[1]
    span_count = row_count // SPAN
    positions = first_row + jnp.arange(row_count, dtype=jnp.int32)
    second = (positions >= lengths[0, 0]).astype(jnp.float32)
    doc_masks = jnp.stack([1.0 - second, second]).reshape(2, span_count, SPAN)
    second_spans = second.reshape(span_count, SPAN)
    causal = jnp.tril(jnp.ones((SPAN, SPAN), jnp.float32))
    allowed = jnp.where(second_spans[:, :, None] == second_spans[:, None, :], causal[None], 0.0)
    earlier_spans = jnp.tril(jnp.ones((span_count, span_count), jnp.float32), -1)
    qkv_weight = w_qkv.reshape(model_width, 3 * local_width)
    inputs = tokens.astype(jnp.float32)
    normed_one, spread_one, scaled_one = norm_rows(inputs, gain_one)
    scaled_low = scaled_one.astype(jnp.bfloat16)
    gathered_one = lax.all_gather(scaled_low, "heads", axis=0, tiled=True)
    qkv = jnp.dot(gathered_one, qkv_weight, preferred_element_type=jnp.float32).astype(jnp.bfloat16)
    attn_parts = attention_parts(qkv, f_query, f_key, doc_masks)
    zero_pair = (
        jnp.zeros((2, head_count, 2 * head_size, head_size), jnp.float32),
        jnp.zeros((2, head_count, 2 * head_size), jnp.float32),
    )
    incoming = forward_states(
        (jnp.sum(attn_parts[7], axis=1), jnp.sum(attn_parts[8], axis=1)), zero_pair
    )
    prefix = state_prefix(incoming, attn_parts[7], attn_parts[8], earlier_spans)
    exact_out, denominator, scores = attend_spans(attn_parts, prefix, doc_masks, allowed)
    attended = exact_out.reshape(row_count, local_width).astype(jnp.bfloat16)
    attn_proj = lax.psum_scatter(
        jnp.dot(attended, w_out, preferred_element_type=jnp.float32).astype(jnp.bfloat16),
        "heads",
        scatter_dimension=0,
        tiled=True,
    ).astype(jnp.float32)
    resid = inputs + attn_proj
    normed_two, spread_two, scaled_two = norm_rows(resid, gain_two)
    scaled_two_low = scaled_two.astype(jnp.bfloat16)
    gathered_two = lax.all_gather(scaled_two_low, "heads", axis=0, tiled=True)
    pre_act = jnp.dot(gathered_two, w_up, preferred_element_type=jnp.float32)
    activation = jax.nn.gelu(pre_act, approximate=True).astype(jnp.bfloat16)
    mlp_proj = lax.psum_scatter(
        jnp.dot(activation, w_down, preferred_element_type=jnp.float32).astype(jnp.bfloat16),
        "heads",
        scatter_dimension=0,
        tiled=True,
    ).astype(jnp.float32)
    mixed = (resid + mlp_proj).astype(jnp.bfloat16)
    cot_full = lax.all_gather(d_out, "heads", axis=0, tiled=True)
    grad_w_down = contract_rows(activation, cot_full)
    grad_act = contract_cols(cot_full, w_down)

    def gelu_tanh(values):
        return jax.nn.gelu(values, approximate=True)

    gelu_out, gelu_pull = jax.vjp(gelu_tanh, pre_act)
    grad_pre = gelu_pull(grad_act)[0].astype(jnp.bfloat16)
    grad_w_up = contract_rows(gathered_two, grad_pre)
    grad_h_two = lax.psum_scatter(
        contract_cols(grad_pre, w_up).astype(jnp.bfloat16), "heads", scatter_dimension=0, tiled=True
    ).astype(jnp.float32)
    back_two, gain_two_part = norm_back(grad_h_two, normed_two, spread_two, gain_two)
    grad_resid = (d_out.astype(jnp.float32) + back_two).astype(jnp.bfloat16)
    resid_full = lax.all_gather(grad_resid, "heads", axis=0, tiled=True)
    grad_w_out = contract_rows(attended, resid_full)
    grad_attended = contract_cols(resid_full, w_out).astype(jnp.bfloat16).astype(jnp.float32)
    grad_attended = grad_attended.reshape(span_count, SPAN, head_count, head_size)
    grad_query, grad_key, grad_values, grad_key_before, grad_norm_before = spans_back(
        attn_parts, prefix, doc_masks, allowed, exact_out, denominator, scores, grad_attended
    )
    later_sums = backward_states(
        (jnp.sum(grad_key_before, axis=1), jnp.sum(grad_norm_before, axis=1)), zero_pair
    )
    grad_key_state = (
        jnp.einsum("cn,dchfe->dnhfe", earlier_spans, grad_key_before, precision=highest)
        + later_sums[0][:, None]
    )
    grad_norm_state = (
        jnp.einsum("cn,dchf->dnhf", earlier_spans, grad_norm_before, precision=highest)
        + later_sums[1][:, None]
    )
    phi_key, values = (attn_parts[5], attn_parts[6])
    to_keys = (
        jnp.einsum("dchfe,cjhe->dcjhf", grad_key_state, values, precision=highest)
        + grad_norm_state[:, :, None]
    )
    grad_key = grad_key + jnp.sum(doc_masks[:, :, :, None, None] * to_keys, axis=0)
    key_masked = doc_masks[:, :, :, None, None] * phi_key[None]
    grad_values = grad_values + jnp.einsum(
        "dcjhf,dchfe->cjhe", key_masked, grad_key_state, precision=highest
    )
    vectors = qkv.reshape(row_count, 3, head_count, head_size)
    grad_q_vec, grad_f_query = feature_back(
        attn_parts[0],
        attn_parts[1],
        grad_query.reshape(row_count, head_count, 2 * head_size),
        vectors[:, 0],
        f_query,
    )
    grad_k_vec, grad_f_key = feature_back(
        attn_parts[2],
        attn_parts[3],
        grad_key.reshape(row_count, head_count, 2 * head_size),
        vectors[:, 1],
        f_key,
    )
    grad_joined = jnp.stack(
        [grad_q_vec, grad_k_vec, grad_values.reshape(row_count, head_count, head_size)], axis=1
    )
    grad_joined = grad_joined.reshape(row_count, 3 * local_width).astype(jnp.bfloat16)
    grad_w_qkv = contract_rows(gathered_one, grad_joined).reshape(model_width, 3, local_width)
    grad_h_one = lax.psum_scatter(
        contract_cols(grad_joined, qkv_weight).astype(jnp.bfloat16),
        "heads",
        scatter_dimension=0,
        tiled=True,
    ).astype(jnp.float32)
    back_one, gain_one_part = norm_back(grad_h_one, normed_one, spread_one, gain_one)
    grad_tokens = (grad_resid.astype(jnp.float32) + back_one).astype(jnp.bfloat16)
    gain_one_sum, gain_two_sum = lax.psum((gain_one_part, gain_two_part), "heads")
    (
        grad_w_qkv,
        grad_f_query,
        grad_f_key,
        grad_w_out,
        grad_w_up,
        grad_w_down,
        gain_one_sum,
        gain_two_sum,
    ) = lax.psum(
        (
            grad_w_qkv,
            grad_f_query,
            grad_f_key,
            grad_w_out,
            grad_w_up,
            grad_w_down,
            gain_one_sum,
            gain_two_sum,
        ),
        ("batch", "ctx"),
    )
    return (
        mixed,
        grad_tokens,
        gain_one_sum,
        grad_w_qkv,
        grad_f_query,
        grad_f_key,
        grad_w_out,
        gain_two_sum,
        grad_w_up,
        grad_w_down,
    )


def solution(mesh):
    in_specs = (
        P(("batch", "ctx", "heads"), None),
        P("batch", None),
        P(),
        P(None, None, "heads"),
        P("heads", None, None),
        P("heads", None, None),
        P("heads", None),
        P(),
        P(None, "heads"),
        P("heads", None),
        P(("batch", "ctx", "heads"), None),
    )
    out_specs = (
        P(("batch", "ctx", "heads"), None),
        P(("batch", "ctx", "heads"), None),
        P(),
        P(None, None, "heads"),
        P("heads", None, None),
        P("heads", None, None),
        P("heads", None),
        P(),
        P(None, "heads"),
        P("heads", None),
    )
    return jax.shard_map(shards, mesh=mesh, in_specs=in_specs, out_specs=out_specs, check_vma=False)
```

profile of v0, /device:TPU:0, one launch (start us, length us, event | category | flops | bytes accessed | tf_op | source)
XLA Modules:
  0.0 1606.1 jit_solution(3365528149852480984)
XLA Ops:
  21.1 59.0 %all-gather.9.cloned.1.call-done = bf16[3072,768]{1,0:T(8,128)(2,1)} async-done(((bf16[1536,768]{1,0:T(8,128)(2,1)}), bf16[3072,768]{1,0:T(8,128)(2,1)}) %all-gather.9.cloned.1.call-update) | async-done | bytes 4718608 | tf_op jit(solution)/shard_map/all_gather | solution.py:203
  151.3 10.2 fusion.172
  232.1 10.0 fusion.170
  242.1 13.9 multiply_reduce_fusion.2
  256.0 11.0 fusion.177
  267.1 9.1 all-gather
  281.1 36.0 %add_bitcast_fusion.1 = f32[2,48,6,128,64]{3,1,4,2,0:T(8,128)} fusion(f32[2,6,128,64]{2,3,1,0:T(8,128)} %copy.150, f32[2,48,6,128,64]{3,4,0,2,1:T(8,128)} %get-tuple-element.206, s32[48]{0:T(128)S(1)} %iota_add_fusion), kind=kOutput, calls=%fused_computation.42 | convolution fusion | flops 2722632192 | bytes 38142144 | tf_op jit(solution)/shard_map/cn,dnhfe->dchfe/dot_general | solution.py:141
  317.1 15.2 fusion.8
  332.4 29.6 %fusion.10 = f32[48,6,64,64,1]{3,2,4,1,0:T(8,128)} fusion(f32[2,48,6,128,64]{3,1,4,2,0:T(8,128)} %add_bitcast_fusion.1, f32[48,64,6,128]{3,1,2,0:T(8,128)S(1)} %bitcast.260, f32[2,48,64]{2,0,1:T(2,128)S(1)} %copy-done.26), kind=kOutput, calls=%fused_computation.16 | convolution fusion | flops 3628597248 | bytes 33054720 | tf_op jit(solution)/shard_map/dcihf,dchfe->cihe/dot_general | solution.py:153
  362.0 15.3 fusion.180
  398.5 71.1 %reduce-scatter.5.cloned.1.call-done = bf16[1536,768]{1,0:T(8,128)(2,1)} async-done(((bf16[3072,768]{1,0:T(8,128)(2,1)}), bf16[1536,768]{1,0:T(8,128)(2,1)}) %reduce-scatter.5.cloned.1.call-update) | async-done | bytes 2359312 | tf_op jit(solution)/shard_map/reduce_scatter | solution.py:216
  477.9 61.7 %all-gather.11.cloned.1.call-done = bf16[3072,768]{1,0:T(8,128)(2,1)} async-done(((bf16[1536,768]{1,0:T(8,128)(2,1)}), bf16[3072,768]{1,0:T(8,128)(2,1)}) %all-gather.11.cloned.1.call-update) | async-done | bytes 4718608 | tf_op jit(solution)/shard_map/all_gather | solution.py:225
  539.7 18.4 %multiply_convert_fusion = (bf16[3072,1536]{1,0:T(8,128)(2,1)}, f32[3072,1536]{1,0:T(8,128)}) fusion(bf16[3072,768]{1,0:T(8,128)(2,1)} %all-gather.11.cloned.1.call-done, bf16[768,1536]{1,0:T(8,128)(2,1)S(1)} %copy-done), kind=kOutput, calls=%fused_computation.40 | convolution fusion | flops 7290224640 | bytes 35389440 | tf_op jit(solution)/shard_map/dot_general | solution.py:226
  558.1 45.8 %all-gather.13.cloned.1.call-done = bf16[3072,768]{1,0:T(8,128)(2,1)} async-done(((bf16[1536,768]{1,0:T(8,128)(2,1)}), bf16[3072,768]{1,0:T(8,128)(2,1)}) %all-gather.13.cloned.1.call-update) | async-done | bytes 4718608 | tf_op jit(solution)/shard_map/all_gather | solution.py:235
  603.8 21.1 %fusion.18 = bf16[3072,1536]{1,0:T(8,128)(2,1)S(1)} fusion(f32[3072,1536]{1,0:T(8,128)} %get-tuple-element.216, bf16[3072,768]{1,0:T(8,128)(2,1)} %all-gather.13.cloned.1.call-done, bf16[1536,768]{1,0:T(8,128)(2,1)} %param.24), kind=kOutput, calls=%fused_computation.26 | convolution fusion | flops 7342129152 | bytes 35389440 | tf_op jit(solution)/shard_map/dot_general | solution.py:45
  628.4 9.2 convolution_convert_fusion.2
  639.3 12.8 convolution_convert_fusion.3
  652.2 45.7 %reduce-scatter.9.cloned.1.call-done = bf16[1536,768]{1,0:T(8,128)(2,1)} async-done(((bf16[3072,768]{1,0:T(8,128)(2,1)}), bf16[1536,768]{1,0:T(8,128)(2,1)}) %reduce-scatter.9.cloned.1.call-update) | async-done | bytes 2359312 | tf_op jit(solution)/shard_map/reduce_scatter | solution.py:245
  703.0 57.0 %reduce-scatter.7.cloned.1.call-done = bf16[1536,768]{1,0:T(8,128)(2,1)} async-done(((bf16[3072,768]{1,0:T(8,128)(2,1)}), bf16[1536,768]{1,0:T(8,128)(2,1)}) %reduce-scatter.7.cloned.1.call-update) | async-done | bytes 2359312 | tf_op jit(solution)/shard_map/reduce_scatter | solution.py:228
  766.7 62.5 %all-gather.15.cloned.1.call-done = bf16[3072,768]{1,0:T(8,128)(2,1)} async-done(((bf16[1536,768]{1,0:T(8,128)(2,1)}), bf16[3072,768]{1,0:T(8,128)(2,1)}) %all-gather.15.cloned.1.call-update) | async-done | bytes 4718608 | tf_op jit(solution)/shard_map/all_gather | solution.py:250
  836.5 9.2 reshape.346
  845.7 11.2 copy.164
  857.0 9.5 multiply_reduce_fusion.1
  866.6 11.2 fusion.171
  877.8 23.8 %fusion.181 = (bf16[2,6,128,64]{2,3,0,1:T(8,128)(2,1)S(1)}, f32[2,48,6,128,64]{3,4,0,2,1:T(8,128)}) fusion(f32[48,64,6,128]{3,1,2,0:T(8,128)S(1)} %bitcast.262, f32[2,48,64]{2,0,1:T(2,128)S(1)} %copy-done.27, f32[48,64,6,64]{1,3,2,0:T(8,128)} %copy.164, f32[48,64,6]{1,2,0:T(8,128)S(1)} %fusion.140), kind=kOutput, calls=%fused_computation.247 | convolution fusion | flops 3634397184 | bytes 33325056 | tf_op jit(solution)/shard_map/dcihf,cihe->dchfe/dot_general | solution.py:177
  901.7 38.3 %fusion.22 = f32[48,64,6,128]{3,1,2,0:T(8,128)} fusion(f32[48,64,6]{1,2,0:T(8,128)S(1)} %negate_divide_fusion, f32[2,48,6,128]{3,0,2,1:T(2,128)S(1)} %copy.172, f32[2,48,64]{2,0,1:T(2,128)S(1)} %copy-done.27, f32[2,48,6,128,64]{3,1,4,2,0:T(8,128)} %add_bitcast_fusion.1, f32[48,64,6,64]{1,3,2,0:T(8,128)} %copy.164, f32[48,64,6]{1,2,0:T(8,128)S(1)} %fusion.140), kind=kOutput, calls=%fused_computation.32 | convolution fusion | flops 3641573376 | bytes 33497088 | tf_op jit(solution)/shard_map/dchfe,cihe->dcihf/dot_general | solution.py:173
  940.0 13.6 fusion.4
  958.8 14.5 bitcast_add_fusion.4
  978.0 8.2 fusion.173
  986.2 8.6 copy.225
  999.7 8.6 copy.226
  1024.5 8.7 all-gather.2
  1036.7 35.6 %add_bitcast_fusion = f32[2,48,6,128,64]{3,1,4,2,0:T(8,128)} fusion(f32[2,6,128,64]{2,3,1,0:T(8,128)S(1)} %copy.179, f32[2,48,6,128,64]{3,4,0,2,1:T(8,128)} %get-tuple-element.218, s32[48]{0:T(128)S(1)} %copy-done.63), kind=kOutput, calls=%fused_computation.39 | convolution fusion | flops 2722632192 | bytes 38142144 | tf_op jit(solution)/shard_map/cn,dchfe->dnhfe/dot_general | solution.py:261
  1072.3 29.8 %fusion.27 = f32[48,6,64,64,1]{3,2,4,1,0:T(8,128)} fusion(f32[2,48,6,128,64]{3,1,4,2,0:T(8,128)} %add_bitcast_fusion, f32[48,64,6,128]{3,1,2,0:T(8,128)S(1)} %bitcast.266, f32[2,48,64]{2,0,1:T(2,128)S(1)} %copy-done.27), kind=kOutput, calls=%fused_computation.37 | convolution fusion | flops 3628597248 | bytes 33054720 | tf_op jit(solution)/shard_map/dcjhf,dchfe->cjhe/dot_general | solution.py:275
  1102.1 22.7 %fusion.39 = bf16[48,64,6,64]{1,3,2,0:T(8,128)(2,1)} fusion(f32[48,6,64,64,1]{3,2,4,1,0:T(8,128)} %fusion.27, f32[48,6,64,64]{2,3,1,0:T(8,128)} %get-tuple-element.212, f32[48,64,64]{1,2,0:T(8,128)S(1)} %copy-done.17, f32[48,64,6,64]{1,3,2,0:T(8,128)} %copy.164, f32[48,64,6]{1,2,0:T(8,128)S(1)} %copy-done.46), kind=kOutput, calls=%fused_computation.57 | convolution fusion | flops 910688256 | bytes 17375232 | tf_op jit(solution)/shard_map/chij,cihe->cjhe/dot_general | solution.py:170
  1124.8 28.5 %fusion.20 = f32[48,64,6,128]{3,1,2,0:T(8,128)} fusion(f32[2,48,6,128]{3,0,2,1:T(2,128)S(1)} %copy.182, f32[2,48,64]{2,0,1:T(2,128)S(1)} %copy-done.27, bf16[48,64,6,64,1]{3,1,4,2,0:T(8,128)(2,1)} %copy.207, f32[2,48,6,128,64]{3,1,4,2,0:T(8,128)} %add_bitcast_fusion), kind=kOutput, calls=%fused_computation.29 | convolution fusion | flops 3635675136 | bytes 30990336 | tf_op jit(solution)/shard_map/dchfe,cjhe->dcjhf/dot_general | solution.py:270
  1153.4 15.5 bitcast_add_fusion.3
  1168.9 9.4 copy.183
  1190.4 14.8 fusion.174
  1205.1 8.6 copy.227
  1218.6 8.6 copy.228
  1246.7 8.2 convolution_convert_fusion.1
  1255.0 13.2 fusion.184
  1268.2 13.9 fusion.183
  1291.6 8.3 fusion.96
  1299.9 14.4 reduce-scatter.11.cloned.1.call-done
  1323.0 35.5 %all-reduce = (f32[768]{0:T(1024)}, f32[768]{0:T(1024)}) all-reduce(f32[768]{0:T(1024)S(1)} %get-tuple-element.191, f32[768]{0:T(1024)S(1)} %get-tuple-element.192), channel_id=1, replica_groups=mesh['batch'=4,'ctx'=4,'heads'=2] {'batch','ctx'}, use_global_device_ids=true, to_apply=%region_39.40 | all-reduce | flops 1536 | bytes 12288 | tf_op jit(solution)/shard_map/psum | solution.py:316
  1363.2 223.8 %all-reduce.5.cloned.1.call-done = (f32[768,3,384]{2,0,1:T(8,128)}, f32[6,64,64]{2,1,0:T(8,128)}, f32[6,64,64]{2,1,0:T(8,128)}, f32[384,768]{1,0:T(8,128)}, f32[768,1536]{1,0:T(8,128)}, /*index=5*/f32[1536,768]{1,0:T(8,128)}) async-done(((f32[768,3,384]{2,0,1:T(8,128)}, f32[6,64,64]{2,1,0:T(8,128)}, f32[6,64,64]{2,1,0:T(8,128)}, f32[384,768]{1,0:T(8,128)}, f32[768,1536]{1,0:T(8,128)}, ...) | async-done | bytes 14352400 | tf_op jit(solution)/shard_map/psum | solution.py:316
  (323 shorter events, 321.6 us)
Async XLA Ops:
  7.2 532.5 %copy-start = (bf16[768,1536]{1,0:T(8,128)(2,1)S(1)}, bf16[768,1536]{1,0:T(8,128)(2,1)}, u32[]{:S(2)}) copy-start(bf16[768,1536]{1,0:T(8,128)(2,1)} %param.23) | copy-start | bytes 7077892
  7.2 72.9 %all-gather.9.cloned.1.call-start = ((), (), s32[]{:S(2)}) async-start(), calls=%async_computation.4 | async-start | bytes 7077888 | tf_op jit(solution)/shard_map/all_gather | solution.py:203
  14.6 454.9 %reduce-scatter.5.cloned.1.call-start = ((), (), s32[]{:S(2)}) async-start(), calls=%async_computation.5 | async-start | bytes 7077888 | tf_op jit(solution)/shard_map/reduce_scatter | solution.py:216
  19.5 261.6 %copy-start.62 = (s32[48]{0:T(128)}, s32[48]{0:T(128)S(1)}, u32[]{:S(2)}) copy-start(s32[48]{0:T(128)S(1)} %iota_add_fusion) | copy-start | bytes 580
  98.1 92.2 %copy-start.41 = (f32[3072,6]{0,1:T(8,128)}, f32[3072,6]{0,1:T(8,128)S(1)}, u32[]{:S(2)}) copy-start(f32[3072,6]{0,1:T(8,128)S(1)} %get-tuple-element.209) | copy-start | bytes 221188
  103.7 104.6 %copy-start.43 = (f32[3072,6]{0,1:T(8,128)}, f32[3072,6]{0,1:T(8,128)S(1)}, u32[]{:S(2)}) copy-start(f32[3072,6]{0,1:T(8,128)S(1)} %get-tuple-element.207) | copy-start | bytes 221188
  114.8 18.0 %copy-start.39 = (f32[3072,6]{0,1:T(8,128)}, f32[3072,6]{0,1:T(8,128)S(1)}, u32[]{:S(2)}) copy-start(f32[3072,6]{0,1:T(8,128)S(1)} %get-tuple-element.203) | copy-start | bytes 221188
  277.4 39.7 %slice-start = ((s8[9437184]{0:T(1024)(128)(4,1)}), s8[1048576]{0:T(1024)(128)(4,1)S(1)}, s32[]{:S(2)}) async-start(s8[9437184]{0:T(1024)(128)(4,1)} %bitcast.259), calls=%async_computation.13 | async-start | bytes 2097152
  281.0 36.1 %copy-start.23 = (f32[2,6,128,48]{2,3,1,0:T(8,128)}, f32[2,6,128,48]{2,3,1,0:T(8,128)S(1)}, u32[]{:S(2)}) copy-start(f32[2,6,128,48]{2,3,1,0:T(8,128)S(1)} %convolution_add_fusion.1) | copy-start | bytes 884740
  281.0 36.1 %slice-start.1 = ((s8[9437184]{0:T(1024)(128)(4,1)}), s8[4194304]{0:T(1024)(128)(4,1)S(1)}, s32[]{:S(2)}) async-start(s8[9437184]{0:T(1024)(128)(4,1)} %bitcast.259), calls=%async_computation.14 | async-start | bytes 8388608
  281.1 36.1 %slice-start.2 = ((s8[9437184]{0:T(1024)(128)(4,1)}), s8[4194304]{0:T(1024)(128)(4,1)S(1)}, s32[]{:S(2)}) async-start(s8[9437184]{0:T(1024)(128)(4,1)} %bitcast.259), calls=%async_computation.15 | async-start | bytes 8388608
  281.1 36.1 %copy-start.26 = (f32[2,48,64]{2,0,1:T(2,128)S(1)}, f32[2,48,64]{2,0,1:T(2,128)}, u32[]{:S(2)}) copy-start(f32[2,48,64]{2,0,1:T(2,128)} %copy.153) | copy-start | bytes 73732
  332.4 29.6 %copy-start.34 = (f32[48,6,1,64,1]{3,2,4,1,0:T(1,128)}, f32[48,6,1,64,1]{3,2,4,1,0:T(1,128)S(1)}, u32[]{:S(2)}) copy-start(f32[48,6,1,64,1]{3,2,4,1,0:T(1,128)S(1)} %fusion.8) | copy-start | bytes 221188
  332.4 29.6 %copy-start.31 = (f32[48,6,64]{2,1,0:T(8,128)S(1)}, f32[48,6,64]{2,1,0:T(8,128)}, u32[]{:S(2)}) copy-start(f32[48,6,64]{2,1,0:T(8,128)} %get-tuple-element.211) | copy-start | bytes 221188
  362.0 539.7 %copy-start.45 = (f32[48,64,6]{1,2,0:T(8,128)}, f32[48,64,6]{1,2,0:T(8,128)S(1)}, u32[]{:S(2)}) copy-start(f32[48,64,6]{1,2,0:T(8,128)S(1)} %fusion.140) | copy-start | bytes 221188
  398.4 76.1 %copy-start.57 = (f32[768]{0:T(1024)S(1)}, f32[768]{0:T(1024)}, u32[]{:S(2)}) copy-start(f32[768]{0:T(1024)} %param.22) | copy-start | bytes 9220
  398.4 141.2 %all-gather.11.cloned.1.call-start = ((), (), s32[]{:S(2)}) async-start(), calls=%async_computation.6 | async-start | bytes 7077888 | tf_op jit(solution)/shard_map/all_gather | solution.py:225
  476.8 127.0 %all-gather.13.cloned.1.call-start = ((), (), s32[]{:S(2)}) async-start(), calls=%async_computation.8 | async-start | bytes 7077888 | tf_op jit(solution)/shard_map/all_gather | solution.py:235
  477.4 220.4 %reduce-scatter.9.cloned.1.call-start = ((), (), s32[]{:S(2)}) async-start(), calls=%async_computation.9 | async-start | bytes 7077888 | tf_op jit(solution)/shard_map/reduce_scatter | solution.py:245
  637.7 122.3 %reduce-scatter.7.cloned.1.call-start = ((), (), s32[]{:S(2)}) async-start(), calls=%async_computation.7 | async-start | bytes 7077888 | tf_op jit(solution)/shard_map/reduce_scatter | solution.py:228
  652.1 45.7 %copy-start.4 = (bf16[1536,768]{1,0:T(8,128)(2,1)S(1)}, bf16[1536,768]{1,0:T(8,128)(2,1)}, u32[]{:S(2)}) copy-start(bf16[1536,768]{1,0:T(8,128)(2,1)} %param.15) | copy-start | bytes 7077892
  652.1 177.1 %all-gather.15.cloned.1.call-start = ((), (), s32[]{:S(2)}) async-start(), calls=%async_computation.10 | async-start | bytes 7077888 | tf_op jit(solution)/shard_map/all_gather | solution.py:250
  766.4 547.8 %reduce-scatter.11.cloned.1.call-start = ((), (), s32[]{:S(2)}) async-start(), calls=%async_computation.11 | async-start | bytes 7077888 | tf_op jit(solution)/shard_map/reduce_scatter | solution.py:298
  857.0 20.8 %slice-start.3 = ((s8[9437184]{0:T(1024)(128)(4,1)}), s8[1048576]{0:T(1024)(128)(4,1)S(1)}, s32[]{:S(2)}) async-start(s8[9437184]{0:T(1024)(128)(4,1)} %bitcast.261), calls=%async_computation.16 | async-start | bytes 2097152
  857.0 20.8 %slice-start.4 = ((s8[9437184]{0:T(1024)(128)(4,1)}), s8[4194304]{0:T(1024)(128)(4,1)S(1)}, s32[]{:S(2)}) async-start(s8[9437184]{0:T(1024)(128)(4,1)} %bitcast.261), calls=%async_computation.17 | async-start | bytes 8388608
  866.5 92.3 %copy-start.29 = (f32[48,6,64]{2,1,0:T(8,128)}, f32[48,6,64]{2,1,0:T(8,128)S(1)}, u32[]{:S(2)}) copy-start(f32[48,6,64]{2,1,0:T(8,128)S(1)} %bitcast_divide_fusion.1) | copy-start | bytes 221188
  940.0 18.8 %copy-start.16 = (f32[48,64,64]{1,2,0:T(8,128)S(1)}, f32[48,64,64]{1,2,0:T(8,128)}, u32[]{:S(2)}) copy-start(f32[48,64,64]{1,2,0:T(8,128)} %compare_select_fusion) | copy-start | bytes 2359300
  953.6 19.8 %copy-start.25 = (f32[48,6,1,2,128]{4,2,3,1,0:T(1,128)}, f32[48,6,1,2,128]{4,2,3,1,0:T(1,128)S(1)}, u32[]{:S(2)}) copy-start(f32[48,6,1,2,128]{4,2,3,1,0:T(1,128)S(1)} %fusion.4) | copy-start | bytes 884740
  1033.3 39.0 %slice-start.6 = ((s8[9437184]{0:T(1024)(128)(4,1)}), s8[1048576]{0:T(1024)(128)(4,1)S(1)}, s32[]{:S(2)}) async-start(s8[9437184]{0:T(1024)(128)(4,1)} %bitcast.265), calls=%async_computation.19 | async-start | bytes 2097152
  1036.6 35.6 %slice-start.7 = ((s8[9437184]{0:T(1024)(128)(4,1)}), s8[4194304]{0:T(1024)(128)(4,1)S(1)}, s32[]{:S(2)}) async-start(s8[9437184]{0:T(1024)(128)(4,1)} %bitcast.265), calls=%async_computation.20 | async-start | bytes 8388608
  1036.7 35.6 %slice-start.8 = ((s8[9437184]{0:T(1024)(128)(4,1)}), s8[4194304]{0:T(1024)(128)(4,1)S(1)}, s32[]{:S(2)}) async-start(s8[9437184]{0:T(1024)(128)(4,1)} %bitcast.265), calls=%async_computation.21 | async-start | bytes 8388608
  1072.3 29.9 %copy-start.17 = (f32[48,64,64]{1,2,0:T(8,128)S(1)}, f32[48,64,64]{1,2,0:T(8,128)}, u32[]{:S(2)}) copy-start(f32[48,64,64]{1,2,0:T(8,128)} %compare_select_fusion) | copy-start | bytes 2359300
  1072.3 29.8 %copy-start.46 = (f32[48,64,6]{1,2,0:T(8,128)S(1)}, f32[48,64,6]{1,2,0:T(8,128)}, u32[]{:S(2)}) copy-start(f32[48,64,6]{1,2,0:T(8,128)} %copy-done.45) | copy-start | bytes 221188
  1124.8 28.5 %copy-start.30 = (f32[48,6,64]{2,1,0:T(8,128)S(1)}, f32[48,6,64]{2,1,0:T(8,128)}, u32[]{:S(2)}) copy-start(f32[48,6,64]{2,1,0:T(8,128)} %copy-done.29) | copy-start | bytes 221188
  1254.9 332.1 %all-reduce.5.cloned.1.call-start = ((), (), s32[]{:S(2)}) async-start(), calls=%async_computation.12 | async-start | bytes 29097984 | tf_op jit(solution)/shard_map/psum | solution.py:316
  1255.0 27.1 %slice-start.9 = ((s8[4718592]{0:T(1024)(128)(4,1)}), s8[4194304]{0:T(1024)(128)(4,1)S(1)}, s32[]{:S(2)}) async-start(s8[4718592]{0:T(1024)(128)(4,1)} %bitcast.268), calls=%async_computation.22 | async-start | bytes 8388608
  1255.0 27.1 %slice-start.13 = ((s8[7077888]{0:T(1024)(128)(4,1)}), s8[4194304]{0:T(1024)(128)(4,1)S(1)}, s32[]{:S(2)}) async-start(s8[7077888]{0:T(1024)(128)(4,1)} %bitcast.277), calls=%async_computation.26 | async-start | bytes 8388608
  1255.0 30.3 %slice-start.11 = ((s8[4718592]{0:T(1024)(128)(4,1)}), s8[4194304]{0:T(1024)(128)(4,1)S(1)}, s32[]{:S(2)}) async-start(s8[4718592]{0:T(1024)(128)(4,1)} %bitcast.270), calls=%async_computation.24 | async-start | bytes 8388608
  1255.0 33.4 %slice-start.23 = ((s8[4718592]{0:T(1024)(128)(4,1)}), s8[4194304]{0:T(1024)(128)(4,1)S(1)}, s32[]{:S(2)}) async-start(s8[4718592]{0:T(1024)(128)(4,1)} %bitcast.304), calls=%async_computation.36 | async-start | bytes 8388608
  1268.2 13.9 slice-start.10
  1268.2 14.0 slice-start.14
  1268.2 17.1 %slice-start.12 = ((s8[4718592]{0:T(1024)(128)(4,1)}), s8[524288]{0:T(1024)(128)(4,1)S(1)}, s32[]{:S(2)}) async-start(s8[4718592]{0:T(1024)(128)(4,1)} %bitcast.270), calls=%async_computation.25 | async-start | bytes 1048576
  1268.2 20.3 %slice-start.24 = ((s8[4718592]{0:T(1024)(128)(4,1)}), s8[524288]{0:T(1024)(128)(4,1)S(1)}, s32[]{:S(2)}) async-start(s8[4718592]{0:T(1024)(128)(4,1)} %bitcast.304), calls=%async_computation.37 | async-start | bytes 1048576
  1299.8 14.4 copy-start.5
  1299.8 14.4 copy-start.48
  1299.8 14.4 copy-start.52
  1299.8 14.4 copy-start.59
  1299.9 18.1 %copy-start.60 = (f32[768]{0:T(1024)S(1)}, f32[768]{0:T(1024)}, u32[]{:S(2)}) copy-start(f32[768]{0:T(1024)} %get-tuple-element.153) | copy-start | bytes 9220
  (52 other events, 289.1 us)
Sparse Core Ops, SparseCore 0:
  14.8 65.3 all-gather.8
  398.5 70.9 reduce-scatter.4
  477.0 62.6 all-gather.10
  541.1 62.6 all-gather.12
  637.8 59.9 reduce-scatter.8
  700.0 59.9 reduce-scatter.6
  766.6 62.6 all-gather.14
  1255.1 59.1 reduce-scatter.10
  1320.1 266.9 all-reduce.4
where the time goes:
time: 1620 us; the launch traced here: 1610 us
  waiting for transfers between devices  642 us (40%)
  matrix products  523 us (32%)
  local copies, waits for them, and re-layouts  234 us (14%)
  other arithmetic  122 us (8%)
  blocking collectives  69.2 us (4%)
    psum x1, waiting for transfers between devices, shards(): lax.psum((grad_w_qkv, grad_f_query, grad_f_key, grad_w_out, grad_w_up, gr...  224 us
    reduce_scatter x1, waiting for transfers between devices, shards(): lax.psum_scatter(jnp.dot(attended, w_out, preferred_element_type=jnp.floa...  71.1 us
    unnamed x193, local copies, waits for them, and re-layouts  67.7 us
    all_gather x1, waiting for transfers between devices, shards(): resid_full = lax.all_gather(grad_resid, 'heads', axis=0, tiled=True)  62.5 us
    all_gather x1, waiting for transfers between devices, shards(): gathered_two = lax.all_gather(scaled_two_low, 'heads', axis=0, tiled=True)  61.7 us
    all_gather x1, waiting for transfers between devices, shards(): gathered_one = lax.all_gather(scaled_low, 'heads', axis=0, tiled=True)  59 us
    reduce_scatter x1, waiting for transfers between devices, shards(): lax.psum_scatter(jnp.dot(activation, w_down, preferred_element_type=jnp.f...  57 us
    all_gather x1, waiting for transfers between devices, shards(): cot_full = lax.all_gather(d_out, 'heads', axis=0, tiled=True)  45.8 us
  transfers between devices with their start and end apart: 9, of which 9 were waited for; matrix products, arithmetic and copies ran while one was open for 6% of the time, Pallas kernels for 0%

commit v1 on v0

v1 whole, which is shorter than its diff:
```python
import functools

import jax
import jax.numpy as jnp
from jax import lax
from jax.experimental import pallas as pl
from jax.experimental.pallas import tpu as pltpu
from jax.sharding import PartitionSpec as P

epsilon = 1e-05
f32 = jnp.float32
bf16 = jnp.bfloat16
CHUNK = 256
VMEM_LIMIT = 60 * 1024 * 1024
GELU_A = 0.7978845608028654
GELU_B = 0.044715


def dot(left, right):
    return lax.dot_general(left, right, (((1,), (0,)), ((), ())), preferred_element_type=f32)


def dot_t(left, right):
    return lax.dot_general(left, right, (((1,), (1,)), ((), ())), preferred_element_type=f32)


def params():
    return pltpu.CompilerParams(
        dimension_semantics=("arbitrary",), vmem_limit_bytes=VMEM_LIMIT
    )


def cost(flops, bytes_accessed):
    return pl.CostEstimate(flops=int(flops), bytes_accessed=int(bytes_accessed), transcendentals=0)


def once(shape):
    zeros = (0,) * len(shape)
    return pl.BlockSpec(shape, lambda *_: zeros, pipeline_mode=pl.Buffered(1))


def first_lanes():
    return lax.broadcasted_iota(jnp.int32, (1, 128), 1) < 64


def first_sublanes():
    return lax.broadcasted_iota(jnp.int32, (128, 1), 0) < 64


def half_blocks(size):
    rows = lax.broadcasted_iota(jnp.int32, (size, size), 0) // 64
    cols = lax.broadcasted_iota(jnp.int32, (size, size), 1) // 64
    return rows, cols


def soft_halves(logits, ones_blocks):
    first = first_lanes()
    parts = []
    for h in range(2):
        own = logits[:, 128 * h : 128 * h + 128]
        low = jnp.max(jnp.where(first, own, -jnp.inf), axis=1, keepdims=True)
        high = jnp.max(jnp.where(first, -jnp.inf, own), axis=1, keepdims=True)
        parts.append(jnp.exp(own - jnp.where(first, low, high)))
    grown = jnp.concatenate(parts, axis=1)
    return grown / dot(grown.astype(bf16), ones_blocks)


def norm_parts(values):
    centred = values - jnp.mean(values, axis=1, keepdims=True)
    spread = lax.rsqrt(jnp.mean(centred * centred, axis=1, keepdims=True) + epsilon)
    return centred * spread, spread


def norm_back(gradient, normed, spread, gain):
    scaled = gradient * gain
    return spread * (
        scaled
        - jnp.mean(scaled, axis=1, keepdims=True)
        - normed * jnp.mean(scaled * normed, axis=1, keepdims=True)
    )


def norm_kernel(tokens, gain, h_out):
    normed, _ = norm_parts(tokens[...].astype(f32))
    h_out[...] = (normed * gain[...]).astype(bf16)


def norm_one(tokens, gain):
    rows, width = tokens.shape
    return pl.pallas_call(
        norm_kernel,
        grid=(rows // 512,),
        in_specs=[pl.BlockSpec((512, width), lambda c: (c, 0)), once((1, width))],
        out_specs=pl.BlockSpec((512, width), lambda c: (c, 0)),
        out_shape=jax.ShapeDtypeStruct((rows, width), bf16),
        compiler_params=params(),
        cost_estimate=cost(0, 4 * rows * width),
        name="norm_one",
    )(tokens, gain)


def keys_kernel(pairs, h, w_kv, fext, ones, k_out, v_out, phi_out, prefix_out, state_out, state):
    step = pl.program_id(0)
    wide = 128 * pairs

    @pl.when(step == 0)
    def _():
        state[...] = jnp.zeros_like(state)

    prefix_out[0] = state[...].astype(bf16)
    kv = dot(h[...], w_kv[...]).astype(bf16)
    k_out[...] = kv[:, :wide]
    v_out[...] = kv[:, wide:]
    top = first_sublanes()
    for p in range(pairs):
        k_two = kv[:, 128 * p : 128 * p + 128]
        v_two = kv[:, wide + 128 * p : wide + 128 * p + 128]
        phi = soft_halves(dot(k_two, fext[p]), ones[...]).astype(bf16)
        phi_out[:, 256 * p : 256 * p + 256] = phi
        turned = v_two.astype(f32).T
        for h_at in range(2):
            sel = top if h_at == 0 else jnp.logical_not(top)
            padded = jnp.where(sel, turned, 1.0).astype(bf16)
            state[2 * p + h_at] += dot(padded, phi[:, 128 * h_at : 128 * h_at + 128])

    @pl.when(step == pl.num_programs(0) - 1)
    def _():
        write_state(state, state_out, pairs)


def write_state(state, state_out, pairs):
    top = first_sublanes()
    sums = []
    for p in range(pairs):
        state_out[128 * p : 128 * p + 128] = jnp.where(top, state[2 * p], state[2 * p + 1])
        sums.append(state[2 * p, 64:65, :])
        sums.append(state[2 * p + 1, 0:1, :])
    tail = state_out.shape[0] - 128 * pairs
    sums.append(jnp.zeros((tail - 2 * pairs, 128), f32))
    state_out[128 * pairs :] = jnp.concatenate(sums, axis=0)


def read_state(packed, p, h_at, pairs):
    row = 128 * pairs + 2 * p + h_at
    whole = packed[128 * p : 128 * p + 128, :]
    sums = packed[row : row + 1, :]
    sel = first_sublanes() if h_at == 0 else jnp.logical_not(first_sublanes())
    return jnp.where(sel, whole, sums)


def key_pass(h, w_kv, fext, ones):
    rows, width = h.shape
    pairs = fext.shape[0]
    wide = 128 * pairs
    count = rows // CHUNK
    packed = wide + 16
    return pl.pallas_call(
        functools.partial(keys_kernel, pairs),
        grid=(count,),
        in_specs=[
            pl.BlockSpec((CHUNK, width), lambda c: (c, 0)),
            once(w_kv.shape),
            once(fext.shape),
            once(ones.shape),
        ],
        out_specs=[
            pl.BlockSpec((CHUNK, wide), lambda c: (c, 0)),
            pl.BlockSpec((CHUNK, wide), lambda c: (c, 0)),
            pl.BlockSpec((CHUNK, 2 * wide), lambda c: (c, 0)),
            pl.BlockSpec((1, 2 * pairs, 128, 128), lambda c: (c, 0, 0, 0)),
            pl.BlockSpec((packed, 128), lambda c: (0, 0)),
        ],
        out_shape=[
            jax.ShapeDtypeStruct((rows, wide), bf16),
            jax.ShapeDtypeStruct((rows, wide), bf16),
            jax.ShapeDtypeStruct((rows, 2 * wide), bf16),
            jax.ShapeDtypeStruct((count, 2 * pairs, 128, 128), bf16),
            jax.ShapeDtypeStruct((packed, 128), f32),
        ],
        scratch_shapes=[pltpu.VMEM((2 * pairs, 128, 128), f32)],
        compiler_params=params(),
        cost_estimate=cost(6 * rows * width * wide, 12 * rows * width),
        name="key_pass",
    )(h, w_kv, fext, ones)


def query_kernel(pairs, h, w_q, k_phi, v, prefix, fext, ones, q_out, phi_out, numer_out):
    q = dot(h[...], w_q[...]).astype(bf16)
    q_out[...] = q
    first = first_lanes()
    size = h.shape[0]
    past = lax.broadcasted_iota(jnp.int32, (size, size), 0) >= lax.broadcasted_iota(
        jnp.int32, (size, size), 1
    )
    for p in range(pairs):
        phi = soft_halves(dot(q[:, 128 * p : 128 * p + 128], fext[p]), ones[...]).astype(bf16)
        phi_out[:, 256 * p : 256 * p + 256] = phi
        v_two = v[:, 128 * p : 128 * p + 128].astype(f32)
        for h_at in range(2):
            at = 256 * p + 128 * h_at
            sel = first if h_at == 0 else jnp.logical_not(first)
            padded = jnp.where(sel, v_two, 1.0).astype(bf16)
            phi_q = phi[:, 128 * h_at : 128 * h_at + 128]
            scores = jnp.where(past, dot_t(phi_q, k_phi[:, at : at + 128]), 0.0).astype(bf16)
            numer_out[:, at : at + 128] = dot(scores, padded) + dot_t(
                phi_q, prefix[0, 2 * p + h_at]
            )


def query_pass(h, w_q, k_phi, v, prefix, fext, ones):
    rows, width = h.shape
    pairs = fext.shape[0]
    wide = 128 * pairs
    return pl.pallas_call(
        functools.partial(query_kernel, pairs),
        grid=(rows // CHUNK,),
        in_specs=[
            pl.BlockSpec((CHUNK, width), lambda c: (c, 0)),
            once(w_q.shape),
            pl.BlockSpec((CHUNK, 2 * wide), lambda c: (c, 0)),
            pl.BlockSpec((CHUNK, wide), lambda c: (c, 0)),
            pl.BlockSpec((1, 2 * pairs, 128, 128), lambda c: (c, 0, 0, 0)),
            once(fext.shape),
            once(ones.shape),
        ],
        out_specs=[
            pl.BlockSpec((CHUNK, wide), lambda c: (c, 0)),
            pl.BlockSpec((CHUNK, 2 * wide), lambda c: (c, 0)),
            pl.BlockSpec((CHUNK, 2 * wide), lambda c: (c, 0)),
        ],
        out_shape=[
            jax.ShapeDtypeStruct((rows, wide), bf16),
            jax.ShapeDtypeStruct((rows, 2 * wide), bf16),
            jax.ShapeDtypeStruct((rows, 2 * wide), f32),
        ],
        compiler_params=params(),
        cost_estimate=cost(5 * rows * width * wide, 16 * rows * width),
        name="query_pass",
    )(h, w_q, k_phi, v, prefix, fext, ones)


def middle_kernel(
    pairs,
    tile,
    tokens,
    d_out,
    numer_own,
    numer_oth,
    phi_own,
    phi_oth,
    incoming,
    wo_own,
    wo_oth,
    up_own,
    up_oth,
    down_own,
    down_oth,
    gain,
    cross,
    attended_out,
    act_out,
    pre_out,
    h_out,
    mixed_out,
    resid_out,
    gn_out,
    gd_out,
    state_out,
    held,
    exact,
    inverse,
    state,
):
    step = pl.program_id(0)
    first = first_lanes()
    top = first_sublanes()
    wide = 128 * pairs
    numer = (numer_own, numer_oth)
    phi = (phi_own, phi_oth)

    @pl.when(step == 0)
    def _():
        state[...] = jnp.zeros_like(state)
        for half in range(2):
            for p in range(pairs):
                for h_at in range(2):
                    held[half, 2 * p + h_at] = read_state(
                        incoming.at[half], p, h_at, pairs
                    ).astype(bf16)

    for half in range(2):
        for p in range(pairs):
            sums = []
            for h_at in range(2):
                at = 256 * p + 128 * h_at
                sums.append(
                    numer[half][:, at : at + 128]
                    + dot_t(phi[half][:, at : at + 128], held[half, 2 * p + h_at])
                )
            numerator = jnp.where(first, sums[0], sums[1])
            swapped = 1.0 / jnp.where(first, sums[1], sums[0])
            inv = pltpu.roll(swapped, 64, 1)
            value = numerator * inv
            at = wide * half + 128 * p
            exact[:, at : at + 128] = value
            inverse[:, at : at + 128] = swapped
            attended_out[:, at : at + 128] = value.astype(bf16)

    resid = (
        tokens[...].astype(f32)
        + dot(attended_out[:, :wide], wo_own[...])
        + dot(attended_out[:, wide:], wo_oth[...])
    )
    normed, spread = norm_parts(resid)
    h_two = (normed * gain[...]).astype(bf16)
    h_out[...] = h_two
    d_low = d_out[...]
    units = up_own.shape[1]
    mixed = grad_h = None
    for half in range(2):
        up = (up_own, up_oth)[half]
        down = (down_own, down_oth)[half]
        for at in range(0, units, tile):
            pre = dot(h_two, up[:, at : at + tile])
            square = pre * pre
            swing = jnp.tanh(GELU_A * pre * (1.0 + GELU_B * square))
            half_up = 0.5 + 0.5 * swing
            act = (pre * half_up).astype(bf16)
            slope = half_up + (0.5 * GELU_A) * pre * (1.0 - swing * swing) * (
                1.0 + (3.0 * GELU_B) * square
            )
            grad_act = dot_t(d_low, down[at : at + tile, :])
            grad_pre = (grad_act * slope).astype(bf16)
            act_out[:, half * units + at : half * units + at + tile] = act
            pre_out[:, half * units + at : half * units + at + tile] = grad_pre
            part = dot(act, down[at : at + tile, :])
            mixed = part if mixed is None else mixed + part
            part = dot_t(grad_pre, up[:, at : at + tile])
            grad_h = part if grad_h is None else grad_h + part
    mixed_out[...] = (resid + mixed).astype(bf16)
    grad_resid = (d_low.astype(f32) + norm_back(grad_h, normed, spread, gain[...])).astype(bf16)
    resid_out[...] = grad_resid

    for half in range(2):
        grad_att = dot_t(grad_resid, (wo_own, wo_oth)[half][...]).astype(bf16).astype(f32)
        for p in range(pairs):
            at = wide * half + 128 * p
            own = grad_att[:, 128 * p : 128 * p + 128]
            swapped = inverse[:, at : at + 128]
            grad_n = own * pltpu.roll(swapped, 64, 1)
            total = dot((own * exact[:, at : at + 128]).astype(bf16), cross[...])
            grad_d = (-1.0 / 64.0) * total * swapped
            gn_out[:, at : at + 128] = grad_n.astype(bf16)
            gd_out[:, at : at + 128] = grad_d.astype(bf16)
            turned_n = grad_n.T
            turned_d = grad_d.T
            for h_at in range(2):
                sel = top if h_at == 0 else jnp.logical_not(top)
                padded = jnp.where(sel, turned_n, turned_d).astype(bf16)
                lane = 256 * p + 128 * h_at
                state[half, 2 * p + h_at] += dot(padded, phi[half][:, lane : lane + 128])

    @pl.when(step == pl.num_programs(0) - 1)
    def _():
        for half in range(2):
            write_state(state.at[half], state_out.at[half], pairs)


def middle_pass(
    tokens, d_out, numers, phis, incoming, w_outs, w_ups, w_downs, gain, cross, block, tile
):
    rows, width = tokens.shape
    wide = w_outs[0].shape[0]
    pairs = wide // 128
    units = w_ups[0].shape[1]
    by_rows = lambda cols: pl.BlockSpec((block, cols), lambda c: (c, 0))
    out = lambda cols: jax.ShapeDtypeStruct((rows, cols), bf16)
    cols_out = [2 * wide, 2 * units, 2 * units, width, width, width, 2 * wide, 2 * wide]
    return pl.pallas_call(
        functools.partial(middle_kernel, pairs, tile),
        grid=(rows // block,),
        in_specs=[by_rows(width)] * 2
        + [by_rows(2 * wide)] * 4
        + [once(incoming.shape)]
        + [once(w.shape) for w in (*w_outs, *w_ups, *w_downs)]
        + [once(gain.shape), once(cross.shape)],
        out_specs=[by_rows(c) for c in cols_out]
        + [pl.BlockSpec(incoming.shape, lambda c: (0, 0, 0))],
        out_shape=[out(c) for c in cols_out] + [jax.ShapeDtypeStruct(incoming.shape, f32)],
        scratch_shapes=[
            pltpu.VMEM((2, 2 * pairs, 128, 128), bf16),
            pltpu.VMEM((block, 2 * wide), f32),
            pltpu.VMEM((block, 2 * wide), f32),
            pltpu.VMEM((2, 2 * pairs, 128, 128), f32),
        ],
        compiler_params=params(),
        cost_estimate=cost(
            2 * rows * width * (8 * units + 8 * wide), 20 * rows * (units + width)
        ),
        name="middle_pass",
    )(tokens, d_out, *numers, *phis, incoming, *w_outs, *w_ups, *w_downs, gain, cross)


def weight_kernel(steps, half, *refs):
    count = len(steps)
    lefts, rights = refs[:count], refs[count : 2 * count]
    outs, turned = refs[2 * count : 2 * count + 2], refs[2 * count + 2]
    step = pl.program_id(0)
    whole = sum(steps)

    @pl.when(step == 0)
    def _():
        for i in range(count):
            turned[i] = lefts[i][...].T

    start = 0
    for i in range(count):

        def product(i=i):
            return dot(turned[i], rights[i][...]).astype(bf16)

        for side in range(2):
            low = side * whole + start

            @pl.when(jnp.logical_and(step >= low, step < low + steps[i]))
            def _(product=product, side=side):
                outs[1 - side][...] = product()

        start += steps[i]


def weight_pass(half, lefts, rights, block):
    rows, width = lefts[0].shape
    part = width // 2
    count = len(lefts)
    steps = [r.shape[1] // 2 // block for r in rights]
    whole = sum(steps)

    def right_map(i):
        start = sum(steps[:i])

        def at(step, half):
            place = step % whole - start
            inside = jnp.clip(place, 0, steps[i] - 1)
            return (0, (1 - step // whole) * steps[i] + inside)

        return at

    own_map = lambda step, half: (0, jnp.maximum(step - whole, 0))
    oth_map = lambda step, half: (0, jnp.minimum(step, whole - 1))
    spec = pltpu.PrefetchScalarGridSpec(
        num_scalar_prefetch=1,
        grid=(2 * whole,),
        in_specs=[
            pl.BlockSpec((rows, part), lambda step, half: (0, half[0]), pipeline_mode=pl.Buffered(1))
            for _ in lefts
        ]
        + [pl.BlockSpec((rows, block), right_map(i)) for i in range(count)],
        out_specs=[pl.BlockSpec((part, block), own_map), pl.BlockSpec((part, block), oth_map)],
        scratch_shapes=[pltpu.VMEM((count, part, rows), bf16)],
    )
    shape = jax.ShapeDtypeStruct((part, whole * block), bf16)
    return pl.pallas_call(
        functools.partial(weight_kernel, steps),
        grid_spec=spec,
        out_shape=[shape, shape],
        compiler_params=params(),
        cost_estimate=cost(
            2 * rows * part * 2 * whole * block, 2 * rows * (part * count + 2 * whole * block)
        ),
        name="weight_pass",
    )(half, *lefts, *rights)


def back_kernel(
    pairs,
    at_pair,
    q_own,
    q_oth,
    k_own,
    k_oth,
    v_own,
    v_oth,
    pq_own,
    pq_oth,
    pk_own,
    pk_oth,
    gn_own,
    gn_oth,
    gd_own,
    gd_oth,
    prefix_own,
    prefix_oth,
    incoming,
    later,
    fq_own,
    fq_oth,
    fk_own,
    fk_oth,
    ones,
    grad_out,
    grad_f,
    held,
    state,
):
    step = pl.program_id(0)
    first = first_lanes()
    top = first_sublanes()
    size = q_own.shape[0]
    rows = lax.broadcasted_iota(jnp.int32, (size, size), 0)
    cols = lax.broadcasted_iota(jnp.int32, (size, size), 1)

    @pl.when(step == 0)
    def _():
        grad_f[...] = jnp.zeros_like(grad_f)
        for half in range(2):
            for h_at in range(2):
                held[half, h_at] = read_state(incoming.at[half], at_pair, h_at, pairs)
                state[half, h_at] = read_state(later.at[half], at_pair, h_at, pairs)

    for half in range(2):
        q_two = (q_own, q_oth)[half][...]
        k_two = (k_own, k_oth)[half][...]
        v_two = (v_own, v_oth)[half][...].astype(f32)
        phi_q = (pq_own, pq_oth)[half][...]
        phi_k = (pk_own, pk_oth)[half][...]
        gn = (gn_own, gn_oth)[half][...].astype(f32)
        gd = (gd_own, gd_oth)[half][...].astype(f32)
        prefix = (prefix_own, prefix_oth)[half]
        turned_n = gn.T
        turned_d = gd.T
        grads_q, grads_k, grads_v = [], [], []
        for h_at in range(2):
            sel = first if h_at == 0 else jnp.logical_not(first)
            sel_top = top if h_at == 0 else jnp.logical_not(top)
            padded_v = jnp.where(sel, v_two, 1.0).astype(bf16)
            padded_g = jnp.where(sel, gn, gd).astype(bf16)
            turned = jnp.where(sel_top, turned_n, turned_d).astype(bf16)
            pq = phi_q[:, 128 * h_at : 128 * h_at + 128]
            pk = phi_k[:, 128 * h_at : 128 * h_at + 128]
            before = (prefix[0, h_at].astype(f32) + held[half, h_at]).astype(bf16)
            after = state[half, h_at].astype(bf16)
            e = jnp.where(rows >= cols, dot_t(padded_g, padded_v), 0.0).astype(bf16)
            e_t = jnp.where(rows <= cols, dot_t(padded_v, padded_g), 0.0).astype(bf16)
            s_t = jnp.where(rows <= cols, dot_t(pk, pq), 0.0).astype(bf16)
            grads_q.append(dot(e, pk) + dot(padded_g, before))
            grads_k.append(dot(e_t, pq) + dot(padded_v, after))
            grads_v.append(dot(s_t, padded_g) + dot_t(pk, after))
            state[half, h_at] += dot(turned, pq)
        for kind in range(2):
            phi = (phi_q, phi_k)[kind].astype(f32)
            grad_phi = jnp.concatenate((grads_q, grads_k)[kind], axis=1)
            shared = dot((phi * grad_phi).astype(bf16), ones[...])
            grad_u = (phi * (grad_phi - shared)).astype(bf16)
            fext = ((fq_own, fq_oth), (fk_own, fk_oth))[kind][half]
            vectors = (q_two, k_two)[kind]
            grad_out[:, 384 * half + 128 * kind : 384 * half + 128 * kind + 128] = dot_t(
                grad_u, fext[0]
            ).astype(bf16)
            grad_f[kind, half] += dot(vectors.astype(f32).T.astype(bf16), grad_u)
        grad_out[:, 384 * half + 256 : 384 * half + 384] = jnp.where(
            first, grads_v[0], grads_v[1]
        ).astype(bf16)


def back_pass(at_pair, q, k, v, pq, pk, gn, gd, prefix, incoming, later, fq, fk, ones):
    rows = q[0].shape[0]
    pairs = fq[0].shape[0]
    count = rows // CHUNK
    lanes = lambda cols, at: pl.BlockSpec((CHUNK, cols), lambda c: (count - 1 - c, at))
    states = pl.BlockSpec((1, 2, 128, 128), lambda c: (count - 1 - c, at_pair, 0, 0))
    weights = pl.BlockSpec((1, 128, 256), lambda c: (at_pair, 0, 0))
    return pl.pallas_call(
        functools.partial(back_kernel, pairs, at_pair),
        grid=(count,),
        in_specs=[lanes(128, at_pair)] * 6
        + [lanes(256, at_pair)] * 4
        + [lanes(128, at_pair), lanes(128, pairs + at_pair)] * 2
        + [states] * 2
        + [once(incoming.shape)] * 2
        + [weights] * 4
        + [once(ones.shape)],
        out_specs=[
            pl.BlockSpec((CHUNK, 768), lambda c: (count - 1 - c, 0)),
            pl.BlockSpec((2, 2, 128, 256), lambda c: (0, 0, 0, 0)),
        ],
        out_shape=[
            jax.ShapeDtypeStruct((rows, 768), bf16),
            jax.ShapeDtypeStruct((2, 2, 128, 256), f32),
        ],
        scratch_shapes=[
            pltpu.VMEM((2, 2, 128, 128), f32),
            pltpu.VMEM((2, 2, 128, 128), f32),
        ],
        compiler_params=params(),
        cost_estimate=cost(rows * 4 * 2 * 2600 * 128, rows * 6000),
        name="back_pass",
    )(*q, *k, *v, *pq, *pk, gn, gn, gd, gd, *prefix, incoming, later, *fq, *fk, ones)


def tokens_kernel(pairs, tokens, resid, w_own, w_oth, gain, *refs):
    grads, out = refs[:pairs], refs[pairs]
    normed, spread = norm_parts(tokens[...].astype(f32))
    total = None
    for half in range(2):
        joined = jnp.concatenate(
            [
                g[:, 384 * half + 128 * kind : 384 * half + 128 * kind + 128]
                for kind in range(3)
                for g in grads
            ],
            axis=1,
        )
        part = dot_t(joined, (w_own, w_oth)[half][...])
        total = part if total is None else total + part
    back = norm_back(total, normed, spread, gain[...])
    out[...] = (resid[...].astype(f32) + back).astype(bf16)


def tokens_pass(tokens, resid, w_own, w_oth, gain, grads, block):
    rows, width = tokens.shape
    by_rows = lambda cols: pl.BlockSpec((block, cols), lambda c: (c, 0))
    return pl.pallas_call(
        functools.partial(tokens_kernel, len(grads)),
        grid=(rows // block,),
        in_specs=[by_rows(width)] * 2
        + [once(w_own.shape), once(w_oth.shape), once(gain.shape)]
        + [by_rows(768)] * len(grads),
        out_specs=by_rows(width),
        out_shape=jax.ShapeDtypeStruct((rows, width), bf16),
        compiler_params=params(),
        cost_estimate=cost(4 * rows * width * w_own.shape[1], 16 * rows * width),
        name="tokens_pass",
    )(tokens, resid, w_own, w_oth, gain, *grads)


def swap(value, axis, bit):
    count = lax.axis_size(axis)
    return lax.ppermute(value, axis, [(i, i ^ (1 << bit)) for i in range(count)])


def bit_of(axis, bit):
    return (lax.axis_index(axis) >> bit) & 1


def bits_of(axis):
    return lax.axis_size(axis).bit_length() - 1


def ordered(bit, mine, theirs):
    return jnp.where(
        bit == 0, jnp.concatenate([mine, theirs], 0), jnp.concatenate([theirs, mine], 0)
    )


def fetch_other(weight):
    count = weight.shape[0] // 2
    place = bit_of("ctx", 0)
    part = lax.dynamic_slice_in_dim(weight, place * count, count, 0)
    direct = swap(part, "heads", 0)
    return ordered(place, direct, swap(direct, "ctx", 0))


def add_low(left, right):
    return (left.astype(f32) + right.astype(f32)).astype(bf16)


def reduce_rows(sends, keeps):
    own, oth = keeps
    got_own, got_oth = swap(sends[0], "ctx", 0), swap(sends[1], "ctx", 0)
    from_pair = swap(add_low(oth, got_oth), "heads", 0)
    left, right = add_low(own, got_own), from_pair
    stages = [("ctx", b) for b in range(1, bits_of("ctx"))]
    stages += [("batch", b) for b in range(bits_of("batch"))]
    for axis, bit in stages:
        place = bit_of(axis, bit)
        count = left.shape[0] // 2
        cut = lambda a, at: lax.dynamic_slice_in_dim(a, at * count, count, 0)
        got = swap(add_low(cut(left, 1 - place), cut(right, 1 - place)), axis, bit)
        left, right = add_low(cut(left, place), cut(right, place)), got
    whole = add_low(left, right)
    for axis, bit in reversed([("ctx", 0)] + stages):
        whole = ordered(bit_of(axis, bit), whole, swap(whole, axis, bit))
    return whole


def scan_runs(total, boundary, rows, backward):
    place = lax.axis_index("ctx") * 2 + lax.axis_index("heads")
    sequence = lambda index: index * rows >= boundary
    steps = [("heads", 0)] + [("ctx", b) for b in range(bits_of("ctx"))]
    received = jnp.zeros_like(total)
    for level, (axis, bit) in enumerate(steps):
        got = swap(total.astype(bf16), axis, bit).astype(f32)
        if axis == "heads":
            got = jnp.flip(got, 0)
        size = 1 << level
        base = (place >> (level + 1)) << (level + 1)
        latter = ((place >> level) & 1) == 1
        if backward:
            near, far = sequence(base), sequence(base + size)
            takes = jnp.logical_and(jnp.logical_not(latter), far == sequence(place))
        else:
            near, far = sequence(base + 2 * size - 1), sequence(base + size - 1)
            takes = jnp.logical_and(latter, far == sequence(place))
        received = received + jnp.where(takes, got, 0.0)
        joins = (near == far).astype(f32)
        keeps_mine = jnp.logical_not(latter) if backward else latter
        total = jnp.where(keeps_mine, total + joins * got, got + joins * total)
    return received


def extended(maps):
    heads, size, _ = maps.shape
    both = jnp.concatenate([maps, -maps], axis=2).reshape(heads // 2, 2, size, 2 * size)
    empty = jnp.zeros_like(both[:, 0])
    return jnp.concatenate(
        [
            jnp.concatenate([both[:, 0], empty], axis=2),
            jnp.concatenate([empty, both[:, 1]], axis=2),
        ],
        axis=1,
    )


def map_gradient(raw):
    pairs = raw.shape[0]
    joined = jnp.stack(
        [
            raw[:, :64, 0:64] - raw[:, :64, 64:128],
            raw[:, 64:, 128:192] - raw[:, 64:, 192:256],
        ],
        axis=1,
    )
    return joined.reshape(2 * pairs * 64, 64)


def shards(tokens, lengths, gain_one, w_qkv, f_query, f_key, w_out, gain_two, w_up, w_down, d_out):
    rows, width = tokens.shape
    heads, size, _ = f_query.shape
    pairs = heads // 2
    wide = heads * size
    assert size == 64 and lax.axis_size("heads") == 2 and 1536 % rows == 0
    boundary = lengths[0, 0]
    place = bit_of("ctx", 0)
    gain_one_row = gain_one.reshape(1, width)
    gain_two_row = gain_two.reshape(1, width)

    low_rows, low_cols = half_blocks(256)
    ones = (low_rows == low_cols).astype(bf16)
    cross_rows, cross_cols = half_blocks(128)
    cross = (cross_rows != cross_cols).astype(bf16)

    qkv_own = w_qkv.reshape(width, 3 * wide)
    qkv_oth = fetch_other(qkv_own)
    maps = jnp.stack([f_query, f_key])
    maps_oth = swap(maps, "heads", 0)
    out_oth = fetch_other(w_out)
    up_oth = fetch_other(w_up)
    down_oth = fetch_other(w_down)

    h_one = norm_one(tokens, gain_one_row)
    fq, fk, k, v, phi_k, prefix, totals, q, phi_q, numer = ([] for _ in range(10))
    for weights, maps_here in ((qkv_own, maps), (qkv_oth, maps_oth)):
        fq.append(extended(maps_here[0]))
        fk.append(extended(maps_here[1]))
        parts = key_pass(h_one, weights[:, wide:], fk[-1], ones)
        for held, value in zip((k, v, phi_k, prefix, totals), parts):
            held.append(value)
    incoming = scan_runs(jnp.stack(totals), boundary, rows, False)
    for at, weights in enumerate((qkv_own, qkv_oth)):
        parts = query_pass(h_one, weights[:, :wide], phi_k[at], v[at], prefix[at], fq[at], ones)
        for held, value in zip((q, phi_q, numer), parts):
            held.append(value)

    attended, act, grad_pre, h_two, mixed, grad_resid, gn, gd, grad_totals = middle_pass(
        tokens,
        d_out,
        numer,
        phi_q,
        incoming,
        (w_out, out_oth),
        (w_up, up_oth),
        (w_down, down_oth),
        gain_two_row,
        cross,
        256,
        512,
    )
    later = scan_runs(grad_totals, boundary, rows, True)

    def weight_sums(lefts, rights, block):
        send = weight_pass((1 - place).reshape(1), lefts, rights, block)
        keep = weight_pass(place.reshape(1), lefts, rights, block)
        return send, keep

    feed = reduce_rows(*weight_sums([h_two, d_out], [grad_pre, act], 768))
    out_sum = reduce_rows(*weight_sums([grad_resid], [attended], 384))

    grads, raw, qkv_sums = [], [], []
    for at in range(pairs):
        grad, raw_map = back_pass(
            at, q, k, v, phi_q, phi_k, gn, gd, prefix, incoming, later, fq, fk, ones
        )
        grads.append(grad)
        raw.append(raw_map)
        qkv_sums.append(reduce_rows(*weight_sums([h_one], [grad], 384)))
    grad_tokens = tokens_pass(tokens, grad_resid, qkv_own, qkv_oth, gain_one_row, grads, 512)

    raw = jnp.stack(raw)
    maps_sum = [
        jnp.concatenate([map_gradient(raw[:, kind, half]) for kind in range(2)], axis=0).astype(bf16)
        for half in range(2)
    ]
    count = maps_sum[0].shape[0] // 2
    cut = lambda at: [lax.dynamic_slice_in_dim(m, at * count, count, 0) for m in maps_sum]
    maps_sum = reduce_rows(cut(1 - place), cut(place)).astype(f32)

    units = w_up.shape[1]
    grad_up = feed[:, :units].astype(f32)
    grad_down = feed[:, units:].astype(f32).T
    grad_out = out_sum.astype(f32).T
    grad_qkv = jnp.concatenate(
        [s.reshape(width, 3, 128) for s in qkv_sums], axis=2
    ).astype(f32)
    gains = jnp.stack(
        [
            jnp.sum(grad_qkv * w_qkv.astype(f32), axis=(1, 2)),
            jnp.sum(grad_up * w_up.astype(f32), axis=1),
        ]
    )
    gains = (gains + swap(gains, "heads", 0)) / jnp.stack([gain_one, gain_two])
    grad_maps = maps_sum.reshape(2, heads, size, size)
    return (
        mixed,
        grad_tokens,
        gains[0],
        grad_qkv,
        grad_maps[0],
        grad_maps[1],
        grad_out,
        gains[1],
        grad_up,
        grad_down,
    )


def solution(mesh):
    in_specs = (
        P(("batch", "ctx", "heads"), None),
        P("batch", None),
        P(),
        P(None, None, "heads"),
        P("heads", None, None),
        P("heads", None, None),
        P("heads", None),
        P(),
        P(None, "heads"),
        P("heads", None),
        P(("batch", "ctx", "heads"), None),
    )
    out_specs = (
        P(("batch", "ctx", "heads"), None),
        P(("batch", "ctx", "heads"), None),
        P(),
        P(None, None, "heads"),
        P("heads", None, None),
        P("heads", None, None),
        P("heads", None),
        P(),
        P(None, "heads"),
        P("heads", None),
    )
    return jax.shard_map(shards, mesh=mesh, in_specs=in_specs, out_specs=out_specs, check_vma=False)
```

time: 1620 us -> 610 us (0.38)
  matrix products: 523 us -> 0 us
  waiting for transfers between devices: 642 us -> 153 us
  Pallas kernels: 0 us -> 257 us
  local copies, waits for them, and re-layouts: 234 us -> 46.5 us
  blocking collectives: 69.2 us -> 0 us
  starting transfers between devices: 1.01 us -> 63.9 us
  other arithmetic: 122 us -> 76.6 us
    dot_general x34 -> x0, matrix products: 501 us -> none  [the longest x4 45.7 us: contract_cols(): lax.dot_general(left, right, (((1,), (1,)), ((), ())), preferred_element_...]
    pallas_call x0 -> x20, Pallas kernels: none -> 257 us  [the longest x10 69.1 us: weight_pass(): pl.pallas_call(functools.partial(weight_kernel, steps), grid_spec=spec, o...]
    all_gather x4 -> x0, waiting for transfers between devices: 229 us -> none  [the longest x1 62.5 us: shards(): resid_full = lax.all_gather(grad_resid, 'heads', axis=0, tiled=True)]
    psum x1 -> x0, waiting for transfers between devices: 224 us -> none  [shards(): lax.psum((grad_w_qkv, grad_f_query, grad_f_key, grad_w_out, grad_w_up, gr...]
    reduce_scatter x4 -> x0, waiting for transfers between devices: 188 us -> none  [the longest x1 71.1 us: shards(): lax.psum_scatter(jnp.dot(attended, w_out, preferred_element_type=jnp.floa...]
    ppermute x0 -> x76, waiting for transfers between devices: none -> 153 us  [swap(): return lax.ppermute(value, axis, [(i, i ^ 1 << bit) for i in range(count)])]
    ppermute x0 -> x76, starting transfers between devices: none -> 63.9 us  [swap(): return lax.ppermute(value, axis, [(i, i ^ 1 << bit) for i in range(count)])]
    unnamed x193 -> x76, local copies, waits for them, and re-layouts: 67.7 us -> 14 us
  transfers between devices with their start and end apart: 9 -> 76, of which waited for: 9 -> 24; matrix products, arithmetic and copies ran while one was open for 6% -> 18% of each run, Pallas kernels for 0% -> 32%
where the time goes in v1:
time: 610 us; the launch traced here: 600 us
  Pallas kernels  257 us (42%)
  waiting for transfers between devices  153 us (25%)
  other arithmetic  76.6 us (13%)
  starting transfers between devices  63.9 us (10%)
  local copies, waits for them, and re-layouts  46.5 us (8%)
    ppermute x76, waiting for transfers between devices, swap(): return lax.ppermute(value, axis, [(i, i ^ 1 << bit) for i in range(count)])  153 us
    pallas_call x10, Pallas kernels, weight_pass(): pl.pallas_call(functools.partial(weight_kernel, steps), grid_spec=spec, o...  69.1 us
    ppermute x76, starting transfers between devices, swap(): return lax.ppermute(value, axis, [(i, i ^ 1 << bit) for i in range(count)])  63.9 us
    pallas_call x1, Pallas kernels, middle_pass(): pl.pallas_call(functools.partial(middle_kernel, pairs, tile), grid=(rows...  63.3 us
    pallas_call x3, Pallas kernels, back_pass(): pl.pallas_call(functools.partial(back_kernel, pairs, at_pair), grid=(coun...  47.1 us
    select_n x35, other arithmetic, ordered(): jnp.where(bit == 0, jnp.concatenate([mine, theirs], 0), jnp.concatenate([...  38.5 us
    pallas_call x2, Pallas kernels, query_pass(): pl.pallas_call(functools.partial(query_kernel, pairs), grid=(rows // CHUN...  34 us
    pallas_call x2, Pallas kernels, key_pass(): pl.pallas_call(functools.partial(keys_kernel, pairs), grid=(count,), in_s...  26.3 us
  transfers between devices with their start and end apart: 76, of which 24 were waited for; matrix products, arithmetic and copies ran while one was open for 18% of the time, Pallas kernels for 32%

profile of v1, /device:TPU:0, one launch (start us, length us, event | category | flops | bytes accessed | tf_op | source)
XLA Modules:
  0.0 599.8 jit_solution(14413953935969077182)
XLA Ops:
  0.7 2.6 copy.86
  5.5 2.9 collective-permute-start
  22.8 4.5 norm_one.1.h.refs_0_
  30.2 13.1 %key_pass.2 = (bf16[1536,384]{1,0:T(8,128)(2,1)}, bf16[1536,384]{1,0:T(8,128)(2,1)}, bf16[1536,768]{1,0:T(8,128)(2,1)}, bf16[6,6,128,128]{3,2,1,0:T(8,128)(2,1)}, f32[400,128]{1,0:T(8,128)}) custom-call(bf16[1536,768]{1,0:T(8,128)(2,1)} %norm_one.1.h.refs_0_, bf16[768,768]{1,0:T(8,128)(2,1)} %slice.167.w_kv, bf16[3,128,256]{2,1,0:T(8,128)(2,1)} %fusion.20.fext.fk_own, ...), custom_call_target="tpu_custom_call" | custom-call | flops 2717908992 | bytes 14155776 | tf_op jit(solution)/shard_map/key_pass/pallas_call | solution.py:157
  43.4 17.0 %query_pass.2 = (bf16[1536,384]{1,0:T(8,128)(2,1)}, bf16[1536,768]{1,0:T(8,128)(2,1)}, f32[1536,768]{1,0:T(8,128)}) custom-call(bf16[1536,768]{1,0:T(8,128)(2,1)} %norm_one.1.h.refs_0_, bf16[768,384]{1,0:T(8,128)(2,1)} %slice.166.w_q, bf16[1536,768]{1,0:T(8,128)(2,1)} %get-tuple-element.61.k_phi.pk_own, bf16[1536,384]{1,0:T(8,128)(2,1)} %get-tuple-element.62.v.v_own, ...), custom_call_target="tpu_custom_call" | custom-call | flops 2264924160 | bytes 18874368 | tf_op jit(solution)/shard_map/query_pass/pallas_call | solution.py:214
  63.5 26.0 %collective-permute-done.6 = bf16[192,768]{1,0:T(8,128)(2,1)} collective-permute-done((bf16[192,768]{1,0:T(8,128)(2,1)S(1)}, bf16[192,768]{1,0:T(8,128)(2,1)}, u32[]{:S(2)}, u32[]{:S(2)}) %collective-permute-start.6) | collective-permute-done | bytes 294944 | tf_op jit(solution)/shard_map/ppermute | solution.py:639
  93.2 13.2 %key_pass.3 = (bf16[1536,384]{1,0:T(8,128)(2,1)}, bf16[1536,384]{1,0:T(8,128)(2,1)}, bf16[1536,768]{1,0:T(8,128)(2,1)}, bf16[6,6,128,128]{3,2,1,0:T(8,128)(2,1)}, f32[400,128]{1,0:T(8,128)}) custom-call(bf16[1536,768]{1,0:T(8,128)(2,1)} %norm_one.1.h.refs_0_, bf16[768,768]{1,0:T(8,128)(2,1)} %slice.173.w_kv, bf16[3,128,256]{2,1,0:T(8,128)(2,1)} %fusion.22.fext.fk_oth, ...), custom_call_target="tpu_custom_call" | custom-call | flops 2717908992 | bytes 14155776 | tf_op jit(solution)/shard_map/key_pass/pallas_call | solution.py:157
  115.2 17.0 %query_pass.3 = (bf16[1536,384]{1,0:T(8,128)(2,1)}, bf16[1536,768]{1,0:T(8,128)(2,1)}, f32[1536,768]{1,0:T(8,128)}) custom-call(bf16[1536,768]{1,0:T(8,128)(2,1)} %norm_one.1.h.refs_0_, bf16[768,384]{1,0:T(8,128)(2,1)} %slice.172.w_q, bf16[1536,768]{1,0:T(8,128)(2,1)} %get-tuple-element.65.k_phi.pk_oth, bf16[1536,384]{1,0:T(8,128)(2,1)} %get-tuple-element.66.v.v_oth, ...), custom_call_target="tpu_custom_call" | custom-call | flops 2264924160 | bytes 18874368 | tf_op jit(solution)/shard_map/query_pass/pallas_call | solution.py:214
  134.2 3.0 maximum_select_fusion.1.up_oth
  137.2 3.9 maximum_select_fusion.2.down_oth
  142.0 63.3 %middle_pass.1 = (bf16[1536,768]{1,0:T(8,128)(2,1)}, bf16[1536,3072]{1,0:T(8,128)(2,1)}, bf16[1536,3072]{1,0:T(8,128)(2,1)}, bf16[1536,768]{1,0:T(8,128)(2,1)}, ...) custom-call(bf16[1536,768]{1,0:T(8,128)(2,1)} %tokens.5, ...), custom_call_target="tpu_custom_call" | custom-call | flops 36238786560 | bytes 70778880 | tf_op jit(solution)/shard_map/middle_pass/pallas_call | solution.py:379
  205.3 4.5 weight_pass.19
  211.9 16.9 %weight_pass.17 = (bf16[384,3072]{1,0:T(8,128)(2,1)}, bf16[384,3072]{1,0:T(8,128)(2,1)}) custom-call(s32[1]{0:T(128)} %bitcast.19.half, bf16[1536,768]{1,0:T(8,128)(2,1)} %get-tuple-element.97.refs_0_, bf16[1536,768]{1,0:T(8,128)(2,1)} %refs_1_.3, bf16[1536,3072]{1,0:T(8,128)(2,1)} %get-tuple-element.98.refs_2_, bf16[1536,3072]{1,0:T(8,128)(2,1)} %get-tuple-element.99.refs_3_), custom_call_target="tpu_custom_call" | custom-call | flops 7247757312 | bytes 21233664 | tf_op jit(solution)/shard_map/weight_pass/pallas_call | solution.py:463
  228.7 16.4 %weight_pass.16 = (bf16[384,3072]{1,0:T(8,128)(2,1)}, bf16[384,3072]{1,0:T(8,128)(2,1)}) custom-call(s32[1]{0:T(128)} %bitcast.18.half, bf16[1536,768]{1,0:T(8,128)(2,1)} %get-tuple-element.97.refs_0_, bf16[1536,768]{1,0:T(8,128)(2,1)} %refs_1_.3, bf16[1536,3072]{1,0:T(8,128)(2,1)} %get-tuple-element.98.refs_2_, bf16[1536,3072]{1,0:T(8,128)(2,1)} %get-tuple-element.99.refs_3_), custom_call_target="tpu_custom_call" | custom-call | flops 7247757312 | bytes 21233664 | tf_op jit(solution)/shard_map/weight_pass/pallas_call | solution.py:463
  245.6 4.4 weight_pass.18
  254.1 6.7 %collective-permute-done.68 = bf16[384,384]{1,0:T(8,128)(2,1)S(1)} collective-permute-done((bf16[384,384]{1,0:T(8,128)(2,1)S(1)}, bf16[384,384]{1,0:T(8,128)(2,1)S(1)}, u32[]{:S(2)}, u32[]{:S(2)}) %collective-permute-start.68) | collective-permute-done | bytes 294944 | tf_op jit(solution)/shard_map/ppermute | solution.py:639
  262.3 15.6 %back_pass.5 = (bf16[1536,768]{1,0:T(8,128)(2,1)}, f32[2,2,128,256]{3,2,1,0:T(8,128)}) custom-call(bf16[1536,384]{1,0:T(8,128)(2,1)} %get-tuple-element.75.q_own, bf16[1536,384]{1,0:T(8,128)(2,1)} %get-tuple-element.76.q_oth, bf16[1536,384]{1,0:T(8,128)(2,1)} %get-tuple-element.77.k_own, bf16[1536,384]{1,0:T(8,128)(2,1)} %get-tuple-element.78.k_oth, ...), custom_call_target="tpu_custom_call" | custom-call | flops 4089446400 | bytes 9216000 | tf_op jit(solution)/shard_map/back_pass/pallas_call | solution.py:573
  277.9 15.8 %back_pass.4 = (bf16[1536,768]{1,0:T(8,128)(2,1)}, f32[2,2,128,256]{3,2,1,0:T(8,128)}) custom-call(bf16[1536,384]{1,0:T(8,128)(2,1)} %get-tuple-element.75.q_own, bf16[1536,384]{1,0:T(8,128)(2,1)} %get-tuple-element.76.q_oth, bf16[1536,384]{1,0:T(8,128)(2,1)} %get-tuple-element.77.k_own, bf16[1536,384]{1,0:T(8,128)(2,1)} %get-tuple-element.78.k_oth, ...), custom_call_target="tpu_custom_call" | custom-call | flops 4089446400 | bytes 9216000 | tf_op jit(solution)/shard_map/back_pass/pallas_call | solution.py:573
  293.8 15.7 %back_pass.3 = (bf16[1536,768]{1,0:T(8,128)(2,1)}, f32[2,2,128,256]{3,2,1,0:T(8,128)}) custom-call(bf16[1536,384]{1,0:T(8,128)(2,1)} %get-tuple-element.75.q_own, bf16[1536,384]{1,0:T(8,128)(2,1)} %get-tuple-element.76.q_oth, bf16[1536,384]{1,0:T(8,128)(2,1)} %get-tuple-element.77.k_own, bf16[1536,384]{1,0:T(8,128)(2,1)} %get-tuple-element.78.k_oth, ...), custom_call_target="tpu_custom_call" | custom-call | flops 4089446400 | bytes 9216000 | tf_op jit(solution)/shard_map/back_pass/pallas_call | solution.py:573
  313.2 4.4 weight_pass.11
  317.6 4.4 weight_pass.10
  322.0 12.8 %tokens_pass.1 = bf16[1536,768]{1,0:T(8,128)(2,1)} custom-call(bf16[1536,768]{1,0:T(8,128)(2,1)} %tokens.5, bf16[1536,768]{1,0:T(8,128)(2,1)} %get-tuple-element.74.resid.refs_0_, bf16[768,1152]{1,0:T(8,128)(2,1)} %copy-done, bf16[768,1152]{1,0:T(8,128)(2,1)} %copy-done.2, f32[1,768]{1,0:T(1,128)} %reshape.131.gain, ...), custom_call_target="tpu_custom_call" | custom-call | flops 5435817984 | bytes 18874368 | tf_op jit(solution)/shard_map/tokens_pass/pallas_call | solution.py:623
  334.9 4.5 weight_pass.13
  340.0 3.5 collective-permute-done.58
  345.2 4.8 weight_pass.12
  351.8 4.4 weight_pass.15
  356.3 2.7 collective-permute-start.61
  359.0 4.0 add_convert_fusion
  364.0 4.4 weight_pass.14
  369.7 3.1 collective-permute-done.63
  373.5 3.6 collective-permute-done.70
  377.7 3.4 collective-permute-done.64
  395.8 18.7 %collective-permute-done.47 = bf16[384,3072]{1,0:T(8,128)(2,1)} collective-permute-done((bf16[384,3072]{1,0:T(8,128)(2,1)}, bf16[384,3072]{1,0:T(8,128)(2,1)}, u32[]{:S(2)}, u32[]{:S(2)}) %collective-permute-start.47) | collective-permute-done | bytes 2359328 | tf_op jit(solution)/shard_map/ppermute | solution.py:639
  423.4 22.2 %collective-permute-done.48 = bf16[192,3072]{1,0:T(8,128)(2,1)S(1)} collective-permute-done((bf16[192,3072]{1,0:T(8,128)(2,1)S(1)}, bf16[192,3072]{1,0:T(8,128)(2,1)S(1)}, u32[]{:S(2)}, u32[]{:S(2)}) %collective-permute-start.48) | collective-permute-done | bytes 1179680 | tf_op jit(solution)/shard_map/ppermute | solution.py:639
  447.2 3.7 collective-permute-done.74
  453.5 7.7 %collective-permute-done.49 = bf16[96,3072]{1,0:T(8,128)(2,1)S(1)} collective-permute-done((bf16[96,3072]{1,0:T(8,128)(2,1)S(1)}, bf16[96,3072]{1,0:T(8,128)(2,1)S(1)}, u32[]{:S(2)}, u32[]{:S(2)}) %collective-permute-start.49) | collective-permute-done | bytes 589856 | tf_op jit(solution)/shard_map/ppermute | solution.py:639
  465.5 10.3 %collective-permute-done.50 = bf16[48,3072]{1,0:T(8,128)(2,1)S(1)} collective-permute-done((bf16[48,3072]{1,0:T(8,128)(2,1)S(1)}, bf16[48,3072]{1,0:T(8,128)(2,1)S(1)}, u32[]{:S(2)}, u32[]{:S(2)}) %collective-permute-start.50) | collective-permute-done | bytes 294944 | tf_op jit(solution)/shard_map/ppermute | solution.py:639
  480.7 9.1 %collective-permute-done.51 = bf16[48,3072]{1,0:T(8,128)(2,1)S(1)} collective-permute-done((bf16[48,3072]{1,0:T(8,128)(2,1)S(1)}, bf16[48,3072]{1,0:T(8,128)(2,1)S(1)}, u32[]{:S(2)}, u32[]{:S(2)}) %collective-permute-start.51) | collective-permute-done | bytes 294944 | tf_op jit(solution)/shard_map/ppermute | solution.py:639
  490.2 3.4 collective-permute-start.30
  493.8 2.9 collective-permute-start.21
  496.7 7.9 %collective-permute-done.30 = bf16[48,384]{1,0:T(8,128)(2,1)S(1)} collective-permute-done((bf16[48,384]{1,0:T(8,128)(2,1)S(1)}, bf16[48,384]{1,0:T(8,128)(2,1)S(1)}, u32[]{:S(2)}, u32[]{:S(2)}) %collective-permute-start.30) | collective-permute-done | bytes 36896 | tf_op jit(solution)/shard_map/ppermute | solution.py:639
  504.6 2.9 collective-permute-done.52
  524.6 12.3 %collective-permute-done.53 = bf16[192,3072]{1,0:T(8,128)(2,1)} collective-permute-done((bf16[192,3072]{1,0:T(8,128)(2,1)S(1)}, bf16[192,3072]{1,0:T(8,128)(2,1)}, u32[]{:S(2)}, u32[]{:S(2)}) %collective-permute-start.53) | collective-permute-done | bytes 1179680 | tf_op jit(solution)/shard_map/ppermute | solution.py:639
  575.3 6.5 %multiply_reduce_fusion.1 = f32[768]{0:T(1024)S(1)} fusion(bf16[768,3,384]{2,0,1:T(8,128)(2,1)S(1)} %copy-done.1, bf16[768,3,128]{2,1,0:T(4,128)(2,1)S(1)} %maximum_select_fusion.8, bf16[768,3,128]{2,1,0:T(4,128)(2,1)S(1)} %maximum_select_fusion.7, bf16[768,3,128]{2,1,0:T(4,128)(2,1)S(1)} %maximum_select_fusion.6), kind=kLoop, calls=%fused_computation.5 | loop fusion | flops 7961856 | bytes 3542016 | tf_op jit(solution)/shard_map/reduce_sum | solution.py:827
  581.8 4.8 maximum_select_fusion
  586.6 2.8 multiply_reduce_fusion
  590.0 2.8 convert_bitcast_fusion
  592.8 6.1 %copy.117 = f32[1536,768]{1,0:T(8,128)} copy(f32[1536,768]{0,1:T(8,128)} %convert_bitcast_fusion) | data formatting | bytes 9437184
  (366 shorter events, 150.6 us)
Async XLA Ops:
  5.5 56.0 %collective-permute-start = (bf16[384,1152]{1,0:T(8,128)(2,1)}, bf16[384,1152]{1,0:T(8,128)(2,1)}, u32[]{:S(2)}, u32[]{:S(2)}) collective-permute-start(bf16[384,1152]{1,0:T(8,128)(2,1)} %constant_dynamic-slice_fusion.13), channel_id=1, source_target_pairs={{0,1},{1,0},{2,3},{3,2},{4,5},{5,4},{6,7},{7,6},{8,9},{9,8},{10,11... | collective-permute-start | bytes 2654216 | tf_op jit(solution)/shard_map/ppermute | solution.py:639
  10.1 51.5 %collective-permute-start.2 = (bf16[2,6,64,64]{3,2,1,0:T(8,128)(2,1)}, bf16[2,6,64,64]{3,2,1,0:T(8,128)(2,1)}, u32[]{:S(2)}, u32[]{:S(2)}) collective-permute-start(bf16[2,6,64,64]{3,2,1,0:T(8,128)(2,1)} %pad_maximum_fusion.2), channel_id=1, source_target_pairs={{0,1},{1,0},{2,3},{3,2},{4,5},{5,4},{6,7},{7,6},{8,9},{9,8},{10,11... | collective-permute-start | bytes 294920 | tf_op jit(solution)/shard_map/ppermute | solution.py:639
  12.5 77.0 %collective-permute-start.8 = (bf16[384,1536]{1,0:T(8,128)(2,1)}, bf16[384,1536]{1,0:T(8,128)(2,1)S(1)}, u32[]{:S(2)}, u32[]{:S(2)}) collective-permute-start(bf16[384,1536]{1,0:T(8,128)(2,1)} %constant_dynamic-slice_fusion.11), channel_id=1, source_target_pairs={{0,1},{1,0},{2,3},{3,2},{4,5},{5,4},{6,7},{7,6},{8,9},{9,8},{10,11... | collective-permute-start | bytes 3538952 | tf_op jit(solution)/shard_map/ppermute | solution.py:639
  16.9 73.1 %collective-permute-start.10 = (bf16[768,768]{1,0:T(8,128)(2,1)}, bf16[768,768]{1,0:T(8,128)(2,1)}, u32[]{:S(2)}, u32[]{:S(2)}) collective-permute-start(bf16[768,768]{1,0:T(8,128)(2,1)} %constant_dynamic-slice_fusion.10), channel_id=1, source_target_pairs={{0,1},{1,0},{2,3},{3,2},{4,5},{5,4},{6,7},{7,6},{8,9},{9,8},{10,11... | collective-permute-start | bytes 3538952 | tf_op jit(solution)/shard_map/ppermute | solution.py:639
  17.9 71.6 %collective-permute-start.6 = (bf16[192,768]{1,0:T(8,128)(2,1)S(1)}, bf16[192,768]{1,0:T(8,128)(2,1)}, u32[]{:S(2)}, u32[]{:S(2)}) collective-permute-start(bf16[192,768]{1,0:T(8,128)(2,1)S(1)} %constant_dynamic-slice_fusion.12), channel_id=1, source_target_pairs={{0,1},{1,0},{2,3},{3,2},{4,5},{5,4},{6,7},{7,6},{8,9},{9,8},{10,11... | collective-permute-start | bytes 884744 | tf_op jit(solution)/shard_map/ppermute | solution.py:639
  61.4 28.6 %collective-permute-start.1 = (bf16[384,1152]{1,0:T(8,128)(2,1)}, bf16[384,1152]{1,0:T(8,128)(2,1)S(1)}, u32[]{:S(2)}, u32[]{:S(2)}) collective-permute-start(bf16[384,1152]{1,0:T(8,128)(2,1)} %collective-permute-done), channel_id=1, source_target_pairs={{0,2},{2,0},{4,6},{6,4},{1,3},{3,1},{5,7},{7,5},{8,10},{10,8},{12,... | collective-permute-start | bytes 2654216 | tf_op jit(solution)/shard_map/ppermute | solution.py:639
  89.5 20.5 %collective-permute-start.7 = (bf16[192,768]{1,0:T(8,128)(2,1)}, bf16[192,768]{1,0:T(8,128)(2,1)S(1)}, u32[]{:S(2)}, u32[]{:S(2)}) collective-permute-start(bf16[192,768]{1,0:T(8,128)(2,1)} %collective-permute-done.6), channel_id=1, source_target_pairs={{0,2},{2,0},{4,6},{6,4},{1,3},{3,1},{5,7},{7,5},{8,10},{10,8},{12,... | collective-permute-start | bytes 884744 | tf_op jit(solution)/shard_map/ppermute | solution.py:639
  89.5 44.7 %collective-permute-start.9 = (bf16[384,1536]{1,0:T(8,128)(2,1)S(1)}, bf16[384,1536]{1,0:T(8,128)(2,1)}, u32[]{:S(2)}, u32[]{:S(2)}) collective-permute-start(bf16[384,1536]{1,0:T(8,128)(2,1)S(1)} %collective-permute-done.8), channel_id=1, source_target_pairs={{0,2},{2,0},{4,6},{6,4},{1,3},{3,1},{5,7},{7,5},{8,10},{10,8},{12,... | collective-permute-start | bytes 3538952 | tf_op jit(solution)/shard_map/ppermute | solution.py:639
  90.0 47.2 %collective-permute-start.11 = (bf16[768,768]{1,0:T(8,128)(2,1)}, bf16[768,768]{1,0:T(8,128)(2,1)}, u32[]{:S(2)}, u32[]{:S(2)}) collective-permute-start(bf16[768,768]{1,0:T(8,128)(2,1)} %collective-permute-done.10), channel_id=1, source_target_pairs={{0,2},{2,0},{4,6},{6,4},{1,3},{3,1},{5,7},{7,5},{8,10},{10,8},{12,... | collective-permute-start | bytes 3538952 | tf_op jit(solution)/shard_map/ppermute | solution.py:639
  115.1 17.1 %collective-permute-start.4 = (bf16[2,400,128]{2,1,0:T(8,128)(2,1)S(1)}, bf16[2,400,128]{2,1,0:T(8,128)(2,1)S(1)}, u32[]{:S(2)}, u32[]{:S(2)}) collective-permute-start(bf16[2,400,128]{2,1,0:T(8,128)(2,1)S(1)} %fusion.49), channel_id=1, source_target_pairs={{0,2},{2,0},{4,6},{6,4},{1,3},{3,1},{5,7},{7,5},{8,10},{10,8},{12,... | collective-permute-start | bytes 614408 | tf_op jit(solution)/shard_map/ppermute | solution.py:639
  209.8 44.3 %collective-permute-start.66 = (bf16[384,384]{1,0:T(8,128)(2,1)}, bf16[384,384]{1,0:T(8,128)(2,1)S(1)}, u32[]{:S(2)}, u32[]{:S(2)}) collective-permute-start(bf16[384,384]{1,0:T(8,128)(2,1)} %get-tuple-element.109), channel_id=1, source_target_pairs={{0,2},{2,0},{4,6},{6,4},{1,3},{3,1},{5,7},{7,5},{8,10},{10,8},{12,... | collective-permute-start | bytes 884744 | tf_op jit(solution)/shard_map/ppermute | solution.py:639
  210.0 40.4 %collective-permute-start.67 = (bf16[384,384]{1,0:T(8,128)(2,1)}, bf16[384,384]{1,0:T(8,128)(2,1)S(1)}, u32[]{:S(2)}, u32[]{:S(2)}) collective-permute-start(bf16[384,384]{1,0:T(8,128)(2,1)} %get-tuple-element.111), channel_id=1, source_target_pairs={{0,2},{2,0},{4,6},{6,4},{1,3},{3,1},{5,7},{7,5},{8,10},{10,8},{12,... | collective-permute-start | bytes 884744 | tf_op jit(solution)/shard_map/ppermute | solution.py:639
  210.3 39.7 %collective-permute-start.12 = (bf16[2,400,128]{2,1,0:T(8,128)(2,1)S(1)}, bf16[2,400,128]{2,1,0:T(8,128)(2,1)S(1)}, u32[]{:S(2)}, u32[]{:S(2)}) collective-permute-start(bf16[2,400,128]{2,1,0:T(8,128)(2,1)S(1)} %convert_element_type.581), channel_id=1, source_target_pairs={{0,1},{1,0},{2,3},{3,2},{4,5},{5,4},{6,7},{7,6},{8,9},{9,8},{10,11... | collective-permute-start | bytes 614408 | tf_op jit(solution)/shard_map/ppermute | solution.py:639
  245.1 147.5 %collective-permute-start.45 = (bf16[384,3072]{1,0:T(8,128)(2,1)}, bf16[384,3072]{1,0:T(8,128)(2,1)}, u32[]{:S(2)}, u32[]{:S(2)}) collective-permute-start(bf16[384,3072]{1,0:T(8,128)(2,1)} %get-tuple-element.101), channel_id=1, source_target_pairs={{0,2},{2,0},{4,6},{6,4},{1,3},{3,1},{5,7},{7,5},{8,10},{10,8},{12,... | collective-permute-start | bytes 7077896 | tf_op jit(solution)/shard_map/ppermute | solution.py:639
  245.1 113.9 %collective-permute-start.46 = (bf16[384,3072]{1,0:T(8,128)(2,1)}, bf16[384,3072]{1,0:T(8,128)(2,1)}, u32[]{:S(2)}, u32[]{:S(2)}) collective-permute-start(bf16[384,3072]{1,0:T(8,128)(2,1)} %get-tuple-element.103), channel_id=1, source_target_pairs={{0,2},{2,0},{4,6},{6,4},{1,3},{3,1},{5,7},{7,5},{8,10},{10,8},{12,... | collective-permute-start | bytes 7077896 | tf_op jit(solution)/shard_map/ppermute | solution.py:639
  260.9 108.1 %collective-permute-start.69 = (bf16[192,384]{1,0:T(8,128)(2,1)S(1)}, bf16[192,384]{1,0:T(8,128)(2,1)S(1)}, u32[]{:S(2)}, u32[]{:S(2)}) collective-permute-start(bf16[192,384]{1,0:T(8,128)(2,1)S(1)} %get-tuple-element.155), channel_id=1, source_target_pairs={{0,4},{2,6},{4,0},{6,2},{1,5},{3,7},{5,1},{7,3},{8,12},{10,14},{12... | collective-permute-start | bytes 442376 | tf_op jit(solution)/shard_map/ppermute | solution.py:639
  311.7 28.3 %collective-permute-start.56 = (bf16[384,64]{0,1:T(8,128)(2,1)S(1)}, bf16[384,64]{0,1:T(8,128)(2,1)S(1)}, u32[]{:S(2)}, u32[]{:S(2)}) collective-permute-start(bf16[384,64]{0,1:T(8,128)(2,1)S(1)} %constant_dynamic-slice_fusion.4), channel_id=1, source_target_pairs={{0,2},{2,0},{4,6},{6,4},{1,3},{3,1},{5,7},{7,5},{8,10},{10,8},{12,... | collective-permute-start | bytes 147464 | tf_op jit(solution)/shard_map/ppermute | solution.py:639
  312.6 26.7 %collective-permute-start.57 = (bf16[384,64]{0,1:T(8,128)(2,1)S(1)}, bf16[384,64]{0,1:T(8,128)(2,1)S(1)}, u32[]{:S(2)}, u32[]{:S(2)}) collective-permute-start(bf16[384,64]{0,1:T(8,128)(2,1)S(1)} %constant_dynamic-slice_fusion), channel_id=1, source_target_pairs={{0,2},{2,0},{4,6},{6,4},{1,3},{3,1},{5,7},{7,5},{8,10},{10,8},{12,... | collective-permute-start | bytes 147464 | tf_op jit(solution)/shard_map/ppermute | solution.py:639
  362.9 51.5 %collective-permute-start.47 = (bf16[384,3072]{1,0:T(8,128)(2,1)}, bf16[384,3072]{1,0:T(8,128)(2,1)}, u32[]{:S(2)}, u32[]{:S(2)}) collective-permute-start(bf16[384,3072]{1,0:T(8,128)(2,1)} %add_convert_fusion), channel_id=1, source_target_pairs={{0,1},{1,0},{2,3},{3,2},{4,5},{5,4},{6,7},{7,6},{8,9},{9,8},{10,11... | collective-permute-start | bytes 7077896 | tf_op jit(solution)/shard_map/ppermute | solution.py:639
  368.4 48.8 %collective-permute-start.15 = (bf16[384,384]{1,0:T(8,128)(2,1)}, bf16[384,384]{1,0:T(8,128)(2,1)S(1)}, u32[]{:S(2)}, u32[]{:S(2)}) collective-permute-start(bf16[384,384]{1,0:T(8,128)(2,1)} %get-tuple-element.86), channel_id=1, source_target_pairs={{0,2},{2,0},{4,6},{6,4},{1,3},{3,1},{5,7},{7,5},{8,10},{10,8},{12,... | collective-permute-start | bytes 884744 | tf_op jit(solution)/shard_map/ppermute | solution.py:639
  368.4 49.4 %collective-permute-start.16 = (bf16[384,384]{1,0:T(8,128)(2,1)}, bf16[384,384]{1,0:T(8,128)(2,1)S(1)}, u32[]{:S(2)}, u32[]{:S(2)}) collective-permute-start(bf16[384,384]{1,0:T(8,128)(2,1)} %get-tuple-element.88), channel_id=1, source_target_pairs={{0,2},{2,0},{4,6},{6,4},{1,3},{3,1},{5,7},{7,5},{8,10},{10,8},{12,... | collective-permute-start | bytes 884744 | tf_op jit(solution)/shard_map/ppermute | solution.py:639
  392.6 25.6 %collective-permute-start.25 = (bf16[384,384]{1,0:T(8,128)(2,1)}, bf16[384,384]{1,0:T(8,128)(2,1)S(1)}, u32[]{:S(2)}, u32[]{:S(2)}) collective-permute-start(bf16[384,384]{1,0:T(8,128)(2,1)} %get-tuple-element.90), channel_id=1, source_target_pairs={{0,2},{2,0},{4,6},{6,4},{1,3},{3,1},{5,7},{7,5},{8,10},{10,8},{12,... | collective-permute-start | bytes 884744 | tf_op jit(solution)/shard_map/ppermute | solution.py:639
  392.6 26.3 %collective-permute-start.26 = (bf16[384,384]{1,0:T(8,128)(2,1)}, bf16[384,384]{1,0:T(8,128)(2,1)S(1)}, u32[]{:S(2)}, u32[]{:S(2)}) collective-permute-start(bf16[384,384]{1,0:T(8,128)(2,1)} %get-tuple-element.92), channel_id=1, source_target_pairs={{0,2},{2,0},{4,6},{6,4},{1,3},{3,1},{5,7},{7,5},{8,10},{10,8},{12,... | collective-permute-start | bytes 884744 | tf_op jit(solution)/shard_map/ppermute | solution.py:639
  414.5 32.0 %collective-permute-start.35 = (bf16[384,384]{1,0:T(8,128)(2,1)S(1)}, bf16[384,384]{1,0:T(8,128)(2,1)S(1)}, u32[]{:S(2)}, u32[]{:S(2)}) collective-permute-start(bf16[384,384]{1,0:T(8,128)(2,1)S(1)} %copy-done.31), channel_id=1, source_target_pairs={{0,2},{2,0},{4,6},{6,4},{1,3},{3,1},{5,7},{7,5},{8,10},{10,8},{12,... | collective-permute-start | bytes 884744 | tf_op jit(solution)/shard_map/ppermute | solution.py:639
  417.2 28.4 %collective-permute-start.48 = (bf16[192,3072]{1,0:T(8,128)(2,1)S(1)}, bf16[192,3072]{1,0:T(8,128)(2,1)S(1)}, u32[]{:S(2)}, u32[]{:S(2)}) collective-permute-start(bf16[192,3072]{1,0:T(8,128)(2,1)S(1)} %get-tuple-element.147), channel_id=1, source_target_pairs={{0,4},{2,6},{4,0},{6,2},{1,5},{3,7},{5,1},{7,3},{8,12},{10,14},{12... | collective-permute-start | bytes 3538952 | tf_op jit(solution)/shard_map/ppermute | solution.py:639
  418.9 32.2 %collective-permute-start.17 = (bf16[384,384]{1,0:T(8,128)(2,1)S(1)}, bf16[384,384]{1,0:T(8,128)(2,1)S(1)}, u32[]{:S(2)}, u32[]{:S(2)}) collective-permute-start(bf16[384,384]{1,0:T(8,128)(2,1)S(1)} %add_convert_fusion.15), channel_id=1, source_target_pairs={{0,1},{1,0},{2,3},{3,2},{4,5},{5,4},{6,7},{7,6},{8,9},{9,8},{10,11... | collective-permute-start | bytes 884744 | tf_op jit(solution)/shard_map/ppermute | solution.py:639
  419.6 32.2 %collective-permute-start.27 = (bf16[384,384]{1,0:T(8,128)(2,1)S(1)}, bf16[384,384]{1,0:T(8,128)(2,1)S(1)}, u32[]{:S(2)}, u32[]{:S(2)}) collective-permute-start(bf16[384,384]{1,0:T(8,128)(2,1)S(1)} %add_convert_fusion.13), channel_id=1, source_target_pairs={{0,1},{1,0},{2,3},{3,2},{4,5},{5,4},{6,7},{7,6},{8,9},{9,8},{10,11... | collective-permute-start | bytes 884744 | tf_op jit(solution)/shard_map/ppermute | solution.py:639
  422.8 38.8 %collective-permute-start.37 = (bf16[384,384]{1,0:T(8,128)(2,1)S(1)}, bf16[384,384]{1,0:T(8,128)(2,1)S(1)}, u32[]{:S(2)}, u32[]{:S(2)}) collective-permute-start(bf16[384,384]{1,0:T(8,128)(2,1)S(1)} %add_convert_fusion.11), channel_id=1, source_target_pairs={{0,1},{1,0},{2,3},{3,2},{4,5},{5,4},{6,7},{7,6},{8,9},{9,8},{10,11... | collective-permute-start | bytes 884744 | tf_op jit(solution)/shard_map/ppermute | solution.py:639
  446.5 14.7 %collective-permute-start.49 = (bf16[96,3072]{1,0:T(8,128)(2,1)S(1)}, bf16[96,3072]{1,0:T(8,128)(2,1)S(1)}, u32[]{:S(2)}, u32[]{:S(2)}) collective-permute-start(bf16[96,3072]{1,0:T(8,128)(2,1)S(1)} %get-tuple-element.149), channel_id=1, source_target_pairs={{0,8},{8,0},{16,24},{24,16},{1,9},{9,1},{17,25},{25,17},{2,10},{10... | collective-permute-start | bytes 1769480 | tf_op jit(solution)/shard_map/ppermute | solution.py:639
  451.0 26.0 %collective-permute-start.75 = (bf16[384,384]{1,0:T(8,128)(2,1)S(1)}, bf16[384,384]{1,0:T(8,128)(2,1)S(1)}, u32[]{:S(2)}, u32[]{:S(2)}) collective-permute-start(bf16[384,384]{1,0:T(8,128)(2,1)S(1)} %maximum_select_fusion.18), channel_id=1, source_target_pairs={{0,2},{2,0},{4,6},{6,4},{1,3},{3,1},{5,7},{7,5},{8,10},{10,8},{12,... | collective-permute-start | bytes 884744 | tf_op jit(solution)/shard_map/ppermute | solution.py:639
  461.2 14.6 %collective-permute-start.50 = (bf16[48,3072]{1,0:T(8,128)(2,1)S(1)}, bf16[48,3072]{1,0:T(8,128)(2,1)S(1)}, u32[]{:S(2)}, u32[]{:S(2)}) collective-permute-start(bf16[48,3072]{1,0:T(8,128)(2,1)S(1)} %add_convert_fusion.9), channel_id=1, source_target_pairs={{0,16},{8,24},{16,0},{24,8},{1,17},{9,25},{17,1},{25,9},{2,18},{10... | collective-permute-start | bytes 884744 | tf_op jit(solution)/shard_map/ppermute | solution.py:639
  461.7 14.3 %collective-permute-start.38 = (bf16[192,384]{1,0:T(8,128)(2,1)S(1)}, bf16[192,384]{1,0:T(8,128)(2,1)S(1)}, u32[]{:S(2)}, u32[]{:S(2)}) collective-permute-start(bf16[192,384]{1,0:T(8,128)(2,1)S(1)} %get-tuple-element.161), channel_id=1, source_target_pairs={{0,4},{2,6},{4,0},{6,2},{1,5},{3,7},{5,1},{7,3},{8,12},{10,14},{12... | collective-permute-start | bytes 442376 | tf_op jit(solution)/shard_map/ppermute | solution.py:639
  463.3 15.2 %collective-permute-start.19 = (bf16[96,384]{1,0:T(8,128)(2,1)S(1)}, bf16[96,384]{1,0:T(8,128)(2,1)S(1)}, u32[]{:S(2)}, u32[]{:S(2)}) collective-permute-start(bf16[96,384]{1,0:T(8,128)(2,1)S(1)} %get-tuple-element.173), channel_id=1, source_target_pairs={{0,8},{8,0},{16,24},{24,16},{1,9},{9,1},{17,25},{25,17},{2,10},{10... | collective-permute-start | bytes 221192 | tf_op jit(solution)/shard_map/ppermute | solution.py:639
  464.0 26.1 %collective-permute-start.29 = (bf16[96,384]{1,0:T(8,128)(2,1)S(1)}, bf16[96,384]{1,0:T(8,128)(2,1)S(1)}, u32[]{:S(2)}, u32[]{:S(2)}) collective-permute-start(bf16[96,384]{1,0:T(8,128)(2,1)S(1)} %get-tuple-element.175), channel_id=1, source_target_pairs={{0,8},{8,0},{16,24},{24,16},{1,9},{9,1},{17,25},{25,17},{2,10},{10... | collective-permute-start | bytes 221192 | tf_op jit(solution)/shard_map/ppermute | solution.py:639
  476.0 13.8 %collective-permute-start.51 = (bf16[48,3072]{1,0:T(8,128)(2,1)S(1)}, bf16[48,3072]{1,0:T(8,128)(2,1)S(1)}, u32[]{:S(2)}, u32[]{:S(2)}) collective-permute-start(bf16[48,3072]{1,0:T(8,128)(2,1)S(1)} %add_convert_fusion.8), channel_id=1, source_target_pairs={{0,16},{8,24},{16,0},{24,8},{1,17},{9,25},{17,1},{25,9},{2,18},{10... | collective-permute-start | bytes 884744 | tf_op jit(solution)/shard_map/ppermute | solution.py:639
  476.1 17.5 %collective-permute-start.39 = (bf16[96,384]{1,0:T(8,128)(2,1)S(1)}, bf16[96,384]{1,0:T(8,128)(2,1)S(1)}, u32[]{:S(2)}, u32[]{:S(2)}) collective-permute-start(bf16[96,384]{1,0:T(8,128)(2,1)S(1)} %get-tuple-element.177), channel_id=1, source_target_pairs={{0,8},{8,0},{16,24},{24,16},{1,9},{9,1},{17,25},{25,17},{2,10},{10... | collective-permute-start | bytes 221192 | tf_op jit(solution)/shard_map/ppermute | solution.py:639
  478.6 15.1 %collective-permute-start.20 = (bf16[48,384]{1,0:T(8,128)(2,1)S(1)}, bf16[48,384]{1,0:T(8,128)(2,1)S(1)}, u32[]{:S(2)}, u32[]{:S(2)}) collective-permute-start(bf16[48,384]{1,0:T(8,128)(2,1)S(1)} %add_convert_fusion.45), channel_id=1, source_target_pairs={{0,16},{8,24},{16,0},{24,8},{1,17},{9,25},{17,1},{25,9},{2,18},{10... | collective-permute-start | bytes 110600 | tf_op jit(solution)/shard_map/ppermute | solution.py:639
  489.9 17.6 %collective-permute-start.52 = (bf16[96,3072]{1,0:T(8,128)(2,1)S(1)}, bf16[96,3072]{1,0:T(8,128)(2,1)S(1)}, u32[]{:S(2)}, u32[]{:S(2)}) collective-permute-start(bf16[96,3072]{1,0:T(8,128)(2,1)S(1)} %maximum_select_fusion.10), channel_id=1, source_target_pairs={{0,8},{8,0},{16,24},{24,16},{1,9},{9,1},{17,25},{25,17},{2,10},{10... | collective-permute-start | bytes 1769480 | tf_op jit(solution)/shard_map/ppermute | solution.py:639
  490.2 14.4 %collective-permute-start.30 = (bf16[48,384]{1,0:T(8,128)(2,1)S(1)}, bf16[48,384]{1,0:T(8,128)(2,1)S(1)}, u32[]{:S(2)}, u32[]{:S(2)}) collective-permute-start(bf16[48,384]{1,0:T(8,128)(2,1)S(1)} %add_convert_fusion.42), channel_id=1, source_target_pairs={{0,16},{8,24},{16,0},{24,8},{1,17},{9,25},{17,1},{25,9},{2,18},{10... | collective-permute-start | bytes 110600 | tf_op jit(solution)/shard_map/ppermute | solution.py:639
  493.6 15.7 %collective-permute-start.40 = (bf16[48,384]{1,0:T(8,128)(2,1)S(1)}, bf16[48,384]{1,0:T(8,128)(2,1)S(1)}, u32[]{:S(2)}, u32[]{:S(2)}) collective-permute-start(bf16[48,384]{1,0:T(8,128)(2,1)S(1)} %add_convert_fusion.39), channel_id=1, source_target_pairs={{0,16},{8,24},{16,0},{24,8},{1,17},{9,25},{17,1},{25,9},{2,18},{10... | collective-permute-start | bytes 110600 | tf_op jit(solution)/shard_map/ppermute | solution.py:639
  493.8 18.7 %collective-permute-start.21 = (bf16[48,384]{1,0:T(8,128)(2,1)S(1)}, bf16[48,384]{1,0:T(8,128)(2,1)S(1)}, u32[]{:S(2)}, u32[]{:S(2)}) collective-permute-start(bf16[48,384]{1,0:T(8,128)(2,1)S(1)} %add_convert_fusion.44), channel_id=1, source_target_pairs={{0,16},{8,24},{16,0},{24,8},{1,17},{9,25},{17,1},{25,9},{2,18},{10... | collective-permute-start | bytes 110600 | tf_op jit(solution)/shard_map/ppermute | solution.py:639
  507.8 29.1 %collective-permute-start.53 = (bf16[192,3072]{1,0:T(8,128)(2,1)S(1)}, bf16[192,3072]{1,0:T(8,128)(2,1)}, u32[]{:S(2)}, u32[]{:S(2)}) collective-permute-start(bf16[192,3072]{1,0:T(8,128)(2,1)S(1)} %maximum_select_fusion.5), channel_id=1, source_target_pairs={{0,4},{2,6},{4,0},{6,2},{1,5},{3,7},{5,1},{7,3},{8,12},{10,14},{12... | collective-permute-start | bytes 3538952 | tf_op jit(solution)/shard_map/ppermute | solution.py:639
  519.0 23.2 %collective-permute-start.23 = (bf16[192,384]{1,0:T(8,128)(2,1)}, bf16[192,384]{1,0:T(8,128)(2,1)}, u32[]{:S(2)}, u32[]{:S(2)}) collective-permute-start(bf16[192,384]{1,0:T(8,128)(2,1)} %maximum_select_fusion.22), channel_id=1, source_target_pairs={{0,4},{2,6},{4,0},{6,2},{1,5},{3,7},{5,1},{7,3},{8,12},{10,14},{12... | collective-permute-start | bytes 442376 | tf_op jit(solution)/shard_map/ppermute | solution.py:639
  520.2 24.4 %collective-permute-start.33 = (bf16[192,384]{1,0:T(8,128)(2,1)}, bf16[192,384]{1,0:T(8,128)(2,1)}, u32[]{:S(2)}, u32[]{:S(2)}) collective-permute-start(bf16[192,384]{1,0:T(8,128)(2,1)} %maximum_select_fusion.23), channel_id=1, source_target_pairs={{0,4},{2,6},{4,0},{6,2},{1,5},{3,7},{5,1},{7,3},{8,12},{10,14},{12... | collective-permute-start | bytes 442376 | tf_op jit(solution)/shard_map/ppermute | solution.py:639
  522.4 24.1 %collective-permute-start.43 = (bf16[192,384]{1,0:T(8,128)(2,1)}, bf16[192,384]{1,0:T(8,128)(2,1)}, u32[]{:S(2)}, u32[]{:S(2)}) collective-permute-start(bf16[192,384]{1,0:T(8,128)(2,1)} %maximum_select_fusion.24), channel_id=1, source_target_pairs={{0,4},{2,6},{4,0},{6,2},{1,5},{3,7},{5,1},{7,3},{8,12},{10,14},{12... | collective-permute-start | bytes 442376 | tf_op jit(solution)/shard_map/ppermute | solution.py:639
  539.1 42.7 %collective-permute-start.54 = (bf16[384,3072]{1,0:T(8,128)(2,1)S(1)}, bf16[384,3072]{1,0:T(8,128)(2,1)}, u32[]{:S(2)}, u32[]{:S(2)}) collective-permute-start(bf16[384,3072]{1,0:T(8,128)(2,1)S(1)} %maximum_select_fusion.3), channel_id=1, source_target_pairs={{0,2},{2,0},{4,6},{6,4},{1,3},{3,1},{5,7},{7,5},{8,10},{10,8},{12,... | collective-permute-start | bytes 7077896 | tf_op jit(solution)/shard_map/ppermute | solution.py:639
  546.5 12.3 %collective-permute-start.34 = (bf16[384,384]{1,0:T(8,128)(2,1)}, bf16[384,384]{1,0:T(8,128)(2,1)}, u32[]{:S(2)}, u32[]{:S(2)}) collective-permute-start(bf16[384,384]{1,0:T(8,128)(2,1)} %maximum_select_fusion.16), channel_id=1, source_target_pairs={{0,2},{2,0},{4,6},{6,4},{1,3},{3,1},{5,7},{7,5},{8,10},{10,8},{12,... | collective-permute-start | bytes 884744 | tf_op jit(solution)/shard_map/ppermute | solution.py:639
  548.5 14.1 %collective-permute-start.44 = (bf16[384,384]{1,0:T(8,128)(2,1)}, bf16[384,384]{1,0:T(8,128)(2,1)}, u32[]{:S(2)}, u32[]{:S(2)}) collective-permute-start(bf16[384,384]{1,0:T(8,128)(2,1)} %maximum_select_fusion.17), channel_id=1, source_target_pairs={{0,2},{2,0},{4,6},{6,4},{1,3},{3,1},{5,7},{7,5},{8,10},{10,8},{12,... | collective-permute-start | bytes 884744 | tf_op jit(solution)/shard_map/ppermute | solution.py:639
  (62 other events, 508.9 us)

commit v2 on v1

v2 whole, which is shorter than its diff:
```python
import functools

import jax
import jax.numpy as jnp
from jax import lax
from jax.experimental import pallas as pl
from jax.experimental.pallas import tpu as pltpu
from jax.sharding import PartitionSpec as P

epsilon = 1e-05
f32 = jnp.float32
bf16 = jnp.bfloat16
CHUNK = 256
BLOCK = 512
VMEM_LIMIT = 60 * 1024 * 1024
GELU_A = 0.7978845608028654
GELU_B = 0.044715


def dot(left, right):
    return lax.dot_general(left, right, (((1,), (0,)), ((), ())), preferred_element_type=f32)


def dot_t(left, right):
    return lax.dot_general(left, right, (((1,), (1,)), ((), ())), preferred_element_type=f32)


def params():
    return pltpu.CompilerParams(
        dimension_semantics=("arbitrary",), vmem_limit_bytes=VMEM_LIMIT
    )


def small_cost():
    return pl.CostEstimate(flops=1000, bytes_accessed=1000, transcendentals=0)


def shaped(shape, kind=bf16):
    return jax.ShapeDtypeStruct(shape, kind)


def once(shape):
    zeros = (0,) * len(shape)
    return pl.BlockSpec(shape, lambda *_: zeros, pipeline_mode=pl.Buffered(1))


def by_rows(count, cols, at=0):
    return pl.BlockSpec((count, cols), lambda c, *_: (c, at))


def by_cols(rows, count, at=0):
    return pl.BlockSpec((rows, count), lambda c, *_: (at, c))


anywhere = pl.BlockSpec(memory_space=pl.ANY)
scalars = pl.BlockSpec(memory_space=pltpu.SMEM)


def first_lanes():
    return lax.broadcasted_iota(jnp.int32, (1, 128), 1) < 64


def first_sublanes():
    return lax.broadcasted_iota(jnp.int32, (128, 1), 0) < 64


def half_blocks(size):
    rows = lax.broadcasted_iota(jnp.int32, (size, size), 0) // 64
    cols = lax.broadcasted_iota(jnp.int32, (size, size), 1) // 64
    return rows, cols


def soft_rows(logits):
    count, size = logits.shape
    groups = logits.reshape(count // 64, 64, size)
    grown = jnp.exp(groups - jnp.max(groups, axis=1, keepdims=True))
    soft = grown * (1.0 / jnp.sum(grown, axis=1, keepdims=True))
    return soft.reshape(count, size)


def norm_parts(values):
    centred = values - jnp.mean(values, axis=1, keepdims=True)
    spread = lax.rsqrt(jnp.mean(centred * centred, axis=1, keepdims=True) + epsilon)
    return centred * spread, spread


def norm_back(gradient, normed, spread, gain):
    scaled = gradient * gain
    return spread * (
        scaled
        - jnp.mean(scaled, axis=1, keepdims=True)
        - normed * jnp.mean(scaled * normed, axis=1, keepdims=True)
    )


def run_copies(copies):
    for copy in copies:
        copy.start()
    for copy in copies:
        copy.wait()


def qkv_copies(pieces, order, kinds, target, sems, first_sem):
    rows = pieces[0].shape[1]
    copies = []
    for i, piece in enumerate(pieces):
        where = 0 if len(pieces) == 1 else pl.multiple_of(order[i] * rows, 16)
        for at, kind in enumerate(kinds):
            wide = piece.shape[2]
            copies.append(
                pltpu.make_async_copy(
                    piece.at[kind],
                    target.at[pl.ds(where, rows), pl.ds(at * wide, wide)],
                    sems.at[first_sem + len(copies)],
                )
            )
    return copies


def norm_kernel(tokens, gain, h_out, turned_out):
    normed, _ = norm_parts(tokens[...].astype(f32))
    low = (normed * gain[...]).astype(bf16)
    h_out[...] = low
    turned_out[...] = low.T


def norm_one(tokens, gain):
    rows, width = tokens.shape
    return pl.pallas_call(
        norm_kernel,
        grid=(rows // BLOCK,),
        in_specs=[by_rows(BLOCK, width), once((1, width))],
        out_specs=[by_rows(BLOCK, width), by_cols(width, BLOCK)],
        out_shape=[shaped((rows, width)), shaped((width, rows))],
        compiler_params=params(),
        cost_estimate=small_cost(),
        name="norm_one",
    )(tokens, gain)


def write_state(state, state_out, pairs):
    top = first_sublanes()
    sums = []
    for p in range(pairs):
        state_out[128 * p : 128 * p + 128] = jnp.where(top, state[2 * p], state[2 * p + 1])
        sums.append(state[2 * p, 64:65, :])
        sums.append(state[2 * p + 1, 0:1, :])
    tail = state_out.shape[0] - 128 * pairs
    sums.append(jnp.zeros((tail - 2 * pairs, 128), f32))
    state_out[128 * pairs :] = jnp.concatenate(sums, axis=0)


def read_state(packed, p, h_at, pairs):
    row = 128 * pairs + 2 * p + h_at
    whole = packed[128 * p : 128 * p + 128, :]
    sums = packed[row : row + 1, :]
    sel = first_sublanes() if h_at == 0 else jnp.logical_not(first_sublanes())
    return jnp.where(sel, whole, sums)


def keys_kernel(pairs, count, order, h, fext, *refs):
    pieces = refs[:count]
    k_out, v_out, turned_v_out, phi_out, turned_phi_out, prefix_out, state_out = refs[count : count + 7]
    w_kv, state, sems = refs[count + 7 :]
    step = pl.program_id(0)
    wide = 128 * pairs

    @pl.when(step == 0)
    def _():
        run_copies(qkv_copies(pieces, order, (1, 2), w_kv, sems, 0))
        state[...] = jnp.zeros_like(state)

    kv_all = dot(h[...], w_kv[...]).astype(bf16)
    turned_k_all = kv_all[:, :wide].T
    turned_v_all = kv_all[:, wide:].T
    k_out[...] = turned_k_all
    v_out[...] = kv_all[:, wide:]
    turned_v_out[...] = turned_v_all
    top = first_sublanes()
    one = jnp.ones((1, 1), bf16)
    for sub in range(h.shape[0] // CHUNK):
        run = slice(CHUNK * sub, CHUNK * sub + CHUNK)
        turned_k, turned_v = turned_k_all[:, run], turned_v_all[:, run]
        prefix_out[sub] = state[...].astype(bf16)
        for p in range(pairs):
            turned_phi = soft_rows(dot(fext[p], turned_k[128 * p : 128 * p + 128])).astype(bf16)
            phi = turned_phi.T
            turned_phi_out[256 * p : 256 * p + 256, run] = turned_phi
            phi_out[run, 256 * p : 256 * p + 256] = phi
            values = turned_v[128 * p : 128 * p + 128]
            for h_at in range(2):
                sel = top if h_at == 0 else jnp.logical_not(top)
                padded = jnp.where(sel, values, one)
                state[2 * p + h_at] += dot(padded, phi[:, 128 * h_at : 128 * h_at + 128])

    @pl.when(step == pl.num_programs(0) - 1)
    def _():
        write_state(state, state_out, pairs)


def key_pass(h, weights, order, fext):
    rows, width = h.shape
    pairs = fext.shape[0]
    wide = 128 * pairs
    count = rows // CHUNK
    packed = wide + 16
    return list(
        pl.pallas_call(
            functools.partial(keys_kernel, pairs, len(weights)),
            grid=(rows // BLOCK,),
            in_specs=[scalars, by_rows(BLOCK, width), once(fext.shape)]
            + [anywhere] * len(weights),
            out_specs=[
                by_cols(wide, BLOCK),
                by_rows(BLOCK, wide),
                by_cols(wide, BLOCK),
                by_rows(BLOCK, 2 * wide),
                by_cols(2 * wide, BLOCK),
                pl.BlockSpec((BLOCK // CHUNK, 2 * pairs, 128, 128), lambda c: (c, 0, 0, 0)),
                pl.BlockSpec((packed, 128), lambda c: (0, 0)),
            ],
            out_shape=[
                shaped((wide, rows)),
                shaped((rows, wide)),
                shaped((wide, rows)),
                shaped((rows, 2 * wide)),
                shaped((2 * wide, rows)),
                shaped((count, 2 * pairs, 128, 128)),
                shaped((packed, 128), f32),
            ],
            scratch_shapes=[
                pltpu.VMEM((width, 2 * wide), bf16),
                pltpu.VMEM((2 * pairs, 128, 128), f32),
                pltpu.SemaphoreType.DMA((2 * len(weights),)),
            ],
            compiler_params=params(),
            cost_estimate=small_cost(),
            name="key_pass",
        )(order, h, fext, *weights)
    )


def query_kernel(pairs, count, order, h, turned_k_phi, v, prefix, fext, *refs):
    pieces = refs[:count]
    q_out, phi_out, turned_phi_out, numer_out, w_q, sems = refs[count:]

    @pl.when(pl.program_id(0) == 0)
    def _():
        run_copies(qkv_copies(pieces, order, (0,), w_q, sems, 0))

    turned_q_all = dot(h[...], w_q[...]).astype(bf16).T
    q_out[...] = turned_q_all
    first = first_lanes()
    one = jnp.ones((1, 1), bf16)
    size = CHUNK
    past = lax.broadcasted_iota(jnp.int32, (size, size), 0) >= lax.broadcasted_iota(
        jnp.int32, (size, size), 1
    )
    for sub in range(h.shape[0] // CHUNK):
        run = slice(CHUNK * sub, CHUNK * sub + CHUNK)
        turned_q = turned_q_all[:, run]
        for p in range(pairs):
            turned_phi = soft_rows(dot(fext[p], turned_q[128 * p : 128 * p + 128])).astype(bf16)
            phi = turned_phi.T
            turned_phi_out[256 * p : 256 * p + 256, run] = turned_phi
            phi_out[run, 256 * p : 256 * p + 256] = phi
            v_two = v[run, 128 * p : 128 * p + 128]
            for h_at in range(2):
                at = 256 * p + 128 * h_at
                sel = first if h_at == 0 else jnp.logical_not(first)
                padded = jnp.where(sel, v_two, one)
                phi_q = phi[:, 128 * h_at : 128 * h_at + 128]
                scores = dot(phi_q, turned_k_phi[at : at + 128, run])
                scores = jnp.where(past, scores, 0.0).astype(bf16)
                numer_out[run, at : at + 128] = dot(scores, padded) + dot_t(
                    phi_q, prefix[sub, 2 * p + h_at]
                )


def query_pass(h, weights, order, turned_k_phi, v, prefix, fext):
    rows, width = h.shape
    pairs = fext.shape[0]
    wide = 128 * pairs
    return list(
        pl.pallas_call(
            functools.partial(query_kernel, pairs, len(weights)),
            grid=(rows // BLOCK,),
            in_specs=[
                scalars,
                by_rows(BLOCK, width),
                by_cols(2 * wide, BLOCK),
                by_rows(BLOCK, wide),
                pl.BlockSpec((BLOCK // CHUNK, 2 * pairs, 128, 128), lambda c: (c, 0, 0, 0)),
                once(fext.shape),
            ]
            + [anywhere] * len(weights),
            out_specs=[
                by_cols(wide, BLOCK),
                by_rows(BLOCK, 2 * wide),
                by_cols(2 * wide, BLOCK),
                by_rows(BLOCK, 2 * wide),
            ],
            out_shape=[
                shaped((wide, rows)),
                shaped((rows, 2 * wide)),
                shaped((2 * wide, rows)),
                shaped((rows, 2 * wide), f32),
            ],
            scratch_shapes=[
                pltpu.VMEM((width, wide), bf16),
                pltpu.SemaphoreType.DMA((len(weights),)),
            ],
            compiler_params=params(),
            cost_estimate=small_cost(),
            name="query_pass",
        )(order, h, turned_k_phi, v, prefix, fext, *weights)
    )


def middle_kernel(
    pairs,
    tile,
    order,
    tokens,
    d_out,
    numer_own,
    numer_oth,
    phi_own,
    phi_oth,
    incoming,
    gain,
    cross,
    wo_any,
    up_any,
    down_any,
    up_0,
    up_1,
    up_2,
    up_3,
    down_0,
    down_1,
    down_2,
    down_3,
    act_out,
    pre_out,
    mixed_out,
    resid_out,
    gn_out,
    gd_out,
    turned_h_out,
    turned_a_out,
    turned_n_out,
    turned_d_out,
    state_out,
    gain_out,
    held,
    attended_out,
    exact,
    inverse,
    wo_own,
    up_own,
    down_own,
    up_oth,
    down_oth,
    sems,
):
    step = pl.program_id(0)
    first = first_lanes()
    top = first_sublanes()
    wide = 128 * pairs
    units = up_own.shape[1]
    numer = (numer_own, numer_oth)
    phi = (phi_own, phi_oth)

    def weight_copies():
        copies = [
            pltpu.make_async_copy(source, target, sems.at[i])
            for i, (source, target) in enumerate(
                ((wo_any, wo_own), (up_any, up_own), (down_any, down_own))
            )
        ]
        for group, target, first_at in (
            ((up_0, up_1, up_2, up_3), up_oth, 2),
            ((down_0, down_1, down_2, down_3), down_oth, 6),
        ):
            for i, piece in enumerate(group):
                count = piece.shape[0]
                where = pl.multiple_of(order[first_at + i] * count, 16)
                copies.append(
                    pltpu.make_async_copy(
                        piece, target.at[pl.ds(where, count)], sems.at[len(copies)]
                    )
                )
        return copies

    @pl.when(step == 0)
    def _():
        for copy in weight_copies():
            copy.start()
        state_out[...] = jnp.zeros_like(state_out)
        gain_out[...] = jnp.zeros_like(gain_out)
        for half in range(2):
            for p in range(pairs):
                for h_at in range(2):
                    held[half, 2 * p + h_at] = read_state(
                        incoming.at[half], p, h_at, pairs
                    ).astype(bf16)

    for half in range(2):
        for p in range(pairs):
            sums = []
            for h_at in range(2):
                at = 256 * p + 128 * h_at
                sums.append(
                    numer[half][:, at : at + 128]
                    + dot_t(phi[half][:, at : at + 128], held[half, 2 * p + h_at])
                )
            numerator = jnp.where(first, sums[0], sums[1])
            swapped = 1.0 / jnp.where(first, sums[1], sums[0])
            inv = pltpu.roll(swapped, 64, 1)
            value = numerator * inv
            at = wide * half + 128 * p
            exact[:, at : at + 128] = value
            inverse[:, at : at + 128] = swapped
            attended = value.astype(bf16)
            attended_out[:, at : at + 128] = attended
            turned_a_out[at : at + 128, :] = attended.T

    @pl.when(step == 0)
    def _():
        for copy in weight_copies():
            copy.wait()

    wo_oth = down_oth.at[pl.ds(units, wide)]
    resid = (
        tokens[...].astype(f32)
        + dot(attended_out[:, :wide], wo_own[...])
        + dot(attended_out[:, wide:], wo_oth[...])
    )
    normed, spread = norm_parts(resid)
    h_two = (normed * gain[...]).astype(bf16)
    turned_h_out[...] = h_two.T
    d_low = d_out[...]
    mixed = grad_h = None
    for half in range(2):
        up = (up_own, up_oth)[half]
        down = (down_own, down_oth)[half]
        for at in range(0, units, tile):
            pre = dot(h_two, up[:, at : at + tile])
            square = pre * pre
            swing = jnp.tanh(GELU_A * pre * (1.0 + GELU_B * square))
            half_up = 0.5 + 0.5 * swing
            act = (pre * half_up).astype(bf16)
            slope = half_up + (0.5 * GELU_A) * pre * (1.0 - swing * swing) * (
                1.0 + (3.0 * GELU_B) * square
            )
            grad_act = dot_t(d_low, down[at : at + tile, :])
            grad_pre = (grad_act * slope).astype(bf16)
            act_out[half * units + at : half * units + at + tile, :] = act.T
            for col in range(0, tile, 256):
                spot = half * units + at + col
                pre_out[spot // 768, :, spot % 768 : spot % 768 + 256] = grad_pre[
                    :, col : col + 256
                ]
            part = dot(act, down[at : at + tile, :])
            mixed = part if mixed is None else mixed + part
            part = dot_t(grad_pre, up[:, at : at + tile])
            grad_h = part if grad_h is None else grad_h + part
    mixed_out[...] = (resid + mixed).astype(bf16)
    gain_out[...] += jnp.sum(grad_h * normed, axis=0, keepdims=True)
    grad_resid = (d_low.astype(f32) + norm_back(grad_h, normed, spread, gain[...])).astype(bf16)
    resid_out[...] = grad_resid

    for half in range(2):
        grad_att = dot_t(grad_resid, (wo_own, wo_oth)[half][...]).astype(bf16).astype(f32)
        for p in range(pairs):
            at = wide * half + 128 * p
            own = grad_att[:, 128 * p : 128 * p + 128]
            swapped = inverse[:, at : at + 128]
            grad_n = (own * pltpu.roll(swapped, 64, 1)).astype(bf16)
            total = dot((own * exact[:, at : at + 128]).astype(bf16), cross[...])
            grad_d = ((-1.0 / 64.0) * total * swapped).astype(bf16)
            gn_out[:, at : at + 128] = grad_n
            gd_out[:, at : at + 128] = grad_d
            turned_n = grad_n.T
            turned_d = grad_d.T
            turned_n_out[at : at + 128, :] = turned_n
            turned_d_out[at : at + 128, :] = turned_d
            left = jnp.concatenate([turned_n, turned_d[0:16], turned_d[64:80]], axis=0)
            sums = dot(left, phi[half][:, 256 * p : 256 * p + 256])
            state_out[half, 128 * p : 128 * p + 128] += jnp.where(
                top, sums[:128, :128], sums[:128, 128:]
            )
            row = wide + 2 * p
            state_out[half, row : row + 1] += sums[144:145, :128]
            state_out[half, row + 1 : row + 2] += sums[128:129, 128:]


def middle_pass(
    order, tokens, d_out, numers, phis, incoming, gain, cross, owns, ups, downs, block, tile
):
    rows, width = tokens.shape
    wide = owns[0].shape[0]
    pairs = wide // 128
    units = owns[1].shape[1]
    cols_out = [width, width, 2 * wide, 2 * wide]
    parts = 2 * units // 768
    return pl.pallas_call(
        functools.partial(middle_kernel, pairs, tile),
        grid=(rows // block,),
        in_specs=[scalars]
        + [by_rows(block, width)] * 2
        + [by_rows(block, 2 * wide)] * 4
        + [once(incoming.shape), once(gain.shape), once(cross.shape)]
        + [anywhere] * 11,
        out_specs=[by_cols(2 * units, block), pl.BlockSpec((parts, block, 768), lambda c: (0, c, 0))]
        + [by_rows(block, c) for c in cols_out]
        + [by_cols(width, block)]
        + [by_cols(2 * wide, block)] * 3
        + [
            pl.BlockSpec(incoming.shape, lambda c: (0, 0, 0)),
            pl.BlockSpec((1, width), lambda c: (0, 0)),
        ],
        out_shape=[shaped((2 * units, rows)), shaped((parts, rows, 768))]
        + [shaped((rows, c)) for c in cols_out]
        + [shaped((width, rows))]
        + [shaped((2 * wide, rows))] * 3
        + [shaped(incoming.shape, f32), shaped((1, width), f32)],
        scratch_shapes=[
            pltpu.VMEM((2, 2 * pairs, 128, 128), bf16),
            pltpu.VMEM((block, 2 * wide), bf16),
            pltpu.VMEM((block, 2 * wide), f32),
            pltpu.VMEM((block, 2 * wide), f32),
            pltpu.VMEM((wide, width), bf16),
            pltpu.VMEM((width, units), bf16),
            pltpu.VMEM((units, width), bf16),
            pltpu.VMEM((width, units), bf16),
            pltpu.VMEM((units + wide, width), bf16),
            pltpu.SemaphoreType.DMA((11,)),
        ],
        compiler_params=params(),
        cost_estimate=small_cost(),
        name="middle_pass",
    )(order, tokens, d_out, *numers, *phis, incoming, gain, cross, *owns, *ups, *downs)


def up_kernel(side, left, right, out):
    out[0] = dot(left[...], right[0]).astype(bf16)


def up_pass(side, left, right):
    width, rows = left.shape
    count, _, part = right.shape
    half = lambda step, side: (step // (count // 2) + side[0]) % 2
    return pl.pallas_call(
        up_kernel,
        grid_spec=pltpu.PrefetchScalarGridSpec(
            num_scalar_prefetch=1,
            grid=(count,),
            in_specs=[once((width, rows)), pl.BlockSpec((1, rows, part), lambda s, c: (s, 0, 0))],
            out_specs=pl.BlockSpec((1, width, part), lambda s, c: (half(s, c), 0, s % (count // 2))),
        ),
        out_shape=shaped((2, width, count // 2 * part)),
        compiler_params=params(),
        cost_estimate=small_cost(),
        name="up_pass",
    )(side, left, right)


def down_kernel(left, right, left_more, right_more, out):
    count = left.shape[0]
    main = dot(left[...], right[...])
    rest = dot(left_more[...], right_more[...])
    out[0, :count] = main.astype(bf16)
    out[0, count:] = rest.astype(bf16)


def down_kept_kernel(left, right, left_more, right_more, got, own_out, oth_out):
    count = left.shape[0]
    main = (dot(left[...], right[...]) + got[0, :count].astype(f32)).astype(bf16)
    rest = (dot(left_more[...], right_more[...]) + got[0, count:].astype(f32)).astype(bf16)

    @pl.when(pl.program_id(0) == 0)
    def _():
        oth_out[:count] = main
        oth_out[count:] = rest

    @pl.when(pl.program_id(0) == 1)
    def _():
        own_out[:count] = main
        own_out[count:] = rest


def down_pass(half, left, right, left_more, right_more, got=()):
    rows, width = right.shape
    part = left.shape[0] // 4
    more = left_more.shape[0] // 4
    out = pl.BlockSpec((1, part + more, width), lambda side, half: (1 - side, 0, 0))
    kept = pl.BlockSpec((part + more, width), lambda side, half: (0, 0))

    def kernel(half, *refs):
        (down_kept_kernel if got else down_kernel)(*refs)

    return pl.pallas_call(
        kernel,
        grid_spec=pltpu.PrefetchScalarGridSpec(
            num_scalar_prefetch=1,
            grid=(2,),
            in_specs=[
                pl.BlockSpec((part, rows), lambda side, half: (2 - 2 * side + half[0], 0)),
                once((rows, width)),
                pl.BlockSpec((more, rows), lambda side, half: (2 - 2 * side + half[0], 0)),
                once((rows, width)),
            ]
            + [out] * len(got),
            out_specs=[kept] * 2 if got else out,
        ),
        out_shape=[shaped((part + more, width))] * 2
        if got
        else shaped((2, part + more, width)),
        compiler_params=params(),
        cost_estimate=small_cost(),
        name="down_pass",
    )(half, left, right, left_more, right_more, *got)


def back_kernel(pairs, side, at_pair, more, core, *refs):
    (q, k, v, turned_v, pq, turned_pq, pk, turned_pk, gn, gd, turned_n, turned_d) = refs[:12]
    prefix, incoming, later, fq, fk, ones, h_any = refs[12:19]
    earlier = refs[19 : 19 + more]
    grad_out, send_out, keep_out, map_out = refs[19 + more : 23 + more]
    held, state, grads, maps, turned_h, sem = refs[23 + more :]
    step = pl.program_id(0)
    last = pl.num_programs(0) - 1
    first = first_lanes()
    top = first_sublanes()
    size = CHUNK
    inner = v.shape[0] // CHUNK
    past = lax.broadcasted_iota(jnp.int32, (size, size), 0) >= lax.broadcasted_iota(
        jnp.int32, (size, size), 1
    )
    one = jnp.ones((1, 1), bf16)

    @pl.when(step == 0)
    def _():
        pltpu.make_async_copy(h_any, turned_h, sem.at[0]).start()
        maps[...] = jnp.zeros_like(maps)
        for h_at in range(2):
            held[h_at] = read_state(incoming.at[side], at_pair, h_at, pairs)
            state[h_at] = read_state(later.at[side], at_pair, h_at, pairs)

    for sub in reversed(range(inner)):
        run = slice(CHUNK * sub, CHUNK * sub + CHUNK)
        grads_q, grads_k, grads_v = [], [], []
        for h_at in range(2):
            sel = first if h_at == 0 else jnp.logical_not(first)
            sel_top = top if h_at == 0 else jnp.logical_not(top)
            lanes = slice(128 * h_at, 128 * h_at + 128)
            padded_v = jnp.where(sel, v[run, :], one)
            padded_vt = jnp.where(sel_top, turned_v[:, run], one)
            padded_g = jnp.where(sel, gn[run, :], gd[run, :])
            padded_gt = jnp.where(sel_top, turned_n[:, run], turned_d[:, run])
            before = (prefix[sub, h_at].astype(f32) + held[h_at]).astype(bf16)
            after = state[h_at].astype(bf16)
            e = jnp.where(past, dot_t(padded_g, padded_v), 0.0).astype(bf16)
            s = jnp.where(past, dot(pq[run, lanes], turned_pk[lanes, run]), 0.0).astype(bf16)
            grads_q.append(dot(e, pk[run, lanes]) + dot(padded_g, before))
            grads_k.append(dot(turned_pq[lanes, run], e) + dot(after.T, padded_vt))
            grads_v.append(dot(padded_gt, s) + dot(after, turned_pk[lanes, run]))
            state[h_at] += dot(padded_gt, pq[run, lanes])

        grad_phi = jnp.concatenate(grads_q, axis=1)
        phi = pq[run, :].astype(f32)
        shared = dot((phi * grad_phi).astype(bf16), ones[...])
        grad_u = (phi * (grad_phi - shared)).astype(bf16)
        maps[0] += dot(q[:, run], grad_u)
        grad_q = dot_t(grad_u, fq[0]).astype(bf16)

        grad_phi = jnp.concatenate(grads_k, axis=0).reshape(4, 64, size)
        phi = turned_pk[:, run].astype(f32).reshape(4, 64, size)
        shared = jnp.sum(phi * grad_phi, axis=1, keepdims=True)
        grad_u = (phi * (grad_phi - shared)).reshape(256, size).astype(bf16)
        maps[1] += dot_t(k[:, run], grad_u)
        grad_k = dot(fk[0], grad_u).astype(bf16).T
        grad_v = jnp.where(top, grads_v[0], grads_v[1]).astype(bf16).T

        joined = jnp.concatenate([grad_q, grad_k, grad_v], axis=1)
        grad_out[run, :] = joined
        where = pl.multiple_of(((last - step) * inner + sub) * size, size)
        grads[pl.ds(where, size), :] = joined

    @pl.when(step == last)
    def _():
        pltpu.make_async_copy(h_any, turned_h, sem.at[0]).wait()
        product = dot(turned_h[...], grads[...]).astype(bf16)
        part = product.shape[0] // 2
        mine = core[0] == 0
        low, high = product[:part], product[part:]
        send_out[0:part] = jnp.where(mine, high, low)
        keep_out[0:part] = jnp.where(mine, low, high)
        joins = [jnp.where(top, maps[i][:, :128], maps[i][:, 128:]) for i in range(2)]
        turns = [pltpu.roll(j, 64, 1) for j in joins]
        own_map = jnp.where(first, joins[0] - turns[0], turns[1] - joins[1]).astype(bf16)
        map_out[...] = own_map
        if more:
            whole = jnp.concatenate([m[...] for m in earlier] + [own_map], axis=1)
            low, high = whole[:64], whole[64:]
            send_out[part : part + 64] = jnp.where(mine, high, low)
            keep_out[part : part + 64] = jnp.where(mine, low, high)
            send_out[part + 64 :] = jnp.zeros_like(low)
            keep_out[part + 64 :] = jnp.zeros_like(low)


def back_pass(side, at, core, firsts, seconds, prefix, incoming, later, fq, fk, ones, turned_h, earlier):
    (q, k, v, turned_v, pq, turned_pq, pk, turned_pk) = firsts
    gn, gd, turned_n, turned_d = seconds
    rows = v.shape[0]
    pairs = fq.shape[0]
    width = turned_h.shape[0]
    count = rows // BLOCK
    both = pairs * side + at
    here = lambda cols, spot: pl.BlockSpec((BLOCK, cols), lambda c, core: (count - 1 - c, spot))
    turned = lambda cols, spot: pl.BlockSpec((cols, BLOCK), lambda c, core: (spot, count - 1 - c))
    weights = pl.BlockSpec((1, 128, 256), lambda c, core: (at, 0, 0))
    more = len(earlier)
    sums = (width // 2 + (128 if more else 0), 384)
    whole = lambda dims: pl.BlockSpec(dims, lambda c, core: (0,) * len(dims))
    return pl.pallas_call(
        functools.partial(back_kernel, pairs, side, at, more),
        grid_spec=pltpu.PrefetchScalarGridSpec(
            num_scalar_prefetch=1,
            grid=(count,),
            in_specs=[turned(128, at), turned(128, at), here(128, at), turned(128, at)]
            + [here(256, at), turned(256, at)] * 2
            + [here(128, both)] * 2
            + [turned(128, both)] * 2
            + [pl.BlockSpec((BLOCK // CHUNK, 2, 128, 128), lambda c, core: (count - 1 - c, at, 0, 0))]
            + [once(incoming.shape)] * 2
            + [weights] * 2
            + [once(ones.shape), anywhere]
            + [once((128, 128))] * more,
            out_specs=[here(384, 0), whole(sums), whole(sums), whole((128, 128))],
            scratch_shapes=[
                pltpu.VMEM((2, 128, 128), f32),
                pltpu.VMEM((2, 128, 128), f32),
                pltpu.VMEM((rows, 384), bf16),
                pltpu.VMEM((2, 128, 256), f32),
                pltpu.VMEM((width, rows), bf16),
                pltpu.SemaphoreType.DMA((1,)),
            ],
        ),
        out_shape=[shaped((rows, 384)), shaped(sums), shaped(sums), shaped((128, 128))],
        compiler_params=params(),
        cost_estimate=small_cost(),
        name="back_pass",
    )(core, *firsts, *seconds, prefix, incoming, later, fq, fk, ones, turned_h, *earlier)


def tokens_kernel(pairs, count, order, tokens, resid, gain, *refs):
    pieces = refs[: 1 + count]
    grads = refs[1 + count : 1 + count + 2 * pairs]
    out, gain_out, w_own, w_oth, sems = refs[1 + count + 2 * pairs :]

    @pl.when(pl.program_id(0) == 0)
    def _():
        copies = qkv_copies(pieces[:1], order, (0, 1, 2), w_own, sems, 0)
        copies += qkv_copies(pieces[1:], order, (0, 1, 2), w_oth, sems, 3)
        run_copies(copies)
        gain_out[...] = jnp.zeros_like(gain_out)

    normed, spread = norm_parts(tokens[...].astype(f32))
    total = None
    for half in range(2):
        joined = jnp.concatenate(
            [
                g[:, 128 * kind : 128 * kind + 128]
                for kind in range(3)
                for g in grads[half * pairs : half * pairs + pairs]
            ],
            axis=1,
        )
        part = dot_t(joined, (w_own, w_oth)[half][...])
        total = part if total is None else total + part
    gain_out[...] += jnp.sum(total * normed, axis=0, keepdims=True)
    back = norm_back(total, normed, spread, gain[...])
    out[...] = (resid[...].astype(f32) + back).astype(bf16)


def tokens_pass(order, tokens, resid, gain, w_own, pieces, grads, block):
    rows, width = tokens.shape
    pairs = len(grads) // 2
    cols = 3 * w_own.shape[2]
    count = len(pieces)
    return pl.pallas_call(
        functools.partial(tokens_kernel, pairs, count),
        grid=(rows // block,),
        in_specs=[scalars]
        + [by_rows(block, width)] * 2
        + [once(gain.shape)]
        + [anywhere] * (1 + count)
        + [by_rows(block, 384)] * len(grads),
        out_specs=[by_rows(block, width), pl.BlockSpec((1, width), lambda c: (0, 0))],
        out_shape=[shaped((rows, width)), shaped((1, width), f32)],
        scratch_shapes=[
            pltpu.VMEM((width, cols), bf16),
            pltpu.VMEM((width, cols), bf16),
            pltpu.SemaphoreType.DMA((3 + 3 * count,)),
        ],
        compiler_params=params(),
        cost_estimate=small_cost(),
        name="tokens_pass",
    )(order, tokens, resid, gain, w_own, *pieces, *grads)


def cross_to(value, axis, flip):
    count = lax.axis_size(axis)
    return lax.ppermute(value, axis, [(i, i ^ flip) for i in range(count)])


def swap(value, axis, bit):
    return cross_to(value, axis, 1 << bit)


def bit_of(axis, bit):
    return (lax.axis_index(axis) >> bit) & 1


def bits_of(axis):
    return lax.axis_size(axis).bit_length() - 1


def ordered(bit, mine, theirs, axis=0):
    return jnp.where(
        bit == 0,
        jnp.concatenate([mine, theirs], axis),
        jnp.concatenate([theirs, mine], axis),
    )


def add_low(*parts):
    total = parts[0].astype(f32)
    for part in parts[1:]:
        total = total + part.astype(f32)
    return total.astype(bf16)


class Flow:
    def __init__(self):
        self.ready = {}
        self.steps = {}
        self.done = {}

    def start(self, name, steps):
        self.steps[name] = steps
        self.ready[name] = next(steps)

    def slot(self, names, others):
        names = [n for n in names if n in self.steps]
        tied, others = lax.optimization_barrier(([self.ready[n] for n in names], others))
        for name, value in zip(names, tied):
            self.move(name, value)
        return others

    def move(self, name, value):
        try:
            self.ready[name] = self.steps[name].send(value)
        except StopIteration as end:
            self.done[name] = end.value
            del self.steps[name], self.ready[name]

    def finish(self, names):
        for name in names:
            while name in self.steps:
                self.move(name, self.ready[name])


def fetch_halves(weight, axis):
    count = weight.shape[axis] // 2
    part = yield lax.dynamic_slice_in_dim(weight, bit_of("ctx", 0) * count, count, axis)
    part = yield swap(part, "heads", 0)
    return [part, swap(part, "ctx", 0)]


def fetch_quarters(weight, across):
    count = weight.shape[0] // 4
    place = 2 * bit_of("ctx", 0) + bit_of(*across)
    part = yield lax.dynamic_slice_in_dim(weight, place * count, count, 0)
    part = yield swap(part, "heads", 0)
    part, second = yield part, swap(part, *across)
    return [part, second, swap(part, "ctx", 0), swap(second, "ctx", 0)]


def fetch_order():
    core = bit_of("ctx", 0)
    order = [core, 1 - core]
    for across in (bit_of("ctx", 1), bit_of("batch", 0)):
        order += [
            2 * core + across,
            2 * core + 1 - across,
            2 - 2 * core + across,
            3 - 2 * core - across,
        ]
    return jnp.stack(order).astype(jnp.int32)


def reduce_sums(send, keep, ways):
    send = yield send
    got = swap(send, "ctx", 0)
    return (yield from reduce_rest(add_low(keep[0], got[0]), add_low(keep[1], got[1]), ways))


def reduce_rest(left, oth, ways):
    left, oth = yield left, oth
    rights = [swap(oth, "heads", 0)]
    stages = [("ctx", b, 1) for b in range(1, bits_of("ctx"))]
    count = bits_of("batch")
    stages += [("batch", b, min(ways, count - b)) for b in range(0, count, ways)]
    for axis, low_bit, bits in stages:
        ways = 1 << bits
        place = (lax.axis_index(axis) >> low_bit) & (ways - 1)
        count = left.shape[0] // ways
        cut = lambda at: add_low(
            *[lax.dynamic_slice_in_dim(a, at * count, count, 0) for a in (left, *rights)]
        )
        sends = [cut(place ^ flip) for flip in range(1, ways)]
        left, sends = yield (cut(place), sends)
        rights = [cross_to(s, axis, (i + 1) << low_bit) for i, s in enumerate(sends)]
    whole = add_low(left, *rights)
    for axis, low_bit, bits in reversed(stages):
        whole = yield whole
        parts = [whole] + [cross_to(whole, axis, flip << low_bit) for flip in range(1, 1 << bits)]
        for b in range(bits):
            bit = bit_of(axis, low_bit + b)
            parts = [ordered(bit, parts[i], parts[i + 1]) for i in range(0, len(parts), 2)]
        whole = parts[0]
    whole = yield whole
    return whole, swap(whole, "ctx", 0)


def send_once(value, axis, bit):
    value = yield value
    return swap(value, axis, bit)


def reduce_gains(value):
    for axis in ("ctx", "heads", "batch"):
        for bit in range(bits_of(axis)):
            value = yield value
            value = value + swap(value, axis, bit)
    return value


def scan_runs(total, boundary, rows, backward):
    place, side = lax.axis_index("ctx"), lax.axis_index("heads")
    second = lambda spot, half: (2 * spot + half) * rows >= boundary
    end = 0 if backward else 1
    low = yield total.astype(bf16)
    got = jnp.flip(swap(low, "heads", 0).astype(f32), 0)
    mine = second(place, side)
    joins = second(place, 0) == second(place, 1)
    received = jnp.where(jnp.logical_and(side == end, joins), got, 0.0)
    near = jnp.where(side == end, total, got)
    far = jnp.where(side == end, got, total)
    low = yield (near + jnp.where(joins, far, 0.0)).astype(bf16)
    for flip in range(1, lax.axis_size("ctx")):
        got = cross_to(low, "ctx", flip).astype(f32)
        spot = place ^ flip
        ahead = spot > place if backward else spot < place
        takes = jnp.logical_and(ahead, second(spot, end) == mine)
        received = received + jnp.where(takes, got, 0.0)
    return received


def extended(maps):
    heads, size, _ = maps.shape
    both = jnp.concatenate([maps, -maps], axis=2).reshape(heads // 2, 2, size, 2 * size)
    empty = jnp.zeros_like(both[:, 0])
    return jnp.concatenate(
        [
            jnp.concatenate([both[:, 0], empty], axis=2),
            jnp.concatenate([empty, both[:, 1]], axis=2),
        ],
        axis=1,
    )


def shards(tokens, lengths, gain_one, w_qkv, f_query, f_key, w_out, gain_two, w_up, w_down, d_out):
    rows, width = tokens.shape
    heads, size, _ = f_query.shape
    pairs = heads // 2
    wide = heads * size
    units = w_up.shape[1]
    assert size == 64 and lax.axis_size("heads") == 2 and 1536 % rows == 0
    boundary = lengths[0, 0]
    place = bit_of("ctx", 0)
    order = fetch_order()
    gain_one_row = gain_one.reshape(1, width)
    gain_two_row = gain_two.reshape(1, width)

    low_rows, low_cols = half_blocks(256)
    ones = (low_rows == low_cols).astype(bf16)
    cross_rows, cross_cols = half_blocks(128)
    cross = (cross_rows != cross_cols).astype(bf16)

    flow = Flow()
    slot = flow.slot
    qkv_own = jnp.transpose(w_qkv, (1, 0, 2))
    flow.start("maps", send_once(jnp.stack([f_query, f_key]), "heads", 0))
    flow.start("qkv", fetch_halves(qkv_own, 1))
    flow.start("up", fetch_quarters(w_up, ("ctx", 1)))
    flow.start("down", fetch_quarters(jnp.concatenate([w_down, w_out], axis=0), ("batch", 0)))
    (tokens,) = slot(["maps", "qkv"], (tokens,))
    turn = lambda a: jnp.swapaxes(a, 1, 2)

    h_one, turned_h = norm_one(tokens, gain_one_row)
    maps_oth = flow.done["maps"]
    fq, fk = [extended(f_query)], [extended(f_key)]
    keys = [key_pass(h_one, [qkv_own], order, turn(fk[0]))]
    (keys[0][1], order, maps_oth, ones, cross) = slot(
        ["qkv", "up", "down"], (keys[0][1], order, maps_oth, ones, cross)
    )
    qkv_oth = flow.done["qkv"]
    fq.append(extended(maps_oth[0]))
    fk.append(extended(maps_oth[1]))
    keys.append(key_pass(h_one, qkv_oth, order, turn(fk[1])))
    flow.start("scan", scan_runs(jnp.stack([keys[0][6], keys[1][6]]), boundary, rows, False))
    (keys[1][1], order, fq[1]) = slot(["scan", "up"], (keys[1][1], order, fq[1]))
    queries = []
    for at, weights in enumerate(([qkv_own], qkv_oth)):
        queries.append(
            query_pass(
                h_one, weights, order, keys[at][4], keys[at][1], keys[at][5], turn(fq[at])
            )
        )
        if at == 0:
            (queries[0][0], order) = slot(["scan", "up", "down"], (queries[0][0], order))
    (queries[1][0], order) = slot(["down"], (queries[1][0], order))
    ups, downs, incoming = (flow.done[n] for n in ("up", "down", "scan"))
    q, phi_q, turned_pq, numer = zip(*queries)
    k, v, turned_v, phi_k, turned_pk, prefix, _ = zip(*keys)

    (
        act,
        grad_pre,
        mixed,
        grad_resid,
        gn,
        gd,
        turned_two,
        turned_a,
        turned_n,
        turned_gd,
        grad_totals,
        gain_two_part,
    ) = middle_pass(
        order,
        tokens,
        d_out,
        numer,
        phi_q,
        incoming,
        gain_two_row,
        cross,
        (w_out, w_up, w_down),
        ups,
        downs,
        256,
        512,
    )
    flow.start("later", scan_runs(grad_totals, boundary, rows, True))
    near = place.reshape(1)
    near, away = place.reshape(1), (1 - place).reshape(1)
    side_at = lax.axis_index("heads").reshape(1).astype(jnp.int32)
    (away, act) = slot(["later"], (away, act))
    send = down_pass(away, act, d_out, turned_a, grad_resid)
    flow.start("down_core", send_once(send, "ctx", 0))
    (side_at,) = slot(["later", "down_core"], (side_at,))
    up_sum = up_pass(side_at, turned_two, grad_pre)
    got, later = flow.done["down_core"], flow.done["later"]
    (near, up_sum, got, later) = slot([], (near, up_sum, got, later))
    up_sum = lax.psum_scatter(
        up_sum.reshape(-1, units), ("heads", "batch", "ctx"), scatter_dimension=0, tiled=True
    )
    keep = down_pass(near, act, d_out, turned_a, grad_resid, (got,))
    flow.start("down", reduce_rest(*keep, 1))
    (near, ones) = slot(["down"], (near, ones))

    grads, maps, sends, keeps = [[], []], [[], []], [], []
    plan = [[], [], ["down"], ["qkv0", "down"], ["qkv0", "down"], ["qkv0", "down", "qkv1"]]
    for at in range(pairs):
        for side in (1, 0):
            grad, send, keep, map_part = back_pass(
                side,
                at,
                near,
                [a[side] for a in (q, k, v, turned_v, phi_q, turned_pq, phi_k, turned_pk)],
                [gn, gd, turned_n, turned_gd],
                prefix[side],
                incoming,
                later,
                fq[side],
                fk[side],
                ones,
                turned_h,
                maps[side] if at == pairs - 1 else [],
            )
            grads[side].append(grad)
            maps[side].append(map_part)
            sends.append(send)
            keeps.append(keep)
            if side == 0 and at == pairs - 2:
                pair_up = lambda a: jnp.stack([jnp.concatenate(a[1::2]), jnp.concatenate(a[0::2])])
                flow.start("qkv0", reduce_sums(pair_up(sends), pair_up(keeps), 2))
                sends, keeps = [], []
            if side == 0 and at == pairs - 1:
                flow.start("qkv1", reduce_sums(pair_up(sends), pair_up(keeps), 2))
            (grads[side][at], near) = slot(plan[2 * at + 1 - side], (grads[side][at], near))
    order = order + 0 * near[0]
    grad_tokens, gain_one_part = tokens_pass(
        order, tokens, grad_resid, gain_one_row, qkv_own, qkv_oth, grads[0] + grads[1], 512
    )
    flow.start("gains", reduce_gains(jnp.concatenate([gain_one_part, gain_two_part], axis=0)))
    (near, grad_tokens, up_sum) = slot(
        ["qkv1", "qkv0", "down", "gains"], (near, grad_tokens, up_sum)
    )
    up_sum = lax.all_gather(up_sum, ("batch", "ctx"), axis=0, tiled=True)
    slot(["qkv1", "qkv0", "down", "gains"], ())
    slot(["qkv1", "gains"], ())
    slot(["qkv1", "qkv0", "gains"], ())
    slot(["qkv1", "down", "qkv0", "gains"], ())
    while flow.steps:
        slot(list(flow.steps), ())
    gains = flow.done["gains"]
    grad_up = up_sum.astype(f32)
    join = lambda mine, theirs: ordered(place, mine, theirs)
    mine, theirs = flow.done["down"]
    grad_down = join(mine[: units // 2], theirs[: units // 2]).astype(f32)
    grad_out = join(mine[units // 2 :], theirs[units // 2 :]).astype(f32)
    part = width // 2
    parts = []
    for name, count in (("qkv0", pairs - 1), ("qkv1", 1)):
        mine, theirs = flow.done[name]
        for at in range(count):
            run = slice(part * at, part * at + part)
            parts.append(join(mine[run], theirs[run]).reshape(width, 3, 128))
    grad_qkv = jnp.concatenate(parts, axis=2).astype(f32)
    maps_sum = join(mine[part : part + 64], theirs[part : part + 64]).astype(f32)
    maps_sum = maps_sum.reshape(2, 64, pairs, 2, 64).transpose(3, 2, 0, 1, 4)
    grad_maps = maps_sum.reshape(2, heads, size, size)
    return (
        mixed,
        grad_tokens,
        gains[0],
        grad_qkv,
        grad_maps[0],
        grad_maps[1],
        grad_out,
        gains[1],
        grad_up,
        grad_down,
    )


def solution(mesh):
    in_specs = (
        P(("batch", "ctx", "heads"), None),
        P("batch", None),
        P(),
        P(None, None, "heads"),
        P("heads", None, None),
        P("heads", None, None),
        P("heads", None),
        P(),
        P(None, "heads"),
        P("heads", None),
        P(("batch", "ctx", "heads"), None),
    )
    out_specs = (
        P(("batch", "ctx", "heads"), None),
        P(("batch", "ctx", "heads"), None),
        P(),
        P(None, None, "heads"),
        P("heads", None, None),
        P("heads", None, None),
        P("heads", None),
        P(),
        P(None, "heads"),
        P("heads", None),
    )
    return jax.shard_map(shards, mesh=mesh, in_specs=in_specs, out_specs=out_specs, check_vma=False)
```

time: 610 us -> 442 us (0.72)
  waiting for transfers between devices: 153 us -> 61.4 us
  other arithmetic: 76.6 us -> 37.3 us
  Pallas kernels: 257 us -> 234 us
  local copies, waits for them, and re-layouts: 46.5 us -> 27.2 us
  between operations: 2.45 us -> 15.8 us
  starting transfers between devices: 63.9 us -> 57.3 us
    ppermute x76 -> x55, waiting for transfers between devices: 153 us -> 61.3 us  [cross_to(): return lax.ppermute(value, axis, [(i, i ^ flip) for i in range(count)])]
    select_n x35 -> x14, other arithmetic: 38.5 us -> 3.07 us  [ordered(): jnp.where(bit == 0, jnp.concatenate([mine, theirs], axis), jnp.concatenat...]
    pallas_call x19 -> x15, Pallas kernels: 194 us -> 174 us  [the longest x6 61 us: back_pass(): pl.pallas_call(functools.partial(back_kernel, pairs, side, at, more), gri...]
    concatenate x17 -> x0, local copies, waits for them, and re-layouts: 11 us -> none  [the longest x15 11 us: ordered(): jnp.concatenate([mine, theirs], 0)]
    reduce_sum x2 -> x0, other arithmetic: 9.27 us -> none  [the longest x1 6.49 us: shards(): jnp.sum(grad_qkv * w_qkv.astype(f32), axis=(1, 2))]
    ppermute x76 -> x55, starting transfers between devices: 63.9 us -> 57.2 us  [cross_to(): return lax.ppermute(value, axis, [(i, i ^ flip) for i in range(count)])]
    unnamed x76 -> x65, local copies, waits for them, and re-layouts: 14 us -> 7.38 us
    convert_element_type x46 -> x22, other arithmetic: 15.8 us -> 19.9 us  [the longest x12 7.7 us: add_low(): return total.astype(bf16)]
  transfers between devices with their start and end apart: 76 -> 57, of which waited for: 24 -> 18; matrix products, arithmetic and copies ran while one was open for 18% -> 12% of each run, Pallas kernels for 32% -> 40%
where the time goes in v2:
time: 442 us; the launch traced here: 433 us
  Pallas kernels  234 us (53%)
  waiting for transfers between devices  61.4 us (14%)
  starting transfers between devices  57.3 us (13%)
  other arithmetic  37.3 us (8%)
  local copies, waits for them, and re-layouts  27.2 us (6%)
  between operations  15.8 us (4%)
    ppermute x55, waiting for transfers between devices, cross_to(): return lax.ppermute(value, axis, [(i, i ^ flip) for i in range(count)])  61.3 us
    pallas_call x6, Pallas kernels, back_pass(): pl.pallas_call(functools.partial(back_kernel, pairs, side, at, more), gri...  61 us
    pallas_call x1, Pallas kernels, middle_pass(): pl.pallas_call(functools.partial(middle_kernel, pairs, tile), grid=(rows...  60.4 us
    ppermute x55, starting transfers between devices, cross_to(): return lax.ppermute(value, axis, [(i, i ^ flip) for i in range(count)])  57.2 us
    pallas_call x2, Pallas kernels, query_pass(): pl.pallas_call(functools.partial(query_kernel, pairs, len(weights)), grid...  30.9 us
    pallas_call x2, Pallas kernels, down_pass(): pl.pallas_call(kernel, grid_spec=pltpu.PrefetchScalarGridSpec(num_scalar_...  30.1 us
    pallas_call x2, Pallas kernels, key_pass(): pl.pallas_call(functools.partial(keys_kernel, pairs, len(weights)), grid=...  20.7 us
    pallas_call x1, Pallas kernels, tokens_pass(): pl.pallas_call(functools.partial(tokens_kernel, pairs, count), grid=(rows...  14.2 us
  transfers between devices with their start and end apart: 57, of which 18 were waited for; matrix products, arithmetic and copies ran while one was open for 12% of the time, Pallas kernels for 40%

profile of v2, /device:TPU:0, one launch (start us, length us, event | category | flops | bytes accessed | tf_op | source)
XLA Modules:
  0.0 433.1 jit_solution(9500653265797277615)
XLA Ops:
  7.3 2.2 dynamic-slice_bitcast_fusion
  10.2 2.9 collective-permute-start
  16.0 5.3 %norm_one.1 = (bf16[1536,768]{1,0:T(8,128)(2,1)}, bf16[768,1536]{1,0:T(8,128)(2,1)}) custom-call(bf16[1536,768]{1,0:T(8,128)(2,1)} %tokens.2, f32[1,768]{1,0:T(1,128)} %reshape.85.gain), custom_call_target="tpu_custom_call" | custom-call | flops 1000 | bytes 1000 | tf_op jit(solution)/shard_map/norm_one/pallas_call | solution.py:129
  22.0 10.4 %key_pass.2 = (bf16[384,1536]{1,0:T(8,128)(2,1)}, bf16[1536,384]{1,0:T(8,128)(2,1)}, bf16[384,1536]{1,0:T(8,128)(2,1)}, bf16[1536,768]{1,0:T(8,128)(2,1)}, bf16[...) custom-call(s32[10]{0:T(128)} %stack.79.order, ...), custom_call_target="tpu_custom_call" | custom-call | flops 1000 | bytes 1000 | tf_op jit(solution)/shard_map/key_pass/pallas_call | solution.py:208
  37.8 2.1 collective-permute-start.3
  42.7 10.3 %key_pass.3 = (bf16[384,1536]{1,0:T(8,128)(2,1)}, bf16[1536,384]{1,0:T(8,128)(2,1)}, bf16[384,1536]{1,0:T(8,128)(2,1)}, bf16[1536,768]{1,0:T(8,128)(2,1)}, bf16[...) custom-call(s32[10]{0:T(128)} %stack.79.order, ...), custom_call_target="tpu_custom_call" | custom-call | flops 1000 | bytes 1000 | tf_op jit(solution)/shard_map/key_pass/pallas_call | solution.py:208
  54.4 2.0 collective-permute-start.5
  59.6 15.3 %query_pass.2 = (bf16[384,1536]{1,0:T(8,128)(2,1)}, bf16[1536,768]{1,0:T(8,128)(2,1)}, bf16[768,1536]{1,0:T(8,128)(2,1)}, f32[1536,768]{1,0:T(8,128)}) custom-call(s32[10]{0:T(128)} %stack.79.order, bf16[1536,768]{1,0:T(8,128)(2,1)} %get-tuple-element.164.h, bf16[768,1536]{1,0:T(8,128)(2,1)} %get-tuple-element.179.turned_k_phi.refs_7_, ...), custom_call_target="tpu_custom_call" | custom-call | flops 1000 | bytes 1000 | tf_op jit(solution)/shard_map/query_pass/pallas_call | solution.py:285
  79.0 15.6 %query_pass.3 = (bf16[384,1536]{1,0:T(8,128)(2,1)}, bf16[1536,768]{1,0:T(8,128)(2,1)}, bf16[768,1536]{1,0:T(8,128)(2,1)}, f32[1536,768]{1,0:T(8,128)}) custom-call(s32[10]{0:T(128)} %stack.79.order, bf16[1536,768]{1,0:T(8,128)(2,1)} %get-tuple-element.164.h, bf16[768,1536]{1,0:T(8,128)(2,1)} %get-tuple-element.185.turned_k_phi.refs_7_, ...), custom_call_target="tpu_custom_call" | custom-call | flops 1000 | bytes 1000 | tf_op jit(solution)/shard_map/query_pass/pallas_call | solution.py:285
  96.8 2.0 collective-permute-done.8
  100.7 5.8 %collective-permute-done.9 = bf16[2,400,128]{2,1,0:T(8,128)(2,1)} collective-permute-done((bf16[2,400,128]{2,1,0:T(8,128)(2,1)}, bf16[2,400,128]{2,1,0:T(8,128)(2,1)}, u32[]{:S(2)}, u32[]{:S(2)}) %collective-permute-start.9) | collective-permute-done | bytes 204832 | tf_op jit(solution)/shard_map/ppermute | solution.py:817
  109.3 60.4 %middle_pass.1 = (bf16[3072,1536]{1,0:T(8,128)(2,1)}, bf16[4,1536,768]{2,1,0:T(8,128)(2,1)}, bf16[1536,768]{1,0:T(8,128)(2,1)}, bf16[1536,768]{1,0:T(8,128)(2,1)...) custom-call(s32[10]{0:T(128)} %stack.79.order, ...), custom_call_target="tpu_custom_call" | custom-call | flops 1000 | bytes 1000 | tf_op jit(solution)/shard_map/middle_pass/pallas_call | solution.py:508
  172.3 19.3 %down_pass.2 = bf16[2,960,768]{2,1,0:T(8,128)(2,1)} custom-call(s32[1]{0:T(128)} %bitcast.1.half, bf16[3072,1536]{1,0:T(8,128)(2,1)} %get-tuple-element.206.refs_0_, bf16[1536,768]{1,0:T(8,128)(2,1)} %refs_1_.3, bf16[768,1536]{1,0:T(8,128)(2,1)} %get-tuple-element.207.refs_2_, bf16[1536,768]{1,0:T(8,128)(2,1)} %get-tuple-element.208.refs_3_.resid), custom_call_target="tpu_custom_call" | custom-call | flops 1000 | bytes 1000 | tf_op jit(solution)/shard_map/down_pass/pallas_call | solution.py:604
  194.4 11.6 %up_pass.1 = bf16[2,768,1536]{2,1,0:T(8,128)(2,1)} custom-call(s32[1]{0:T(128)} %bitcast.33.side, bf16[768,1536]{1,0:T(8,128)(2,1)} %get-tuple-element.210.left, bf16[4,1536,768]{2,1,0:T(8,128)(2,1)} %get-tuple-element.211.right), custom_call_target="tpu_custom_call" | custom-call | flops 1000 | bytes 1000 | tf_op jit(solution)/shard_map/up_pass/pallas_call | solution.py:555
  206.0 2.0 select_add_fusion.refs_14_
  209.6 10.8 %down_pass.3 = (bf16[960,768]{1,0:T(8,128)(2,1)}, bf16[960,768]{1,0:T(8,128)(2,1)}) custom-call(s32[1]{0:T(128)} %bitcast.half.core, bf16[3072,1536]{1,0:T(8,128)(2,1)} %get-tuple-element.206.refs_0_, bf16[1536,768]{1,0:T(8,128)(2,1)} %refs_1_.3, bf16[768,1536]{1,0:T(8,128)(2,1)} %get-tuple-element.207.refs_2_, ...), custom_call_target="tpu_custom_call" | custom-call | flops 1000 | bytes 1000 | tf_op jit(solution)/shard_map/down_pass/pallas_call | solution.py:604
  220.9 10.1 %back_pass.6 = (bf16[1536,384]{1,0:T(8,128)(2,1)}, bf16[384,384]{1,0:T(8,128)(2,1)}, bf16[384,384]{1,0:T(8,128)(2,1)}, bf16[128,128]{1,0:T(8,128)(2,1)}) custom-call(s32[1]{0:T(128)} %bitcast.half.core, bf16[384,1536]{1,0:T(8,128)(2,1)} %get-tuple-element.220.refs_0_, bf16[384,1536]{1,0:T(8,128)(2,1)} %get-tuple-element.221.refs_1_, ...), custom_call_target="tpu_custom_call" | custom-call | flops 1000 | bytes 1000 | tf_op jit(solution)/shard_map/back_pass/pallas_call | solution.py:728
  231.0 10.1 %back_pass.7 = (bf16[1536,384]{1,0:T(8,128)(2,1)}, bf16[384,384]{1,0:T(8,128)(2,1)}, bf16[384,384]{1,0:T(8,128)(2,1)}, bf16[128,128]{1,0:T(8,128)(2,1)}) custom-call(s32[1]{0:T(128)} %bitcast.half.core, bf16[384,1536]{1,0:T(8,128)(2,1)} %get-tuple-element.234.refs_0_, bf16[384,1536]{1,0:T(8,128)(2,1)} %get-tuple-element.235.refs_1_, ...), custom_call_target="tpu_custom_call" | custom-call | flops 1000 | bytes 1000 | tf_op jit(solution)/shard_map/back_pass/pallas_call | solution.py:728
  241.1 10.2 %back_pass.8 = (bf16[1536,384]{1,0:T(8,128)(2,1)}, bf16[384,384]{1,0:T(8,128)(2,1)}, bf16[384,384]{1,0:T(8,128)(2,1)}, bf16[128,128]{1,0:T(8,128)(2,1)}) custom-call(s32[1]{0:T(128)} %bitcast.half.core, bf16[384,1536]{1,0:T(8,128)(2,1)} %get-tuple-element.220.refs_0_, bf16[384,1536]{1,0:T(8,128)(2,1)} %get-tuple-element.221.refs_1_, ...), custom_call_target="tpu_custom_call" | custom-call | flops 1000 | bytes 1000 | tf_op jit(solution)/shard_map/back_pass/pallas_call | solution.py:728
  251.4 4.4 %collective-permute-done.20 = bf16[960,768]{1,0:T(8,128)(2,1)} collective-permute-done((bf16[960,768]{1,0:T(8,128)(2,1)}, bf16[960,768]{1,0:T(8,128)(2,1)}, u32[]{:S(2)}, u32[]{:S(2)}) %collective-permute-start.20) | collective-permute-done | bytes 1474592 | tf_op jit(solution)/shard_map/ppermute | solution.py:817
  255.7 3.0 add_convert_fusion
  258.9 10.2 %back_pass.9 = (bf16[1536,384]{1,0:T(8,128)(2,1)}, bf16[384,384]{1,0:T(8,128)(2,1)}, bf16[384,384]{1,0:T(8,128)(2,1)}, bf16[128,128]{1,0:T(8,128)(2,1)}) custom-call(s32[1]{0:T(128)} %bitcast.half.core, bf16[384,1536]{1,0:T(8,128)(2,1)} %get-tuple-element.234.refs_0_, bf16[384,1536]{1,0:T(8,128)(2,1)} %get-tuple-element.235.refs_1_, ...), custom_call_target="tpu_custom_call" | custom-call | flops 1000 | bytes 1000 | tf_op jit(solution)/shard_map/back_pass/pallas_call | solution.py:728
  270.3 12.4 %collective-permute-done.21 = bf16[480,768]{1,0:T(8,128)(2,1)S(1)} collective-permute-done((bf16[480,768]{1,0:T(8,128)(2,1)}, bf16[480,768]{1,0:T(8,128)(2,1)S(1)}, u32[]{:S(2)}, u32[]{:S(2)}) %collective-permute-start.21) | collective-permute-done | bytes 737312 | tf_op jit(solution)/shard_map/ppermute | solution.py:817
  285.2 10.2 %back_pass.10 = (bf16[1536,384]{1,0:T(8,128)(2,1)}, bf16[512,384]{1,0:T(8,128)(2,1)}, bf16[512,384]{1,0:T(8,128)(2,1)}, bf16[128,128]{1,0:T(8,128)(2,1)}) custom-call(s32[1]{0:T(128)} %bitcast.half.core, bf16[384,1536]{1,0:T(8,128)(2,1)} %get-tuple-element.220.refs_0_, bf16[384,1536]{1,0:T(8,128)(2,1)} %get-tuple-element.221.refs_1_, ...), custom_call_target="tpu_custom_call" | custom-call | flops 1000 | bytes 1000 | tf_op jit(solution)/shard_map/back_pass/pallas_call | solution.py:728
  295.4 3.0 collective-permute-done.23
  302.2 2.6 collective-permute-start.25
  304.8 10.2 %back_pass.11 = (bf16[1536,384]{1,0:T(8,128)(2,1)}, bf16[512,384]{1,0:T(8,128)(2,1)}, bf16[512,384]{1,0:T(8,128)(2,1)}, bf16[128,128]{1,0:T(8,128)(2,1)}) custom-call(s32[1]{0:T(128)} %bitcast.half.core, bf16[384,1536]{1,0:T(8,128)(2,1)} %get-tuple-element.234.refs_0_, bf16[384,1536]{1,0:T(8,128)(2,1)} %get-tuple-element.235.refs_1_, ...), custom_call_target="tpu_custom_call" | custom-call | flops 1000 | bytes 1000 | tf_op jit(solution)/shard_map/back_pass/pallas_call | solution.py:728
  317.1 2.3 collective-permute-start.28
  319.4 14.2 %tokens_pass.1 = (bf16[1536,768]{1,0:T(8,128)(2,1)}, f32[1,768]{1,0:T(1,128)}) custom-call(s32[10]{0:T(128)} %stack.79.order, bf16[1536,768]{1,0:T(8,128)(2,1)} %tokens.2, bf16[1536,768]{1,0:T(8,128)(2,1)} %get-tuple-element.208.refs_3_.resid, f32[1,768]{1,0:T(1,128)} %reshape.85.gain, bf16[3,768,384]{2,1,0:T(8,128)(2,1)} %bitcast.93, ...), custom_call_target="tpu_custom_call" | custom-call | flops 1000 | bytes 1000 | tf_op jit(solution)/shard_map/tokens_pass/pallas_call | solution.py:794
  335.0 2.8 collective-permute-start.33
  338.1 4.0 collective-permute-start.32
  344.8 6.6 %collective-permute-done.30 = bf16[96,384]{1,0:T(8,128)(2,1)S(1)} collective-permute-done((bf16[96,384]{1,0:T(8,128)(2,1)S(1)}, bf16[96,384]{1,0:T(8,128)(2,1)S(1)}, u32[]{:S(2)}, u32[]{:S(2)}) %collective-permute-start.30) | collective-permute-done | bytes 73760 | tf_op jit(solution)/shard_map/ppermute | solution.py:817
  352.6 2.0 collective-permute-done.29
  354.8 2.1 collective-permute-start.36
  356.8 2.6 collective-permute-start.41
  361.2 2.0 collective-permute-start.47
  363.2 2.6 collective-permute-done.41
  365.9 3.1 collective-permute-done.35
  370.6 2.6 collective-permute-start.38
  379.2 2.1 collective-permute-start.44
  383.1 2.5 collective-permute-start.46
  387.1 2.6 collective-permute-done.46
  389.8 4.8 %collective-permute-done.48 = bf16[384,384]{1,0:T(8,128)(2,1)S(1)} collective-permute-done((bf16[384,384]{1,0:T(8,128)(2,1)S(1)}, bf16[384,384]{1,0:T(8,128)(2,1)S(1)}, u32[]{:S(2)}, u32[]{:S(2)}) %collective-permute-start.48) | collective-permute-done | bytes 294944 | tf_op jit(solution)/shard_map/ppermute | solution.py:817
  396.8 5.4 %collective-permute-done.52 = bf16[256,384]{1,0:T(8,128)(2,1)S(1)} collective-permute-done((bf16[256,384]{1,0:T(8,128)(2,1)S(1)}, bf16[256,384]{1,0:T(8,128)(2,1)S(1)}, u32[]{:S(2)}, u32[]{:S(2)}) %collective-permute-start.52) | collective-permute-done | bytes 196640 | tf_op jit(solution)/shard_map/ppermute | solution.py:817
  403.1 2.4 slice.124
  412.0 2.9 copy.59
  418.6 2.7 fusion
  421.3 4.5 %convert_element_type.408 = f32[768,1536]{1,0:T(8,128)} convert(bf16[768,1536]{1,0:T(8,128)(2,1)} %all-gather.2.cloned.1.call-done) | non-fusion elementwise | flops 1179648 | bytes 7077888 | tf_op jit(solution)/shard_map/convert_element_type | solution.py:1134
  (251 shorter events, 76.0 us)
Async XLA Ops:
  7.2 327.7 %reduce-scatter.2.cloned.1.call-start = ((), (), s32[]{:S(2)}) async-start(), calls=%async_computation.1 | async-start | bytes 4866048 | tf_op jit(solution)/shard_map/reduce_scatter | solution.py:1081
  10.2 27.5 %collective-permute-start = (bf16[3,384,384]{2,1,0:T(8,128)(2,1)}, bf16[3,384,384]{2,1,0:T(8,128)(2,1)S(1)}, u32[]{:S(2)}, u32[]{:S(2)}) collective-permute-start(bf16[3,384,384]{2,1,0:T(8,128)(2,1)} %dynamic-slice_bitcast_fusion), channel_id=1, source_target_pairs={{0,1},{1,0},{2,3},{3,2},{4,5},{5,4},{6,7},{7,6},{8,9},{9,8},{10,11... | collective-permute-start | bytes 2654216 | tf_op jit(solution)/shard_map/ppermute | solution.py:817
  13.1 24.5 %collective-permute-start.1 = (bf16[2,6,64,64]{3,2,1,0:T(8,128)(2,1)}, bf16[2,6,64,64]{3,2,1,0:T(8,128)(2,1)S(1)}, u32[]{:S(2)}, u32[]{:S(2)}) collective-permute-start(bf16[2,6,64,64]{3,2,1,0:T(8,128)(2,1)} %pad_maximum_fusion.3), channel_id=1, source_target_pairs={{0,1},{1,0},{2,3},{3,2},{4,5},{5,4},{6,7},{7,6},{8,9},{9,8},{10,11... | collective-permute-start | bytes 294920 | tf_op jit(solution)/shard_map/ppermute | solution.py:817
  37.8 16.6 %collective-permute-start.3 = (bf16[192,1536]{1,0:T(8,128)(2,1)}, bf16[192,1536]{1,0:T(8,128)(2,1)}, u32[]{:S(2)}, u32[]{:S(2)}) collective-permute-start(bf16[192,1536]{1,0:T(8,128)(2,1)} %constant_dynamic-slice_fusion), channel_id=1, source_target_pairs={{0,1},{1,0},{2,3},{3,2},{4,5},{5,4},{6,7},{7,6},{8,9},{9,8},{10,11... | collective-permute-start | bytes 1769480 | tf_op jit(solution)/shard_map/ppermute | solution.py:817
  39.9 35.9 %collective-permute-start.6 = (bf16[480,768]{1,0:T(8,128)(2,1)}, bf16[480,768]{1,0:T(8,128)(2,1)S(1)}, u32[]{:S(2)}, u32[]{:S(2)}) collective-permute-start(bf16[480,768]{1,0:T(8,128)(2,1)} %fusion.5), channel_id=1, source_target_pairs={{0,1},{1,0},{2,3},{3,2},{4,5},{5,4},{6,7},{7,6},{8,9},{9,8},{10,11... | collective-permute-start | bytes 2211848 | tf_op jit(solution)/shard_map/ppermute | solution.py:817
  54.4 21.4 %collective-permute-start.5 = (bf16[192,1536]{1,0:T(8,128)(2,1)}, bf16[192,1536]{1,0:T(8,128)(2,1)S(1)}, u32[]{:S(2)}, u32[]{:S(2)}) collective-permute-start(bf16[192,1536]{1,0:T(8,128)(2,1)} %collective-permute-done.3.up_0), channel_id=1, source_target_pairs={{0,4},{2,6},{4,0},{6,2},{1,5},{3,7},{5,1},{7,3},{8,12},{10,14},{12... | collective-permute-start | bytes 1769480 | tf_op jit(solution)/shard_map/ppermute | solution.py:817
  56.4 18.5 %collective-permute-start.4 = (bf16[2,400,128]{2,1,0:T(8,128)(2,1)S(1)}, bf16[2,400,128]{2,1,0:T(8,128)(2,1)S(1)}, u32[]{:S(2)}, u32[]{:S(2)}) collective-permute-start(bf16[2,400,128]{2,1,0:T(8,128)(2,1)S(1)} %fusion.15), channel_id=1, source_target_pairs={{0,1},{1,0},{2,3},{3,2},{4,5},{5,4},{6,7},{7,6},{8,9},{9,8},{10,11... | collective-permute-start | bytes 614408 | tf_op jit(solution)/shard_map/ppermute | solution.py:817
  76.6 18.0 %collective-permute-start.7 = (bf16[480,768]{1,0:T(8,128)(2,1)S(1)}, bf16[480,768]{1,0:T(8,128)(2,1)S(1)}, u32[]{:S(2)}, u32[]{:S(2)}) collective-permute-start(bf16[480,768]{1,0:T(8,128)(2,1)S(1)} %collective-permute-done.6.down_0), channel_id=1, source_target_pairs={{0,8},{8,0},{16,24},{24,16},{1,9},{9,1},{17,25},{25,17},{2,10},{10... | collective-permute-start | bytes 2211848 | tf_op jit(solution)/shard_map/ppermute | solution.py:817
  78.2 18.2 %collective-permute-start.10 = (bf16[2,400,128]{2,1,0:T(8,128)(2,1)}, bf16[2,400,128]{2,1,0:T(8,128)(2,1)S(1)}, u32[]{:S(2)}, u32[]{:S(2)}) collective-permute-start(bf16[2,400,128]{2,1,0:T(8,128)(2,1)} %add_convert_fusion.7), channel_id=1, source_target_pairs={{0,6},{2,4},{4,2},{6,0},{1,7},{3,5},{5,3},{7,1},{8,14},{10,12},{12... | collective-permute-start | bytes 614408 | tf_op jit(solution)/shard_map/ppermute | solution.py:817
  94.7 13.8 %collective-permute-start.13 = (bf16[480,768]{1,0:T(8,128)(2,1)S(1)}, bf16[480,768]{1,0:T(8,128)(2,1)}, u32[]{:S(2)}, u32[]{:S(2)}) collective-permute-start(bf16[480,768]{1,0:T(8,128)(2,1)S(1)} %collective-permute-done.6.down_0), channel_id=1, source_target_pairs={{0,2},{2,0},{4,6},{6,4},{1,3},{3,1},{5,7},{7,5},{8,10},{10,8},{12,... | collective-permute-start | bytes 2211848 | tf_op jit(solution)/shard_map/ppermute | solution.py:817
  95.8 12.7 %collective-permute-start.14 = (bf16[480,768]{1,0:T(8,128)(2,1)S(1)}, bf16[480,768]{1,0:T(8,128)(2,1)}, u32[]{:S(2)}, u32[]{:S(2)}) collective-permute-start(bf16[480,768]{1,0:T(8,128)(2,1)S(1)} %collective-permute-done.7.down_1), channel_id=1, source_target_pairs={{0,2},{2,0},{4,6},{6,4},{1,3},{3,1},{5,7},{7,5},{8,10},{10,8},{12,... | collective-permute-start | bytes 2211848 | tf_op jit(solution)/shard_map/ppermute | solution.py:817
  96.3 12.2 %collective-permute-start.11 = (bf16[192,1536]{1,0:T(8,128)(2,1)}, bf16[192,1536]{1,0:T(8,128)(2,1)S(1)}, u32[]{:S(2)}, u32[]{:S(2)}) collective-permute-start(bf16[192,1536]{1,0:T(8,128)(2,1)} %collective-permute-done.3.up_0), channel_id=1, source_target_pairs={{0,2},{2,0},{4,6},{6,4},{1,3},{3,1},{5,7},{7,5},{8,10},{10,8},{12,... | collective-permute-start | bytes 1769480 | tf_op jit(solution)/shard_map/ppermute | solution.py:817
  96.4 12.1 %collective-permute-start.12 = (bf16[192,1536]{1,0:T(8,128)(2,1)S(1)}, bf16[192,1536]{1,0:T(8,128)(2,1)}, u32[]{:S(2)}, u32[]{:S(2)}) collective-permute-start(bf16[192,1536]{1,0:T(8,128)(2,1)S(1)} %copy-done.18), channel_id=1, source_target_pairs={{0,2},{2,0},{4,6},{6,4},{1,3},{3,1},{5,7},{7,5},{8,10},{10,8},{12,... | collective-permute-start | bytes 1769480 | tf_op jit(solution)/shard_map/ppermute | solution.py:817
  98.9 7.7 %collective-permute-start.9 = (bf16[2,400,128]{2,1,0:T(8,128)(2,1)}, bf16[2,400,128]{2,1,0:T(8,128)(2,1)}, u32[]{:S(2)}, u32[]{:S(2)}) collective-permute-start(bf16[2,400,128]{2,1,0:T(8,128)(2,1)} %add_convert_fusion.7), channel_id=1, source_target_pairs={{0,4},{2,6},{4,0},{6,2},{1,5},{3,7},{5,1},{7,3},{8,12},{10,14},{12... | collective-permute-start | bytes 614408 | tf_op jit(solution)/shard_map/ppermute | solution.py:817
  170.7 20.9 %collective-permute-start.15 = (bf16[2,400,128]{2,1,0:T(8,128)(2,1)S(1)}, bf16[2,400,128]{2,1,0:T(8,128)(2,1)S(1)}, u32[]{:S(2)}, u32[]{:S(2)}) collective-permute-start(bf16[2,400,128]{2,1,0:T(8,128)(2,1)S(1)} %convert_element_type.316), channel_id=1, source_target_pairs={{0,1},{1,0},{2,3},{3,2},{4,5},{5,4},{6,7},{7,6},{8,9},{9,8},{10,11... | collective-permute-start | bytes 614408 | tf_op jit(solution)/shard_map/ppermute | solution.py:817
  192.4 15.6 %collective-permute-start.16 = (bf16[2,960,768]{2,1,0:T(8,128)(2,1)}, bf16[2,960,768]{2,1,0:T(8,128)(2,1)S(1)}, u32[]{:S(2)}, u32[]{:S(2)}) collective-permute-start(bf16[2,960,768]{2,1,0:T(8,128)(2,1)} %down_pass.2), channel_id=1, source_target_pairs={{0,2},{2,0},{4,6},{6,4},{1,3},{3,1},{5,7},{7,5},{8,10},{10,8},{12,... | collective-permute-start | bytes 8847368 | tf_op jit(solution)/shard_map/ppermute | solution.py:817
  192.4 13.6 %collective-permute-start.17 = (bf16[2,400,128]{2,1,0:T(8,128)(2,1)}, bf16[2,400,128]{2,1,0:T(8,128)(2,1)}, u32[]{:S(2)}, u32[]{:S(2)}) collective-permute-start(bf16[2,400,128]{2,1,0:T(8,128)(2,1)} %add_convert_fusion.6), channel_id=1, source_target_pairs={{0,2},{2,0},{4,6},{6,4},{1,3},{3,1},{5,7},{7,5},{8,10},{10,8},{12,... | collective-permute-start | bytes 614408 | tf_op jit(solution)/shard_map/ppermute | solution.py:817
  192.9 13.1 %collective-permute-start.18 = (bf16[2,400,128]{2,1,0:T(8,128)(2,1)}, bf16[2,400,128]{2,1,0:T(8,128)(2,1)}, u32[]{:S(2)}, u32[]{:S(2)}) collective-permute-start(bf16[2,400,128]{2,1,0:T(8,128)(2,1)} %add_convert_fusion.6), channel_id=1, source_target_pairs={{0,4},{2,6},{4,0},{6,2},{1,5},{3,7},{5,1},{7,3},{8,12},{10,14},{12... | collective-permute-start | bytes 614408 | tf_op jit(solution)/shard_map/ppermute | solution.py:817
  193.4 12.6 %collective-permute-start.19 = (bf16[2,400,128]{2,1,0:T(8,128)(2,1)}, bf16[2,400,128]{2,1,0:T(8,128)(2,1)}, u32[]{:S(2)}, u32[]{:S(2)}) collective-permute-start(bf16[2,400,128]{2,1,0:T(8,128)(2,1)} %add_convert_fusion.6), channel_id=1, source_target_pairs={{0,6},{2,4},{4,2},{6,0},{1,7},{3,5},{5,3},{7,1},{8,14},{10,12},{12... | collective-permute-start | bytes 614408 | tf_op jit(solution)/shard_map/ppermute | solution.py:817
  209.6 211.7 %all-gather.2.cloned.1.call-start = ((), (), s32[]{:S(2)}) async-start(), calls=%async_computation.2 | async-start | bytes 2506752 | tf_op jit(solution)/shard_map/all_gather | solution.py:1126
  220.4 35.3 %collective-permute-start.20 = (bf16[960,768]{1,0:T(8,128)(2,1)}, bf16[960,768]{1,0:T(8,128)(2,1)}, u32[]{:S(2)}, u32[]{:S(2)}) collective-permute-start(bf16[960,768]{1,0:T(8,128)(2,1)} %get-tuple-element.241), channel_id=1, source_target_pairs={{0,1},{1,0},{2,3},{3,2},{4,5},{5,4},{6,7},{7,6},{8,9},{9,8},{10,11... | collective-permute-start | bytes 4423688 | tf_op jit(solution)/shard_map/ppermute | solution.py:817
  258.8 24.0 %collective-permute-start.21 = (bf16[480,768]{1,0:T(8,128)(2,1)}, bf16[480,768]{1,0:T(8,128)(2,1)S(1)}, u32[]{:S(2)}, u32[]{:S(2)}) collective-permute-start(bf16[480,768]{1,0:T(8,128)(2,1)} %get-tuple-element.252), channel_id=1, source_target_pairs={{0,4},{2,6},{4,0},{6,2},{1,5},{3,7},{5,1},{7,3},{8,12},{10,14},{12... | collective-permute-start | bytes 2211848 | tf_op jit(solution)/shard_map/ppermute | solution.py:817
  283.7 15.5 %collective-permute-start.22 = (bf16[2,768,384]{2,1,0:T(8,128)(2,1)S(1)}, bf16[2,768,384]{2,1,0:T(8,128)(2,1)S(1)}, u32[]{:S(2)}, u32[]{:S(2)}) collective-permute-start(bf16[2,768,384]{2,1,0:T(8,128)(2,1)S(1)} %pad_maximum_fusion), channel_id=1, source_target_pairs={{0,2},{2,0},{4,6},{6,4},{1,3},{3,1},{5,7},{7,5},{8,10},{10,8},{12,... | collective-permute-start | bytes 3538952 | tf_op jit(solution)/shard_map/ppermute | solution.py:817
  283.7 14.7 %collective-permute-start.23 = (bf16[240,768]{1,0:T(8,128)(2,1)}, bf16[240,768]{1,0:T(8,128)(2,1)S(1)}, u32[]{:S(2)}, u32[]{:S(2)}) collective-permute-start(bf16[240,768]{1,0:T(8,128)(2,1)} %get-tuple-element.258), channel_id=1, source_target_pairs={{0,8},{8,0},{16,24},{24,16},{1,9},{9,1},{17,25},{25,17},{2,10},{10... | collective-permute-start | bytes 1105928 | tf_op jit(solution)/shard_map/ppermute | solution.py:817
  300.7 15.5 %collective-permute-start.24 = (bf16[768,384]{1,0:T(8,128)(2,1)S(1)}, bf16[768,384]{1,0:T(8,128)(2,1)S(1)}, u32[]{:S(2)}, u32[]{:S(2)}) collective-permute-start(bf16[768,384]{1,0:T(8,128)(2,1)S(1)} %get-tuple-element.268), channel_id=1, source_target_pairs={{0,1},{1,0},{2,3},{3,2},{4,5},{5,4},{6,7},{7,6},{8,9},{9,8},{10,11... | collective-permute-start | bytes 1769480 | tf_op jit(solution)/shard_map/ppermute | solution.py:817
  302.2 13.9 %collective-permute-start.25 = (bf16[120,768]{1,0:T(8,128)(2,1)}, bf16[120,768]{1,0:T(8,128)(2,1)S(1)}, u32[]{:S(2)}, u32[]{:S(2)}) collective-permute-start(bf16[120,768]{1,0:T(8,128)(2,1)} %get-tuple-element.270), channel_id=1, source_target_pairs={{0,16},{8,24},{16,0},{24,8},{1,17},{9,25},{17,1},{25,9},{2,18},{10... | collective-permute-start | bytes 552968 | tf_op jit(solution)/shard_map/ppermute | solution.py:817
  317.1 17.5 %collective-permute-start.26 = (bf16[2,512,384]{2,1,0:T(8,128)(2,1)S(1)}, bf16[2,512,384]{2,1,0:T(8,128)(2,1)S(1)}, u32[]{:S(2)}, u32[]{:S(2)}) collective-permute-start(bf16[2,512,384]{2,1,0:T(8,128)(2,1)S(1)} %pad_maximum_fusion.1), channel_id=1, source_target_pairs={{0,2},{2,0},{4,6},{6,4},{1,3},{3,1},{5,7},{7,5},{8,10},{10,8},{12,... | collective-permute-start | bytes 2359304 | tf_op jit(solution)/shard_map/ppermute | solution.py:817
  317.1 17.3 %collective-permute-start.28 = (bf16[120,768]{1,0:T(8,128)(2,1)S(1)}, bf16[120,768]{1,0:T(8,128)(2,1)S(1)}, u32[]{:S(2)}, u32[]{:S(2)}) collective-permute-start(bf16[120,768]{1,0:T(8,128)(2,1)S(1)} %add_convert_fusion.10), channel_id=1, source_target_pairs={{0,16},{8,24},{16,0},{24,8},{1,17},{9,25},{17,1},{25,9},{2,18},{10... | collective-permute-start | bytes 552968 | tf_op jit(solution)/shard_map/ppermute | solution.py:817
  319.4 15.1 %collective-permute-start.27 = (bf16[384,384]{1,0:T(8,128)(2,1)}, bf16[384,384]{1,0:T(8,128)(2,1)S(1)}, u32[]{:S(2)}, u32[]{:S(2)}) collective-permute-start(bf16[384,384]{1,0:T(8,128)(2,1)} %get-tuple-element.277), channel_id=1, source_target_pairs={{0,4},{2,6},{4,0},{6,2},{1,5},{3,7},{5,1},{7,3},{8,12},{10,14},{12... | collective-permute-start | bytes 884744 | tf_op jit(solution)/shard_map/ppermute | solution.py:817
  335.0 17.4 %collective-permute-start.33 = (bf16[240,768]{1,0:T(8,128)(2,1)S(1)}, bf16[240,768]{1,0:T(8,128)(2,1)S(1)}, u32[]{:S(2)}, u32[]{:S(2)}) collective-permute-start(bf16[240,768]{1,0:T(8,128)(2,1)S(1)} %maximum_select_fusion.9), channel_id=1, source_target_pairs={{0,8},{8,0},{16,24},{24,16},{1,9},{9,1},{17,25},{25,17},{2,10},{10... | collective-permute-start | bytes 1105928 | tf_op jit(solution)/shard_map/ppermute | solution.py:817
  337.7 13.7 %collective-permute-start.30 = (bf16[96,384]{1,0:T(8,128)(2,1)S(1)}, bf16[96,384]{1,0:T(8,128)(2,1)S(1)}, u32[]{:S(2)}, u32[]{:S(2)}) collective-permute-start(bf16[96,384]{1,0:T(8,128)(2,1)S(1)} %get-tuple-element.293), channel_id=1, source_target_pairs={{0,8},{8,0},{16,24},{24,16},{1,9},{9,1},{17,25},{25,17},{2,10},{10... | collective-permute-start | bytes 221192 | tf_op jit(solution)/shard_map/ppermute | solution.py:817
  337.8 13.6 %collective-permute-start.31 = (bf16[96,384]{1,0:T(8,128)(2,1)S(1)}, bf16[96,384]{1,0:T(8,128)(2,1)S(1)}, u32[]{:S(2)}, u32[]{:S(2)}) collective-permute-start(bf16[96,384]{1,0:T(8,128)(2,1)S(1)} %get-tuple-element.294), channel_id=1, source_target_pairs={{0,16},{8,24},{16,0},{24,8},{1,17},{9,25},{17,1},{25,9},{2,18},{10... | collective-permute-start | bytes 221192 | tf_op jit(solution)/shard_map/ppermute | solution.py:817
  338.1 14.2 %collective-permute-start.32 = (bf16[96,384]{1,0:T(8,128)(2,1)S(1)}, bf16[96,384]{1,0:T(8,128)(2,1)S(1)}, u32[]{:S(2)}, u32[]{:S(2)}) collective-permute-start(bf16[96,384]{1,0:T(8,128)(2,1)S(1)} %get-tuple-element.295), channel_id=1, source_target_pairs={{0,24},{8,16},{16,8},{24,0},{1,25},{9,17},{17,9},{25,1},{2,26},{10... | collective-permute-start | bytes 221192 | tf_op jit(solution)/shard_map/ppermute | solution.py:817
  343.4 11.2 %collective-permute-start.29 = (bf16[512,384]{1,0:T(8,128)(2,1)S(1)}, bf16[512,384]{1,0:T(8,128)(2,1)S(1)}, u32[]{:S(2)}, u32[]{:S(2)}) collective-permute-start(bf16[512,384]{1,0:T(8,128)(2,1)S(1)} %get-tuple-element.291), channel_id=1, source_target_pairs={{0,1},{1,0},{2,3},{3,2},{4,5},{5,4},{6,7},{7,6},{8,9},{9,8},{10,11... | collective-permute-start | bytes 1179656 | tf_op jit(solution)/shard_map/ppermute | solution.py:817
  354.7 8.5 %collective-permute-start.40 = (bf16[96,384]{1,0:T(8,128)(2,1)S(1)}, bf16[96,384]{1,0:T(8,128)(2,1)S(1)}, u32[]{:S(2)}, u32[]{:S(2)}) collective-permute-start(bf16[96,384]{1,0:T(8,128)(2,1)S(1)} %add_convert_fusion.13), channel_id=1, source_target_pairs={{0,8},{8,0},{16,24},{24,16},{1,9},{9,1},{17,25},{25,17},{2,10},{10... | collective-permute-start | bytes 221192 | tf_op jit(solution)/shard_map/ppermute | solution.py:817
  354.8 6.4 %collective-permute-start.36 = (f32[2,768]{1,0:T(2,128)S(1)}, f32[2,768]{1,0:T(2,128)S(1)}, u32[]{:S(2)}, u32[]{:S(2)}) collective-permute-start(f32[2,768]{1,0:T(2,128)S(1)} %add.325), channel_id=1, source_target_pairs={{0,4},{2,6},{4,0},{6,2},{1,5},{3,7},{5,1},{7,3},{8,12},{10,14},{12... | collective-permute-start | bytes 18440 | tf_op jit(solution)/shard_map/ppermute | solution.py:817
  356.8 9.0 %collective-permute-start.41 = (bf16[96,384]{1,0:T(8,128)(2,1)S(1)}, bf16[96,384]{1,0:T(8,128)(2,1)S(1)}, u32[]{:S(2)}, u32[]{:S(2)}) collective-permute-start(bf16[96,384]{1,0:T(8,128)(2,1)S(1)} %add_convert_fusion.13), channel_id=1, source_target_pairs={{0,16},{8,24},{16,0},{24,8},{1,17},{9,25},{17,1},{25,9},{2,18},{10... | collective-permute-start | bytes 221192 | tf_op jit(solution)/shard_map/ppermute | solution.py:817
  359.4 6.5 %collective-permute-start.42 = (bf16[96,384]{1,0:T(8,128)(2,1)S(1)}, bf16[96,384]{1,0:T(8,128)(2,1)S(1)}, u32[]{:S(2)}, u32[]{:S(2)}) collective-permute-start(bf16[96,384]{1,0:T(8,128)(2,1)S(1)} %add_convert_fusion.13), channel_id=1, source_target_pairs={{0,24},{8,16},{16,8},{24,0},{1,25},{9,17},{17,9},{25,1},{2,26},{10... | collective-permute-start | bytes 221192 | tf_op jit(solution)/shard_map/ppermute | solution.py:817
  361.1 7.8 %collective-permute-start.35 = (bf16[256,384]{1,0:T(8,128)(2,1)S(1)}, bf16[256,384]{1,0:T(8,128)(2,1)S(1)}, u32[]{:S(2)}, u32[]{:S(2)}) collective-permute-start(bf16[256,384]{1,0:T(8,128)(2,1)S(1)} %get-tuple-element.299), channel_id=1, source_target_pairs={{0,4},{2,6},{4,0},{6,2},{1,5},{3,7},{5,1},{7,3},{8,12},{10,14},{12... | collective-permute-start | bytes 589832 | tf_op jit(solution)/shard_map/ppermute | solution.py:817
  361.2 33.7 %collective-permute-start.47 = (bf16[480,768]{1,0:T(8,128)(2,1)S(1)}, bf16[480,768]{1,0:T(8,128)(2,1)S(1)}, u32[]{:S(2)}, u32[]{:S(2)}) collective-permute-start(bf16[480,768]{1,0:T(8,128)(2,1)S(1)} %maximum_select_fusion.2), channel_id=1, source_target_pairs={{0,4},{2,6},{4,0},{6,2},{1,5},{3,7},{5,1},{7,3},{8,12},{10,14},{12... | collective-permute-start | bytes 2211848 | tf_op jit(solution)/shard_map/ppermute | solution.py:817
  370.6 6.1 %collective-permute-start.37 = (bf16[64,384]{1,0:T(8,128)(2,1)S(1)}, bf16[64,384]{1,0:T(8,128)(2,1)S(1)}, u32[]{:S(2)}, u32[]{:S(2)}) collective-permute-start(bf16[64,384]{1,0:T(8,128)(2,1)S(1)} %get-tuple-element.302), channel_id=1, source_target_pairs={{0,8},{8,0},{16,24},{24,16},{1,9},{9,1},{17,25},{25,17},{2,10},{10... | collective-permute-start | bytes 147464 | tf_op jit(solution)/shard_map/ppermute | solution.py:817
  370.6 7.8 %collective-permute-start.38 = (bf16[64,384]{1,0:T(8,128)(2,1)S(1)}, bf16[64,384]{1,0:T(8,128)(2,1)S(1)}, u32[]{:S(2)}, u32[]{:S(2)}) collective-permute-start(bf16[64,384]{1,0:T(8,128)(2,1)S(1)} %get-tuple-element.303), channel_id=1, source_target_pairs={{0,16},{8,24},{16,0},{24,8},{1,17},{9,25},{17,1},{25,9},{2,18},{10... | collective-permute-start | bytes 147464 | tf_op jit(solution)/shard_map/ppermute | solution.py:817
  379.2 7.9 %collective-permute-start.44 = (bf16[64,384]{1,0:T(8,128)(2,1)S(1)}, bf16[64,384]{1,0:T(8,128)(2,1)S(1)}, u32[]{:S(2)}, u32[]{:S(2)}) collective-permute-start(bf16[64,384]{1,0:T(8,128)(2,1)S(1)} %add_convert_fusion.18), channel_id=1, source_target_pairs={{0,8},{8,0},{16,24},{24,16},{1,9},{9,1},{17,25},{25,17},{2,10},{10... | collective-permute-start | bytes 147464 | tf_op jit(solution)/shard_map/ppermute | solution.py:817
  383.1 6.6 %collective-permute-start.46 = (bf16[64,384]{1,0:T(8,128)(2,1)S(1)}, bf16[64,384]{1,0:T(8,128)(2,1)S(1)}, u32[]{:S(2)}, u32[]{:S(2)}) collective-permute-start(bf16[64,384]{1,0:T(8,128)(2,1)S(1)} %add_convert_fusion.18), channel_id=1, source_target_pairs={{0,24},{8,16},{16,8},{24,0},{1,25},{9,17},{17,9},{25,1},{2,26},{10... | collective-permute-start | bytes 147464 | tf_op jit(solution)/shard_map/ppermute | solution.py:817
  385.6 9.0 %collective-permute-start.48 = (bf16[384,384]{1,0:T(8,128)(2,1)S(1)}, bf16[384,384]{1,0:T(8,128)(2,1)S(1)}, u32[]{:S(2)}, u32[]{:S(2)}) collective-permute-start(bf16[384,384]{1,0:T(8,128)(2,1)S(1)} %maximum_select_fusion.10), channel_id=1, source_target_pairs={{0,4},{2,6},{4,0},{6,2},{1,5},{3,7},{5,1},{7,3},{8,12},{10,14},{12... | collective-permute-start | bytes 884744 | tf_op jit(solution)/shard_map/ppermute | solution.py:817
  402.4 6.1 %collective-permute-start.53 = (bf16[512,384]{1,0:T(8,128)(2,1)S(1)}, bf16[512,384]{1,0:T(8,128)(2,1)S(1)}, u32[]{:S(2)}, u32[]{:S(2)}) collective-permute-start(bf16[512,384]{1,0:T(8,128)(2,1)S(1)} %maximum_select_fusion.8), channel_id=1, source_target_pairs={{0,2},{2,0},{4,6},{6,4},{1,3},{3,1},{5,7},{7,5},{8,10},{10,8},{12,... | collective-permute-start | bytes 1179656 | tf_op jit(solution)/shard_map/ppermute | solution.py:817
  402.5 12.5 %collective-permute-start.54 = (bf16[960,768]{1,0:T(8,128)(2,1)}, bf16[960,768]{1,0:T(8,128)(2,1)}, u32[]{:S(2)}, u32[]{:S(2)}) collective-permute-start(bf16[960,768]{1,0:T(8,128)(2,1)} %maximum_select_fusion.1), channel_id=1, source_target_pairs={{0,2},{2,0},{4,6},{6,4},{1,3},{3,1},{5,7},{7,5},{8,10},{10,8},{12,... | collective-permute-start | bytes 4423688 | tf_op jit(solution)/shard_map/ppermute | solution.py:817
  402.9 7.6 %collective-permute-start.51 = (bf16[768,384]{1,0:T(8,128)(2,1)S(1)}, bf16[768,384]{1,0:T(8,128)(2,1)S(1)}, u32[]{:S(2)}, u32[]{:S(2)}) collective-permute-start(bf16[768,384]{1,0:T(8,128)(2,1)S(1)} %maximum_select_fusion.3), channel_id=1, source_target_pairs={{0,2},{2,0},{4,6},{6,4},{1,3},{3,1},{5,7},{7,5},{8,10},{10,8},{12,... | collective-permute-start | bytes 1769480 | tf_op jit(solution)/shard_map/ppermute | solution.py:817
  (41 other events, 335.4 us)
Sparse Core Ops, SparseCore 0:
  208.1 115.2 reduce-scatter.1
  342.3 51.2 all-gather.1
